TPU v7x, 32 devices: a whole 2x2x4 slice. The times are simulated.
32 devices in a mesh: subj: 16 (over z, y, x), vert: 2 (over core).
Axes of the slice: x: 2, y: 2, z: 4, core: 2. Of those that a mesh axis runs over, the one named last changes fastest.
Arguments:
- data: bfloat16 [32, 256, 4096], P('subj', None, 'vert'), may hold values from -6 to 6
- template: bfloat16 [256, 4096], P(None, 'vert'), may hold values from -6 to 6
- centres: int32 [32], P('vert'), may hold values from 0 to 4095, as said below
- neighbours: int32 [32, 128], P('vert'), may hold values from -128 to 127, as said below
Outputs:
- aligned: bfloat16 [32, 256, 4096], P('subj', None, 'vert')
- new_template: float32 [256, 4096], P(None, 'vert')
Inputs may be any that keep to these rules, and one draw needn't show every extreme that they name: The 16 centres of each aligned block of 16 entries are distinct vertices of the matching block of 2048 vertices, and include that block's first and last vertex. `neighbours`: A searchlight's 128 offsets are distinct and include -128 and 127.
All inputs are finite; a program needn't handle non-finite values.
Results may differ from a plain program's by a relative error of at most 0.0005.
Values may be sent and summed in bfloat16 or wider, within the bound.
No kernel may reach another device: no remote copies, remote signals or barrier semaphores. Data moves between devices by JAX's collectives and lax.ppermute only.
A program may use at most 64 MiB of HBM per device.

v0:
```python
import functools
import math

import jax
import jax.numpy as jnp
from jax import lax
from jax.experimental import pallas as pl
from jax.experimental.pallas import tpu as pltpu
from jax.sharding import PartitionSpec as P

NS_STEPS = 4
LANES = 128
ROWS = 8
BF16 = jnp.bfloat16
F32 = jnp.float32


def dot(a, b):
    return lax.dot_general(a, b, (((1,), (0,)), ((), ())), preferred_element_type=F32)


def dot_t(a, b):
    return lax.dot_general(a, b, (((1,), (1,)), ((), ())), preferred_element_type=F32)


def split(x):
    hi = x.astype(BF16)
    return hi, (x - hi.astype(F32)).astype(BF16)


def halves(x):
    mid = x.shape[1] // 2
    return x[:, :mid] + x[:, mid:]


def polar_factor_t(z):
    norm_sq = jnp.sum(z * z, keepdims=True)
    z = z / jnp.sqrt(norm_sq + 1e-06)
    for _ in range(NS_STEPS):
        hi, lo = split(z)
        both = jnp.concatenate([hi, lo], axis=1)
        pair = jnp.concatenate(
            [jnp.concatenate([hi, hi], axis=1), jnp.concatenate([lo, lo], axis=1)], axis=0
        )
        gram = halves(dot_t(both, pair))
        g_hi, g_lo = split(gram)
        moved = halves(
            dot(jnp.concatenate([g_hi, g_lo], axis=1), jnp.concatenate([both, both], axis=0))
        )
        z = 1.5 * z - 0.5 * moved
    return z


def align_kernel(
    n_subjects, n_centres, group, pos_ref, nb_ref, data_ref, tmpl_ref, low_ref, high_ref,
    aligned_ref, partial_ref, low_out, high_out, edge_out, hits_out, wide, acc, hits, sems,
):
    k = nb_ref.shape[1]
    span = 2 * k
    own = data_ref.shape[2]
    frames = data_ref.shape[1]
    n_wide = own + 2 * k

    copies = []
    for i in range(n_subjects + 1):
        body = data_ref.at[i] if i < n_subjects else tmpl_ref
        copies.append(pltpu.make_async_copy(body, wide.at[i, :, pl.ds(k, own)], sems.at[i, 0]))
        copies.append(pltpu.make_async_copy(low_ref.at[i], wide.at[i, :, pl.ds(0, k)], sems.at[i, 1]))
        copies.append(
            pltpu.make_async_copy(high_ref.at[i], wide.at[i, :, pl.ds(k + own, k)], sems.at[i, 2])
        )
    for copy in copies:
        copy.start()
    acc[...] = jnp.zeros_like(acc)
    hits[...] = jnp.zeros_like(hits)
    for copy in copies:
        copy.wait()

    spot = lax.broadcasted_iota(jnp.int32, (span, k), 0)
    lane = lax.broadcasted_iota(jnp.int32, (1, k), 1)
    ones = jnp.ones((ROWS, k), BF16)

    def place(ref, first, keep, value):
        left, right = value[:, :k], value[:, k:]
        ref[:, pl.ds(first, k)] += jnp.where(keep, left, 0.0)
        ref[:, pl.ds(first + k, k)] += right
        ref[:, pl.ds(first + span, k)] += jnp.where(keep, 0.0, left)

    def one_group(step, carry):
        results = []
        for member in range(group):
            c = step * group + member
            pos = pos_ref[c]
            first = pl.multiple_of((pos // k) * k, k)
            off = pos - first
            keep = lane >= off
            want = (nb_ref[pl.ds(c, 1), :] + (k + off)) & (span - 1)
            pick = jnp.where(spot == want, 1.0, 0.0).astype(BF16)

            def window(i, first=first, keep=keep):
                a = wide[i, :, pl.ds(first, k)]
                b = wide[i, :, pl.ds(first + k, k)]
                d = wide[i, :, pl.ds(first + span, k)]
                return jnp.concatenate([jnp.where(keep, a, d), b], axis=1)

            xs = [dot(window(i), pick).astype(BF16) for i in range(n_subjects)]
            m_t = dot(window(n_subjects), pick).T.astype(BF16)
            crosses = dot(m_t, jnp.concatenate(xs, axis=1))
            outs = []
            for i in range(n_subjects):
                z = polar_factor_t(crosses[:, i * k : (i + 1) * k])
                hi, lo = split(z)
                spread = dot(pick, jnp.concatenate([hi, lo], axis=1)).astype(BF16)
                outs.append(dot_t(jnp.concatenate([xs[i], xs[i]], axis=1), spread))
            results.append((first, keep, outs, dot_t(ones, pick)))
        for first, keep, outs, count in results:
            for i in range(n_subjects):
                place(acc.at[i], first, keep, outs[i])
            place(hits, first, keep, count)
        return carry

    lax.fori_loop(0, n_centres // group, one_group, 0)

    low_out[:, :frames, :] = acc[:, :, :k]
    high_out[:, :frames, :] = acc[:, :, own + k :]
    for i in range(n_subjects):
        low_out[i, frames:, :] = hits[:, :k]
        high_out[i, frames:, :] = hits[:, own + k :]
    edge_out[:, :, :k] = acc[:, :, k:span]
    edge_out[:, :, k:] = acc[:, :, own : own + k]
    hits_out[:, :k] = hits[:, k:span]
    hits_out[:, k:] = hits[:, own : own + k]
    inverse = 1.0 / jnp.maximum(hits[:, k : k + own], 1.0)

    def one_rows(step, carry):
        rows = pl.ds(pl.multiple_of(step * 2 * ROWS, 2 * ROWS), 2 * ROWS)
        scale = jnp.concatenate([inverse, inverse], axis=0)
        total = jnp.zeros((2 * ROWS, own), F32)
        for i in range(n_subjects):
            mapped = acc[i, rows, k : k + own] * scale
            aligned_ref[i, rows, :] = mapped.astype(BF16)
            total = total + mapped
        partial_ref[rows, :] = total
        return carry

    lax.fori_loop(0, frames // (2 * ROWS), one_rows, 0)


def align(data, template, low, high, local_pos, neighbours):
    n_subjects, frames, own = data.shape
    n_centres, k = neighbours.shape
    n_wide = own + 2 * k
    group = 2 if n_centres % 2 == 0 else 1
    vmem = pl.BlockSpec(memory_space=pltpu.VMEM)
    hbm = pl.BlockSpec(memory_space=pl.ANY)
    smem = pl.BlockSpec(memory_space=pltpu.SMEM)
    return pl.pallas_call(
        functools.partial(align_kernel, n_subjects, n_centres, group),
        out_shape=(
            jax.ShapeDtypeStruct((n_subjects, frames, own), BF16),
            jax.ShapeDtypeStruct((frames, own), F32),
            jax.ShapeDtypeStruct((n_subjects, frames + ROWS, k), F32),
            jax.ShapeDtypeStruct((n_subjects, frames + ROWS, k), F32),
            jax.ShapeDtypeStruct((n_subjects, frames, 2 * k), F32),
            jax.ShapeDtypeStruct((ROWS, 2 * k), F32),
        ),
        in_specs=[smem, vmem, hbm, hbm, hbm, hbm],
        out_specs=(vmem,) * 6,
        scratch_shapes=[
            pltpu.VMEM((n_subjects + 1, frames, n_wide), BF16),
            pltpu.VMEM((n_subjects, frames, n_wide), F32),
            pltpu.VMEM((ROWS, n_wide), F32),
            pltpu.SemaphoreType.DMA((n_subjects + 1, 3)),
        ],
        compiler_params=pltpu.CompilerParams(vmem_limit_bytes=48 * 1024 * 1024),
        name="align",
    )(local_pos, neighbours, data, template, low, high)


def along_vert(up_value, down_value):
    size = lax.axis_size("vert")
    up = [(i, i + 1) for i in range(size - 1)]
    down = [(i + 1, i) for i in range(size - 1)]
    return lax.ppermute(up_value, "vert", up), lax.ppermute(down_value, "vert", down)


class Hypercube:
    def __init__(self):
        self.size = lax.axis_size("subj")
        self.verts = lax.axis_size("vert")
        n_bits = self.size.bit_length() - 1
        bits = list(range(n_bits))
        self.phases = [bits[i : i + 2] for i in range(0, n_bits, 2)]

    def order(self, phase, v):
        return phase if v % 2 == 0 else phase[::-1]

    def mine(self, phase):
        s = lax.axis_index("subj")

        def number(bits):
            return sum(((s >> b) & 1) << i for i, b in enumerate(bits))

        even = number(self.order(phase, 0))
        odd = number(self.order(phase, 1))
        return jnp.where(lax.axis_index("vert") % 2 == 0, even, odd)

    def pairs(self, phase, m):
        out = []
        for s in range(self.size):
            for v in range(self.verts):
                mask = sum(((m >> i) & 1) << b for i, b in enumerate(self.order(phase, v)))
                out.append((s * self.verts + v, (s ^ mask) * self.verts + v))
        return out

    def swap(self, value, phase, m):
        return lax.ppermute(value, ("subj", "vert"), self.pairs(phase, m))

    def reduce(self, total, top):
        for phase in self.phases:
            count = 1 << len(phase)
            rows = total.shape[0] // count
            j = self.mine(phase)
            inverse = 1024.0 / top[0, 0]
            got = []
            for m in range(1, count):
                block = lax.dynamic_slice_in_dim(total, (j ^ m) * rows, rows)
                sent = (block * inverse).astype(jnp.float16)
                got.append((self.swap(sent, phase, m), self.swap(top, phase, m)))
            total = lax.dynamic_slice_in_dim(total, j * rows, rows)
            for value, other in got:
                total = total + value.astype(F32) * (other[0, 0] * (1.0 / 1024.0))
                top = jnp.maximum(top, other)
        return total, top

    def gather(self, value):
        for phase in reversed(self.phases):
            count = 1 << len(phase)
            j = self.mine(phase)
            parts = [value] + [self.swap(value, phase, m) for m in range(1, count)]
            placed = []
            for q in range(count):
                chosen = parts[0]
                for m in range(1, count):
                    chosen = jnp.where((j ^ q) == m, parts[m], chosen)
                placed.append(chosen)
            value = jnp.concatenate(placed, axis=0)
        return value


def local(data, template, centres, neighbours):
    k = neighbours.shape[1]
    n_subjects, frames, own = data.shape
    everything_low = jnp.concatenate([data[:, :, :k], template[None, :, :k]], axis=0)
    everything_high = jnp.concatenate([data[:, :, own - k :], template[None, :, own - k :]], axis=0)
    low, high = along_vert(everything_high, everything_low)
    local_pos = centres - lax.axis_index("vert") * own
    aligned, partial, low_out, high_out, edges, edge_hits = align(
        data, template, low, high, local_pos, neighbours
    )
    from_low, from_high = along_vert(high_out, low_out)
    total_edges = edges + jnp.concatenate([from_low[:, :frames], from_high[:, :frames]], axis=2)
    more_hits = jnp.concatenate([from_low[0, frames], from_high[0, frames]], axis=0)
    mapped = total_edges / jnp.maximum(edge_hits[0] + more_hits, 1.0)
    rounded = mapped.astype(BF16)
    aligned = aligned.at[:, :, :k].set(rounded[:, :, :k])
    aligned = aligned.at[:, :, own - k :].set(rounded[:, :, k:])
    edge_sum = jnp.sum(mapped, axis=0)
    partial = partial.at[:, :k].set(edge_sum[:, :k])
    partial = partial.at[:, own - k :].set(edge_sum[:, k:])
    top = jnp.maximum(jnp.max(jnp.abs(partial)), 1e-30)
    cube = Hypercube()
    total, top = cube.reduce(partial, jnp.full((ROWS, LANES), top, F32))
    subjects = n_subjects * lax.axis_size("subj")
    sent = (total * (1024.0 / top[0, 0])).astype(jnp.float16)
    whole = cube.gather(sent)
    return aligned, whole.astype(F32) * (top[0, 0] * (1.0 / (1024.0 * subjects)))


def solution(mesh):
    in_specs = (P("subj", None, "vert"), P(None, "vert"), P("vert"), P("vert", None))
    out_specs = (P("subj", None, "vert"), P(None, "vert"))
    return jax.shard_map(local, mesh=mesh, in_specs=in_specs, out_specs=out_specs, check_vma=False)
```

profile of v0, /device:TPU:0, one launch (start us, length us, event | category | flops | bytes accessed | tf_op | source)
XLA Modules:
  0.0 139.5 jit_solution(15454517370345728955)
XLA Ops:
  0.6 1.0 slice_bitcast_fusion
  1.6 1.0 fusion.5
  2.6 2.4 %collective-permute-start = (bf16[3,256,128]{2,1,0:T(8,128)(2,1)S(1)}, bf16[3,256,128]{2,1,0:T(8,128)(2,1)S(1)}, u32[]{:S(2)}, u32[]{:S(2)}) collective-permute-start(bf16[3,256,128]{2,1,0:T(8,128)(2,1)S(1)} %pad_maximum_fusion.1), channel_id=1, source_target_pairs={{0,1},{2,3},{4,5},{6,7},{8,9},{10,11},{12,13},{14,15},{16,17},{18,... | collective-permute-start | bytes 589832 | tf_op jit(solution)/shard_map/ppermute | solution.py:184
  5.0 1.3 collective-permute-start.1
  6.3 0.7 broadcast_subtract_fusion.pos_ref
  7.0 1.4 collective-permute-done.1.high_ref
  8.4 0.7 copy-done.2
  9.1 59.4 %align.1 = (bf16[2,256,2048]{2,1,0:T(8,128)(2,1)}, f32[256,2048]{1,0:T(8,128)S(1)}, f32[2,264,128]{2,1,0:T(8,128)}, f32[2,264,128]{2,1,0:T(8,128)}, f32[2,256,256]{2,1,0:T(8,128)S(1)}, /*index=5*/f32[8,256]{1,0:T(8,128)S(1)}) custom-call(s32[16]{0:T(128)S(1)} %broadcast_subtract_fusion.pos_ref, s32[16,128]{1,0:T(8,128)S(1)} %copy-done.2, ...), custom_call_target="tpu_custom_call" | custom-call | tf_op jit(solution)/shard_map/align/pallas_call | solution.py:157
  68.5 0.0 copy-start.1
  68.5 0.8 copy-done.1
  69.3 1.3 collective-permute-start.3
  70.5 3.1 %collective-permute-start.2 = (f32[2,264,128]{2,1,0:T(8,128)}, f32[2,264,128]{2,1,0:T(8,128)S(1)}, u32[]{:S(2)}, u32[]{:S(2)}) collective-permute-start(f32[2,264,128]{2,1,0:T(8,128)} %get-tuple-element.58), channel_id=1, source_target_pairs={{0,1},{2,3},{4,5},{6,7},{8,9},{10,11},{12,13},{14,15},{16,17},{18,... | collective-permute-start | bytes 811016 | tf_op jit(solution)/shard_map/ppermute | solution.py:184
  73.7 0.7 compare_reduce_fusion
  74.4 0.0 collective-permute-done.3
  74.4 0.6 collective-permute-done.2
  75.0 1.2 fusion.3
  76.2 0.7 fusion.1
  76.9 0.7 abs_reduce_fusion
  78.3 1.0 multiply_convert_fusion.2
  79.3 3.3 %collective-permute-start.8 = (f16[64,2048]{1,0:T(8,128)(2,1)}, f16[64,2048]{1,0:T(8,128)(2,1)S(1)}, u32[]{:S(2)}, u32[]{:S(2)}) collective-permute-start(f16[64,2048]{1,0:T(8,128)(2,1)} %get-tuple-element.63), channel_id=1, source_target_pairs={{0,6},{1,7},{2,4},{3,5},{4,2},{5,3},{6,0},{7,1},{8,14},{9,15},{10,... | collective-permute-start | bytes 786440 | tf_op jit(solution)/shard_map/ppermute | solution.py:217
  82.6 0.5 collective-permute-start.6
  83.1 0.0 collective-permute-start.4
  83.2 2.9 %collective-permute-start.9 = (f32[8,128]{1,0:T(8,128)S(1)}, f32[8,128]{1,0:T(8,128)S(1)}, u32[]{:S(2)}, u32[]{:S(2)}) collective-permute-start(f32[8,128]{1,0:T(8,128)S(1)} %broadcast_in_dim.12), channel_id=1, source_target_pairs={{0,6},{1,7},{2,4},{3,5},{4,2},{5,3},{6,0},{7,1},{8,14},{9,15},{10,... | collective-permute-start | bytes 12296 | tf_op jit(solution)/shard_map/ppermute | solution.py:217
  86.1 0.5 collective-permute-start.7
  86.6 8.8 %collective-permute-done.9 = f32[8,128]{1,0:T(8,128)S(1)} collective-permute-done((f32[8,128]{1,0:T(8,128)S(1)}, f32[8,128]{1,0:T(8,128)S(1)}, u32[]{:S(2)}, u32[]{:S(2)}) %collective-permute-start.9) | collective-permute-done | bytes 4128 | tf_op jit(solution)/shard_map/ppermute | solution.py:217
  95.4 1.7 %collective-permute-start.5 = (f32[8,128]{1,0:T(8,128)S(1)}, f32[8,128]{1,0:T(8,128)S(1)}, u32[]{:S(2)}, u32[]{:S(2)}) collective-permute-start(f32[8,128]{1,0:T(8,128)S(1)} %broadcast_in_dim.12), channel_id=1, source_target_pairs={{0,2},{1,5},{2,0},{3,7},{4,6},{5,1},{6,4},{7,3},{8,10},{9,13},{10,... | collective-permute-start | bytes 12296 | tf_op jit(solution)/shard_map/ppermute | solution.py:217
  97.1 0.0 collective-permute-done.7
  97.1 1.9 %collective-permute-done.5 = f32[8,128]{1,0:T(8,128)S(1)} collective-permute-done((f32[8,128]{1,0:T(8,128)S(1)}, f32[8,128]{1,0:T(8,128)S(1)}, u32[]{:S(2)}, u32[]{:S(2)}) %collective-permute-start.5) | collective-permute-done | bytes 4128 | tf_op jit(solution)/shard_map/ppermute | solution.py:217
  99.0 0.5 slice.162
  99.6 3.8 %collective-permute-start.15 = (f32[8,128]{1,0:T(8,128)S(1)}, f32[8,128]{1,0:T(8,128)S(1)}, u32[]{:S(2)}, u32[]{:S(2)}) collective-permute-start(f32[8,128]{1,0:T(8,128)S(1)} %maximum_maximum_fusion.1), channel_id=1, source_target_pairs={{0,24},{1,25},{2,26},{3,27},{4,28},{5,29},{6,30},{7,31},{8,16},{9,... | collective-permute-start | bytes 12296 | tf_op jit(solution)/shard_map/ppermute | solution.py:217
  103.4 0.5 slice.161
  104.5 0.5 slice.160
  105.7 0.5 slice.159
  107.5 0.7 collective-permute-start.11
  108.1 0.0 collective-permute-done.6
  108.2 0.0 collective-permute-done.4
  108.2 0.2 multiply_add_fusion
  108.4 3.9 %collective-permute-start.14 = (f16[16,2048]{1,0:T(8,128)(2,1)S(1)}, f16[16,2048]{1,0:T(8,128)(2,1)S(1)}, u32[]{:S(2)}, u32[]{:S(2)}) collective-permute-start(f16[16,2048]{1,0:T(8,128)(2,1)S(1)} %get-tuple-element.76), channel_id=1, source_target_pairs={{0,24},{1,25},{2,26},{3,27},{4,28},{5,29},{6,30},{7,31},{8,16},{9,... | collective-permute-start | bytes 196616 | tf_op jit(solution)/shard_map/ppermute | solution.py:217
  112.2 0.0 collective-permute-start.12
  112.2 0.0 collective-permute-done.15
  112.2 0.6 collective-permute-start.10
  112.9 0.0 collective-permute-done.13
  112.9 0.5 slice.166
  114.1 0.5 slice.165
  115.2 0.6 slice.164
  116.5 0.6 slice.163
  117.8 0.1 multiply_convert_fusion.3
  117.8 3.8 %collective-permute-start.16 = (f16[16,2048]{1,0:T(8,128)(2,1)S(1)}, f16[16,2048]{1,0:T(8,128)(2,1)S(1)}, u32[]{:S(2)}, u32[]{:S(2)}) collective-permute-start(f16[16,2048]{1,0:T(8,128)(2,1)S(1)} %multiply_convert_fusion.3), channel_id=1, source_target_pairs={{0,24},{1,25},{2,26},{3,27},{4,28},{5,29},{6,30},{7,31},{8,16},{9,... | collective-permute-start | bytes 196616 | tf_op jit(solution)/shard_map/ppermute | solution.py:217
  121.7 0.6 collective-permute-start.18
  122.3 1.7 %collective-permute-done.16 = f16[16,2048]{1,0:T(8,128)(2,1)S(1)} collective-permute-done((f16[16,2048]{1,0:T(8,128)(2,1)S(1)}, f16[16,2048]{1,0:T(8,128)(2,1)S(1)}, u32[]{:S(2)}, u32[]{:S(2)}) %collective-permute-start.16) | collective-permute-done | bytes 65568 | tf_op jit(solution)/shard_map/ppermute | solution.py:217
  124.0 2.8 %collective-permute-done.17 = f16[16,2048]{1,0:T(8,128)(2,1)S(1)} collective-permute-done((f16[16,2048]{1,0:T(8,128)(2,1)S(1)}, f16[16,2048]{1,0:T(8,128)(2,1)S(1)}, u32[]{:S(2)}, u32[]{:S(2)}) %collective-permute-start.17) | collective-permute-done | bytes 65568 | tf_op jit(solution)/shard_map/ppermute | solution.py:217
  126.8 0.1 select_select_fusion.7
  126.9 0.1 pad_maximum_fusion
  127.0 2.5 %collective-permute-start.19 = (f16[64,2048]{1,0:T(8,128)(2,1)S(1)}, f16[64,2048]{1,0:T(8,128)(2,1)S(1)}, u32[]{:S(2)}, u32[]{:S(2)}) collective-permute-start(f16[64,2048]{1,0:T(8,128)(2,1)S(1)} %pad_maximum_fusion), channel_id=1, source_target_pairs={{0,6},{1,7},{2,4},{3,5},{4,2},{5,3},{6,0},{7,1},{8,14},{9,15},{10,... | collective-permute-start | bytes 786440 | tf_op jit(solution)/shard_map/ppermute | solution.py:217
  129.5 0.5 collective-permute-start.20
  130.0 0.5 collective-permute-start.21
  130.6 0.7 slice_dynamic-update-slice_fusion.2
  131.2 0.7 slice_dynamic-update-slice_fusion.1
  132.6 1.9 %collective-permute-done.19 = f16[64,2048]{1,0:T(8,128)(2,1)S(1)} collective-permute-done((f16[64,2048]{1,0:T(8,128)(2,1)S(1)}, f16[64,2048]{1,0:T(8,128)(2,1)S(1)}, u32[]{:S(2)}, u32[]{:S(2)}) %collective-permute-start.19) | collective-permute-done | bytes 262176 | tf_op jit(solution)/shard_map/ppermute | solution.py:217
  134.5 2.7 %collective-permute-done.20 = f16[64,2048]{1,0:T(8,128)(2,1)S(1)} collective-permute-done((f16[64,2048]{1,0:T(8,128)(2,1)S(1)}, f16[64,2048]{1,0:T(8,128)(2,1)S(1)}, u32[]{:S(2)}, u32[]{:S(2)}) %collective-permute-start.20) | collective-permute-done | bytes 262176 | tf_op jit(solution)/shard_map/ppermute | solution.py:217
  137.2 0.1 collective-permute-done.21
  137.3 0.3 select_select_fusion.3
  137.5 0.3 select_select_fusion.2
  137.8 1.7 %convert_multiply_fusion = f32[256,2048]{1,0:T(8,128)} fusion(f16[64,2048]{1,0:T(8,128)(2,1)S(1)} %get-tuple-element.70, f16[64,2048]{1,0:T(8,128)(2,1)S(1)} %get-tuple-element.72, f16[64,2048]{1,0:T(8,128)(2,1)S(1)} %get-tuple-element.71, f16[64,2048]{1,0:T(8,128)(2,1)S(1)} %get-tuple-element.69, f32[]{:T(128)} %bitcast.13), kind=kLoop, calls=%fused_computation | loop fusion | flops 2621440 | bytes 3145732 | tf_op jit(solution)/shard_map/mul | solution.py:277
  (25 shorter events, 0.2 us)
Async XLA Ops:
  0.6 7.8 %copy-start = (bf16[256,2048]{1,0:T(8,128)(2,1)S(1)}, bf16[256,2048]{1,0:T(8,128)(2,1)}, u32[]{:S(2)}) copy-start(bf16[256,2048]{1,0:T(8,128)(2,1)} %tmpl_ref.1) | copy-start | bytes 3145732
  2.6 4.4 %collective-permute-start = (bf16[3,256,128]{2,1,0:T(8,128)(2,1)S(1)}, bf16[3,256,128]{2,1,0:T(8,128)(2,1)S(1)}, u32[]{:S(2)}, u32[]{:S(2)}) collective-permute-start(bf16[3,256,128]{2,1,0:T(8,128)(2,1)S(1)} %pad_maximum_fusion.1), channel_id=1, source_target_pairs={{0,1},{2,3},{4,5},{6,7},{8,9},{10,11},{12,13},{14,15},{16,17},{18,... | collective-permute-start | bytes 589832 | tf_op jit(solution)/shard_map/ppermute | solution.py:184
  5.0 3.3 %collective-permute-start.1 = (bf16[3,256,128]{2,1,0:T(8,128)(2,1)S(1)}, bf16[3,256,128]{2,1,0:T(8,128)(2,1)S(1)}, u32[]{:S(2)}, u32[]{:S(2)}) collective-permute-start(bf16[3,256,128]{2,1,0:T(8,128)(2,1)S(1)} %pad_maximum_fusion.2), channel_id=1, source_target_pairs={{1,0},{3,2},{5,4},{7,6},{9,8},{11,10},{13,12},{15,14},{17,16},{19,... | collective-permute-start | bytes 589832 | tf_op jit(solution)/shard_map/ppermute | solution.py:184
  8.4 0.7 copy-start.2
  68.5 0.8 copy-start.1
  69.3 5.1 %collective-permute-start.3 = (f32[2,264,128]{2,1,0:T(8,128)}, f32[2,264,128]{2,1,0:T(8,128)S(1)}, u32[]{:S(2)}, u32[]{:S(2)}) collective-permute-start(f32[2,264,128]{2,1,0:T(8,128)} %get-tuple-element.59), channel_id=1, source_target_pairs={{1,0},{3,2},{5,4},{7,6},{9,8},{11,10},{13,12},{15,14},{17,16},{19,... | collective-permute-start | bytes 811016 | tf_op jit(solution)/shard_map/ppermute | solution.py:184
  70.5 4.4 %collective-permute-start.2 = (f32[2,264,128]{2,1,0:T(8,128)}, f32[2,264,128]{2,1,0:T(8,128)S(1)}, u32[]{:S(2)}, u32[]{:S(2)}) collective-permute-start(f32[2,264,128]{2,1,0:T(8,128)} %get-tuple-element.58), channel_id=1, source_target_pairs={{0,1},{2,3},{4,5},{6,7},{8,9},{10,11},{12,13},{14,15},{16,17},{18,... | collective-permute-start | bytes 811016 | tf_op jit(solution)/shard_map/ppermute | solution.py:184
  79.3 28.2 %collective-permute-start.8 = (f16[64,2048]{1,0:T(8,128)(2,1)}, f16[64,2048]{1,0:T(8,128)(2,1)S(1)}, u32[]{:S(2)}, u32[]{:S(2)}) collective-permute-start(f16[64,2048]{1,0:T(8,128)(2,1)} %get-tuple-element.63), channel_id=1, source_target_pairs={{0,6},{1,7},{2,4},{3,5},{4,2},{5,3},{6,0},{7,1},{8,14},{9,15},{10,... | collective-permute-start | bytes 786440 | tf_op jit(solution)/shard_map/ppermute | solution.py:217
  82.6 25.6 %collective-permute-start.6 = (f16[64,2048]{1,0:T(8,128)(2,1)}, f16[64,2048]{1,0:T(8,128)(2,1)S(1)}, u32[]{:S(2)}, u32[]{:S(2)}) collective-permute-start(f16[64,2048]{1,0:T(8,128)(2,1)} %get-tuple-element.64), channel_id=1, source_target_pairs={{0,4},{1,3},{2,6},{3,1},{4,0},{5,7},{6,2},{7,5},{8,12},{9,11},{10,... | collective-permute-start | bytes 786440 | tf_op jit(solution)/shard_map/ppermute | solution.py:217
  83.1 25.0 %collective-permute-start.4 = (f16[64,2048]{1,0:T(8,128)(2,1)S(1)}, f16[64,2048]{1,0:T(8,128)(2,1)S(1)}, u32[]{:S(2)}, u32[]{:S(2)}) collective-permute-start(f16[64,2048]{1,0:T(8,128)(2,1)S(1)} %get-tuple-element.62), channel_id=1, source_target_pairs={{0,2},{1,5},{2,0},{3,7},{4,6},{5,1},{6,4},{7,3},{8,10},{9,13},{10,... | collective-permute-start | bytes 786440 | tf_op jit(solution)/shard_map/ppermute | solution.py:217
  83.2 12.3 %collective-permute-start.9 = (f32[8,128]{1,0:T(8,128)S(1)}, f32[8,128]{1,0:T(8,128)S(1)}, u32[]{:S(2)}, u32[]{:S(2)}) collective-permute-start(f32[8,128]{1,0:T(8,128)S(1)} %broadcast_in_dim.12), channel_id=1, source_target_pairs={{0,6},{1,7},{2,4},{3,5},{4,2},{5,3},{6,0},{7,1},{8,14},{9,15},{10,... | collective-permute-start | bytes 12296 | tf_op jit(solution)/shard_map/ppermute | solution.py:217
  86.1 11.0 %collective-permute-start.7 = (f32[8,128]{1,0:T(8,128)S(1)}, f32[8,128]{1,0:T(8,128)S(1)}, u32[]{:S(2)}, u32[]{:S(2)}) collective-permute-start(f32[8,128]{1,0:T(8,128)S(1)} %broadcast_in_dim.12), channel_id=1, source_target_pairs={{0,4},{1,3},{2,6},{3,1},{4,0},{5,7},{6,2},{7,5},{8,12},{9,11},{10,... | collective-permute-start | bytes 12296 | tf_op jit(solution)/shard_map/ppermute | solution.py:217
  95.4 3.6 %collective-permute-start.5 = (f32[8,128]{1,0:T(8,128)S(1)}, f32[8,128]{1,0:T(8,128)S(1)}, u32[]{:S(2)}, u32[]{:S(2)}) collective-permute-start(f32[8,128]{1,0:T(8,128)S(1)} %broadcast_in_dim.12), channel_id=1, source_target_pairs={{0,2},{1,5},{2,0},{3,7},{4,6},{5,1},{6,4},{7,3},{8,10},{9,13},{10,... | collective-permute-start | bytes 12296 | tf_op jit(solution)/shard_map/ppermute | solution.py:217
  99.6 12.7 %collective-permute-start.15 = (f32[8,128]{1,0:T(8,128)S(1)}, f32[8,128]{1,0:T(8,128)S(1)}, u32[]{:S(2)}, u32[]{:S(2)}) collective-permute-start(f32[8,128]{1,0:T(8,128)S(1)} %maximum_maximum_fusion.1), channel_id=1, source_target_pairs={{0,24},{1,25},{2,26},{3,27},{4,28},{5,29},{6,30},{7,31},{8,16},{9,... | collective-permute-start | bytes 12296 | tf_op jit(solution)/shard_map/ppermute | solution.py:217
  103.4 9.5 %collective-permute-start.13 = (f32[8,128]{1,0:T(8,128)S(1)}, f32[8,128]{1,0:T(8,128)S(1)}, u32[]{:S(2)}, u32[]{:S(2)}) collective-permute-start(f32[8,128]{1,0:T(8,128)S(1)} %maximum_maximum_fusion.1), channel_id=1, source_target_pairs={{0,16},{1,9},{2,18},{3,11},{4,20},{5,13},{6,22},{7,15},{8,24},{9,1... | collective-permute-start | bytes 12296 | tf_op jit(solution)/shard_map/ppermute | solution.py:217
  107.5 5.4 %collective-permute-start.11 = (f32[8,128]{1,0:T(8,128)S(1)}, f32[8,128]{1,0:T(8,128)S(1)}, u32[]{:S(2)}, u32[]{:S(2)}) collective-permute-start(f32[8,128]{1,0:T(8,128)S(1)} %maximum_maximum_fusion.1), channel_id=1, source_target_pairs={{0,8},{1,17},{2,10},{3,19},{4,12},{5,21},{6,14},{7,23},{8,0},{9,25... | collective-permute-start | bytes 12296 | tf_op jit(solution)/shard_map/ppermute | solution.py:217
  108.4 9.4 %collective-permute-start.14 = (f16[16,2048]{1,0:T(8,128)(2,1)S(1)}, f16[16,2048]{1,0:T(8,128)(2,1)S(1)}, u32[]{:S(2)}, u32[]{:S(2)}) collective-permute-start(f16[16,2048]{1,0:T(8,128)(2,1)S(1)} %get-tuple-element.76), channel_id=1, source_target_pairs={{0,24},{1,25},{2,26},{3,27},{4,28},{5,29},{6,30},{7,31},{8,16},{9,... | collective-permute-start | bytes 196616 | tf_op jit(solution)/shard_map/ppermute | solution.py:217
  112.2 5.5 %collective-permute-start.12 = (f16[16,2048]{1,0:T(8,128)(2,1)S(1)}, f16[16,2048]{1,0:T(8,128)(2,1)S(1)}, u32[]{:S(2)}, u32[]{:S(2)}) collective-permute-start(f16[16,2048]{1,0:T(8,128)(2,1)S(1)} %get-tuple-element.77), channel_id=1, source_target_pairs={{0,16},{1,9},{2,18},{3,11},{4,20},{5,13},{6,22},{7,15},{8,24},{9,1... | collective-permute-start | bytes 196616 | tf_op jit(solution)/shard_map/ppermute | solution.py:217
  112.2 5.5 %collective-permute-start.10 = (f16[16,2048]{1,0:T(8,128)(2,1)S(1)}, f16[16,2048]{1,0:T(8,128)(2,1)S(1)}, u32[]{:S(2)}, u32[]{:S(2)}) collective-permute-start(f16[16,2048]{1,0:T(8,128)(2,1)S(1)} %get-tuple-element.75), channel_id=1, source_target_pairs={{0,8},{1,17},{2,10},{3,19},{4,12},{5,21},{6,14},{7,23},{8,0},{9,25... | collective-permute-start | bytes 196616 | tf_op jit(solution)/shard_map/ppermute | solution.py:217
  117.8 6.2 %collective-permute-start.16 = (f16[16,2048]{1,0:T(8,128)(2,1)S(1)}, f16[16,2048]{1,0:T(8,128)(2,1)S(1)}, u32[]{:S(2)}, u32[]{:S(2)}) collective-permute-start(f16[16,2048]{1,0:T(8,128)(2,1)S(1)} %multiply_convert_fusion.3), channel_id=1, source_target_pairs={{0,24},{1,25},{2,26},{3,27},{4,28},{5,29},{6,30},{7,31},{8,16},{9,... | collective-permute-start | bytes 196616 | tf_op jit(solution)/shard_map/ppermute | solution.py:217
  121.6 5.2 %collective-permute-start.17 = (f16[16,2048]{1,0:T(8,128)(2,1)S(1)}, f16[16,2048]{1,0:T(8,128)(2,1)S(1)}, u32[]{:S(2)}, u32[]{:S(2)}) collective-permute-start(f16[16,2048]{1,0:T(8,128)(2,1)S(1)} %multiply_convert_fusion.3), channel_id=1, source_target_pairs={{0,16},{1,9},{2,18},{3,11},{4,20},{5,13},{6,22},{7,15},{8,24},{9,1... | collective-permute-start | bytes 196616 | tf_op jit(solution)/shard_map/ppermute | solution.py:217
  121.7 5.2 %collective-permute-start.18 = (f16[16,2048]{1,0:T(8,128)(2,1)S(1)}, f16[16,2048]{1,0:T(8,128)(2,1)S(1)}, u32[]{:S(2)}, u32[]{:S(2)}) collective-permute-start(f16[16,2048]{1,0:T(8,128)(2,1)S(1)} %multiply_convert_fusion.3), channel_id=1, source_target_pairs={{0,8},{1,17},{2,10},{3,19},{4,12},{5,21},{6,14},{7,23},{8,0},{9,25... | collective-permute-start | bytes 196616 | tf_op jit(solution)/shard_map/ppermute | solution.py:217
  127.0 7.4 %collective-permute-start.19 = (f16[64,2048]{1,0:T(8,128)(2,1)S(1)}, f16[64,2048]{1,0:T(8,128)(2,1)S(1)}, u32[]{:S(2)}, u32[]{:S(2)}) collective-permute-start(f16[64,2048]{1,0:T(8,128)(2,1)S(1)} %pad_maximum_fusion), channel_id=1, source_target_pairs={{0,6},{1,7},{2,4},{3,5},{4,2},{5,3},{6,0},{7,1},{8,14},{9,15},{10,... | collective-permute-start | bytes 786440 | tf_op jit(solution)/shard_map/ppermute | solution.py:217
  129.5 7.6 %collective-permute-start.20 = (f16[64,2048]{1,0:T(8,128)(2,1)S(1)}, f16[64,2048]{1,0:T(8,128)(2,1)S(1)}, u32[]{:S(2)}, u32[]{:S(2)}) collective-permute-start(f16[64,2048]{1,0:T(8,128)(2,1)S(1)} %pad_maximum_fusion), channel_id=1, source_target_pairs={{0,4},{1,3},{2,6},{3,1},{4,0},{5,7},{6,2},{7,5},{8,12},{9,11},{10,... | collective-permute-start | bytes 786440 | tf_op jit(solution)/shard_map/ppermute | solution.py:217
  130.0 7.2 %collective-permute-start.21 = (f16[64,2048]{1,0:T(8,128)(2,1)S(1)}, f16[64,2048]{1,0:T(8,128)(2,1)S(1)}, u32[]{:S(2)}, u32[]{:S(2)}) collective-permute-start(f16[64,2048]{1,0:T(8,128)(2,1)S(1)} %pad_maximum_fusion), channel_id=1, source_target_pairs={{0,2},{1,5},{2,0},{3,7},{4,6},{5,1},{6,4},{7,3},{8,10},{9,13},{10,... | collective-permute-start | bytes 786440 | tf_op jit(solution)/shard_map/ppermute | solution.py:217
where the time goes:
time: 140 us; the launch traced here: 139 us
  Pallas kernels  59.4 us (42%)
  starting transfers between devices  33.9 us (24%)
  waiting for transfers between devices  22 us (16%)
  local copies, waits for them, and re-layouts  9.16 us (7%)
  other arithmetic  7.67 us (5%)
  between operations  7.4 us (5%)
    pallas_call x1, Pallas kernels, align(): pl.pallas_call(functools.partial(align_kernel, n_subjects, n_centres, gro...  59.4 us
    ppermute x18, starting transfers between devices, swap(): return lax.ppermute(value, ('subj', 'vert'), self.pairs(phase, m))  25.9 us
    ppermute x18, waiting for transfers between devices, swap(): return lax.ppermute(value, ('subj', 'vert'), self.pairs(phase, m))  20 us
    ppermute x2, starting transfers between devices, along_vert(): lax.ppermute(up_value, 'vert', up)  5.43 us
    slice x6, local copies, waits for them, and re-layouts, reduce(): total = total + value.astype(F32) * (other[0, 0] * (1.0 / 1024.0))  3.27 us
  transfers between devices with their start and end apart: 22, of which 9 were waited for; matrix products, arithmetic and copies ran while one was open for 5% of the time, Pallas kernels for 0%

commit v1 on v0

v1 whole, which is shorter than its diff:
```python
import functools
import math

import jax
import jax.numpy as jnp
from jax import lax
from jax.experimental import pallas as pl
from jax.experimental.pallas import tpu as pltpu
from jax.sharding import PartitionSpec as P

NS_STEPS = 4
LANES = 128
ROWS = 8
HEADROOM = 10.0
BF16 = jnp.bfloat16
F32 = jnp.float32


def dot(a, b):
    return lax.dot_general(a, b, (((1,), (0,)), ((), ())), preferred_element_type=F32)


def dot_t(a, b):
    return lax.dot_general(a, b, (((1,), (1,)), ((), ())), preferred_element_type=F32)


def split(x):
    hi = x.astype(BF16)
    return hi, (x - hi.astype(F32)).astype(BF16)


def halves(x):
    mid = x.shape[1] // 2
    return x[:, :mid] + x[:, mid:]


def polar_factors_t(zs):
    sums = [jnp.sum(z * z, keepdims=True) for z in zs]
    zs = [z / jnp.sqrt(norm_sq + 1e-06) for z, norm_sq in zip(zs, sums)]
    for _ in range(NS_STEPS):
        boths = [jnp.concatenate(split(z), axis=1) for z in zs]
        grams = []
        for both in boths:
            k = both.shape[0]
            hi, lo = both[:, :k], both[:, k:]
            pair = jnp.concatenate(
                [jnp.concatenate([hi, hi], axis=1), jnp.concatenate([lo, lo], axis=1)], axis=0
            )
            grams.append(dot_t(both, pair))
        grams = [jnp.concatenate(split(halves(gram)), axis=1) for gram in grams]
        moved = [
            dot(gram, jnp.concatenate([both, both], axis=0)) for gram, both in zip(grams, boths)
        ]
        zs = [1.5 * z - 0.5 * halves(move) for z, move in zip(zs, moved)]
    return zs


def align_kernel(
    n_subjects, n_centres, group, side_ref, pos_ref, nb_ref, data_ref, tmpl_ref, low_ref, high_ref,
    aligned_ref, first_ref, rest_ref, low_out, high_out, edge_out, hits_out, wide, acc, hits, sems,
):
    k = nb_ref.shape[1]
    span = 2 * k
    own = data_ref.shape[2]
    frames = data_ref.shape[1]

    copies = []
    for i in range(n_subjects + 1):
        body = data_ref.at[i] if i < n_subjects else tmpl_ref
        copies.append(pltpu.make_async_copy(body, wide.at[i, :, pl.ds(k, own)], sems.at[i, 0]))
        copies.append(pltpu.make_async_copy(low_ref.at[i], wide.at[i, :, pl.ds(0, k)], sems.at[i, 1]))
        copies.append(
            pltpu.make_async_copy(high_ref.at[i], wide.at[i, :, pl.ds(k + own, k)], sems.at[i, 2])
        )
    for copy in copies:
        copy.start()
    acc[...] = jnp.zeros_like(acc)
    hits[...] = jnp.zeros_like(hits)
    for copy in copies:
        copy.wait()

    @pl.when(side_ref[0] == 0)
    def _():
        wide[:, :, :k] = jnp.zeros((n_subjects + 1, frames, k), BF16)

    @pl.when(side_ref[1] == 0)
    def _():
        wide[:, :, k + own :] = jnp.zeros((n_subjects + 1, frames, k), BF16)

    spot = lax.broadcasted_iota(jnp.int32, (span, k), 0)
    lane = lax.broadcasted_iota(jnp.int32, (1, k), 1)
    ones = jnp.ones((ROWS, k), BF16)

    def place(ref, first, keep, value):
        left, right = value[:, :k], value[:, k:]
        ref[:, pl.ds(first, k)] += jnp.where(keep, left, 0.0)
        ref[:, pl.ds(first + k, k)] += right
        ref[:, pl.ds(first + span, k)] += jnp.where(keep, 0.0, left)

    def one_group(step, carry):
        members = []
        for member in range(group):
            c = step * group + member
            pos = pos_ref[c]
            first = pl.multiple_of((pos // k) * k, k)
            off = pos - first
            keep = lane >= off
            want = (nb_ref[pl.ds(c, 1), :] + (k + off)) & (span - 1)
            pick = jnp.where(spot == want, 1.0, 0.0).astype(BF16)
            members.append((first, keep, pick))

        def window(i, first, keep):
            a = wide[i, :, pl.ds(first, k)]
            b = wide[i, :, pl.ds(first + k, k)]
            d = wide[i, :, pl.ds(first + span, k)]
            return jnp.concatenate([jnp.where(keep, a, d), b], axis=1)

        xs = []
        m_ts = []
        for first, keep, pick in members:
            for i in range(n_subjects):
                xs.append(dot(window(i, first, keep), pick).astype(BF16))
            m_ts.append(dot(window(n_subjects, first, keep), pick))
        m_ts = [m.T.astype(BF16) for m in m_ts]
        zs = []
        for member in range(group):
            mine = xs[member * n_subjects : (member + 1) * n_subjects]
            crosses = dot(m_ts[member], jnp.concatenate(mine, axis=1))
            zs += [crosses[:, i * k : (i + 1) * k] for i in range(n_subjects)]
        zs = polar_factors_t(zs)
        spreads = []
        for n, z in enumerate(zs):
            pick = members[n // n_subjects][2]
            spreads.append(dot(pick, jnp.concatenate(split(z), axis=1)).astype(BF16))
        outs = [
            dot_t(jnp.concatenate([x, x], axis=1), spread) for x, spread in zip(xs, spreads)
        ]
        for member, (first, keep, pick) in enumerate(members):
            for i in range(n_subjects):
                place(acc.at[i], first, keep, outs[member * n_subjects + i])
            place(hits, first, keep, dot_t(ones, pick))
        return carry

    lax.fori_loop(0, n_centres // group, one_group, 0)

    low_out[:, :frames, :] = acc[:, :, :k]
    high_out[:, :frames, :] = acc[:, :, own + k :]
    for i in range(n_subjects):
        low_out[i, frames:, :] = hits[:, :k]
        high_out[i, frames:, :] = hits[:, own + k :]
    edge_out[:, :, :k] = acc[:, :, k:span]
    edge_out[:, :, k:] = acc[:, :, own : own + k]
    hits_out[:, :k] = hits[:, k:span]
    hits_out[:, k:] = hits[:, own : own + k]
    half = own // 2
    hits[...] = 1.0 / jnp.maximum(hits[...], 1.0)
    scale = hits[:, span:own]

    def one_rows(step, top):
        rows = pl.ds(pl.multiple_of(step * 2 * ROWS, 2 * ROWS), 2 * ROWS)
        both = jnp.concatenate([scale, scale], axis=0)
        total = jnp.zeros((2 * ROWS, own - span), F32)
        for i in range(n_subjects):
            mapped = acc[i, rows, span:own] * both
            aligned_ref[i, rows, k : own - k] = mapped.astype(BF16)
            total = total + mapped
        first_ref[rows, :half] = total[:, :half]
        rest_ref[rows, :] = total[:, half:]
        tops = jnp.abs(total[:, :half])
        while tops.shape[1] > k:
            tops = jnp.maximum(tops[:, : tops.shape[1] // 2], tops[:, tops.shape[1] // 2 :])
        return jnp.maximum(top, tops)

    top = lax.fori_loop(0, frames // (2 * ROWS), one_rows, jnp.zeros((2 * ROWS, k), F32))
    scale_out(first_ref, jnp.max(top, keepdims=True))


def scale_out(ref, top):
    width = ref.shape[1] - LANES
    power = jnp.clip(jnp.ceil(jnp.log(jnp.maximum(top, 1e-30)) * (1.0 / math.log(2.0))), -99.0, 99.0)
    ref[:, :width] = ref[:, :width] * jnp.exp2(HEADROOM - power)
    ref[:, width:] = jnp.broadcast_to(power, (ref.shape[0], LANES))


def align(data, template, low, high, sides, local_pos, neighbours):
    n_subjects, frames, own = data.shape
    n_centres, k = neighbours.shape
    n_wide = own + 2 * k
    group = math.gcd(n_centres, 8)
    vmem = pl.BlockSpec(memory_space=pltpu.VMEM)
    hbm = pl.BlockSpec(memory_space=pl.ANY)
    smem = pl.BlockSpec(memory_space=pltpu.SMEM)
    return pl.pallas_call(
        functools.partial(align_kernel, n_subjects, n_centres, group),
        out_shape=(
            jax.ShapeDtypeStruct((n_subjects, frames, own), BF16),
            jax.ShapeDtypeStruct((frames, own // 2 + LANES), F32),
            jax.ShapeDtypeStruct((frames, own // 2 - 2 * k), F32),
            jax.ShapeDtypeStruct((n_subjects, frames + ROWS, k), F32),
            jax.ShapeDtypeStruct((n_subjects, frames + ROWS, k), F32),
            jax.ShapeDtypeStruct((n_subjects, frames, 2 * k), F32),
            jax.ShapeDtypeStruct((ROWS, 2 * k), F32),
        ),
        in_specs=[smem, smem, vmem, hbm, hbm, hbm, hbm],
        out_specs=(vmem,) * 7,
        scratch_shapes=[
            pltpu.VMEM((n_subjects + 1, frames, n_wide), BF16),
            pltpu.VMEM((n_subjects, frames, n_wide), F32),
            pltpu.VMEM((ROWS, n_wide), F32),
            pltpu.SemaphoreType.DMA((n_subjects + 1, 3)),
        ],
        compiler_params=pltpu.CompilerParams(vmem_limit_bytes=32 * 1024 * 1024),
        name="align",
    )(sides, local_pos, neighbours, data, template, low, high)


def edges_kernel(
    n_subjects, side_ref, edge_ref, hits_ref, low_ref, high_ref, rest_ref, before_ref,
    aligned_ref, out_ref, left, right, sems,
):
    k = low_ref.shape[2]
    frames = edge_ref.shape[1]
    own = aligned_ref.shape[2]
    inner = rest_ref.shape[1]
    out_ref[:, :inner] = rest_ref[...]
    copies = []
    for n, (got_ref, block) in enumerate(((low_ref, left), (high_ref, right))):
        lanes = slice(n * k, (n + 1) * k)
        there = side_ref[n] > 0
        counts = hits_ref[:, lanes] + jnp.where(there, got_ref[0, frames:, :], 0.0)
        inverse = (1.0 / jnp.maximum(counts, 1.0))[:1]
        total = jnp.zeros((frames, k), F32)
        for i in range(n_subjects):
            mapped = edge_ref[i, :, lanes] + jnp.where(there, got_ref[i, :frames, :], 0.0)
            mapped = mapped * inverse
            block[i] = mapped.astype(BF16)
            total = total + mapped
        out_ref[:, inner + n * k : inner + (n + 1) * k] = total
        copy = pltpu.make_async_copy(
            block, aligned_ref.at[:, :, pl.ds(n * (own - k), k)], sems.at[n]
        )
        copy.start()
        copies.append(copy)
    scale_out(out_ref, jnp.max(jnp.abs(out_ref[:, : inner + 2 * k]), keepdims=True))
    for copy in copies:
        copy.wait()


def finish_edges(edges, edge_hits, from_low, from_high, sides, rest, aligned):
    n_subjects, frames, _ = edges.shape
    k = from_low.shape[2]
    vmem = pl.BlockSpec(memory_space=pltpu.VMEM)
    hbm = pl.BlockSpec(memory_space=pl.ANY)
    smem = pl.BlockSpec(memory_space=pltpu.SMEM)
    return pl.pallas_call(
        functools.partial(edges_kernel, n_subjects),
        out_shape=(
            jax.ShapeDtypeStruct(aligned.shape, BF16),
            jax.ShapeDtypeStruct((frames, rest.shape[1] + 2 * k + LANES), F32),
        ),
        in_specs=[smem, vmem, vmem, vmem, vmem, vmem, hbm],
        out_specs=(hbm, vmem),
        input_output_aliases={6: 0},
        scratch_shapes=[
            pltpu.VMEM((n_subjects, frames, k), BF16),
            pltpu.VMEM((n_subjects, frames, k), BF16),
            pltpu.SemaphoreType.DMA((2,)),
        ],
        compiler_params=pltpu.CompilerParams(vmem_limit_bytes=16 * 1024 * 1024),
        name="edges",
    )(sides, edges, edge_hits, from_low, from_high, rest, aligned)


def along_vert(up_value, down_value):
    size = lax.axis_size("vert")
    if size == 2:
        sent = jnp.where(lax.axis_index("vert") == 0, up_value, down_value)
        got = lax.ppermute(sent, "vert", [(0, 1), (1, 0)])
        return got, got
    up = [(i, i + 1) for i in range(size - 1)]
    down = [(i + 1, i) for i in range(size - 1)]
    return lax.ppermute(up_value, "vert", up), lax.ppermute(down_value, "vert", down)


class Hypercube:
    def __init__(self):
        self.size = lax.axis_size("subj")
        self.verts = lax.axis_size("vert")
        n_bits = self.size.bit_length() - 1
        bits = list(range(n_bits))
        self.phases = [bits[i : i + 2] for i in range(0, n_bits, 2)]

    def order(self, phase, v):
        return phase if v % 2 == 0 else phase[::-1]

    def mine(self, phase):
        s = lax.axis_index("subj")

        def number(bits):
            return sum(((s >> b) & 1) << i for i, b in enumerate(bits))

        even = number(self.order(phase, 0))
        odd = number(self.order(phase, 1))
        return jnp.where(lax.axis_index("vert") % 2 == 0, even, odd)

    def pairs(self, phase, m):
        out = []
        for s in range(self.size):
            for v in range(self.verts):
                mask = sum(((m >> i) & 1) << b for i, b in enumerate(self.order(phase, v)))
                out.append((s * self.verts + v, (s ^ mask) * self.verts + v))
        return out

    def swap(self, value, phase, m):
        return lax.ppermute(value, ("subj", "vert"), self.pairs(phase, m))

    def reduce(self, block):
        width = block.shape[1] - LANES
        for phase in self.phases:
            count = 1 << len(phase)
            rows = block.shape[0] // count
            j = self.mine(phase)
            parts = [lax.dynamic_slice_in_dim(block, j * rows, rows)]
            for m in range(1, count):
                sent = lax.dynamic_slice_in_dim(block, (j ^ m) * rows, rows).astype(jnp.float16)
                parts.append(self.swap(sent, phase, m).astype(F32))
            powers = [part[:, width : width + 1] for part in parts]
            top = functools.reduce(jnp.maximum, powers)
            total = sum(part[:, :width] * jnp.exp2(p - top) for part, p in zip(parts, powers))
            block = jnp.concatenate([total, jnp.broadcast_to(top, (rows, LANES))], axis=1)
        return block[:, :width], block[0, width]

    def gather(self, value):
        for phase in reversed(self.phases):
            count = 1 << len(phase)
            j = self.mine(phase)
            parts = [value] + [self.swap(value, phase, m) for m in range(1, count)]
            placed = []
            for q in range(count):
                chosen = parts[0]
                for m in range(1, count):
                    chosen = jnp.where((j ^ q) == m, parts[m], chosen)
                placed.append(chosen)
            value = jnp.concatenate(placed, axis=0)
        return value


def local(data, template, centres, neighbours):
    k = neighbours.shape[1]
    n_subjects, frames, own = data.shape
    v = lax.axis_index("vert")
    sides = jnp.stack([v > 0, v < lax.axis_size("vert") - 1]).astype(jnp.int32)
    first_edge = jnp.concatenate([data[:, :, :k], template[None, :, :k]], axis=0)
    last_edge = jnp.concatenate([data[:, :, own - k :], template[None, :, own - k :]], axis=0)
    low, high = along_vert(last_edge, first_edge)
    local_pos = centres - v * own
    aligned, first, rest, low_out, high_out, edges, edge_hits = align(
        data, template, low, high, sides, local_pos, neighbours
    )
    from_low, from_high = along_vert(high_out, low_out)
    aligned, rest = finish_edges(edges, edge_hits, from_low, from_high, sides, rest, aligned)
    cube = Hypercube()
    subjects = n_subjects * lax.axis_size("subj")
    wholes = []
    for block in (first, rest):
        total, power = cube.reduce(block)
        whole = cube.gather(total.astype(jnp.float16))
        wholes.append(whole.astype(F32) * (jnp.exp2(power - HEADROOM) * (1.0 / subjects)))
    begin, end = wholes
    inner = end.shape[1] - 2 * k
    new_template = jnp.concatenate(
        [end[:, inner : inner + k], begin, end[:, :inner], end[:, inner + k :]], axis=1
    )
    return aligned, new_template


def solution(mesh):
    in_specs = (P("subj", None, "vert"), P(None, "vert"), P("vert"), P("vert", None))
    out_specs = (P("subj", None, "vert"), P(None, "vert"))
    return jax.shard_map(local, mesh=mesh, in_specs=in_specs, out_specs=out_specs, check_vma=False)
```

time: 140 us -> 91.6 us (0.65)
  Pallas kernels: 59.4 us -> 17.1 us
  between operations: 7.4 us -> 2.39 us
  waiting for transfers between devices: 22 us -> 25.3 us
  local copies, waits for them, and re-layouts: 9.16 us -> 7.08 us
  other arithmetic: 7.67 us -> 5.6 us
    pallas_call x1, Pallas kernels: 59.4 us -> 15.7 us  [align(): pl.pallas_call(functools.partial(align_kernel, n_subjects, n_centres, gro...]
    ppermute x4 -> x2, starting transfers between devices: 8 us -> 0.59 us  [along_vert(): got = lax.ppermute(sent, 'vert', [(0, 1), (1, 0)])]
    ppermute x18 -> x24, starting transfers between devices: 25.9 us -> 33.2 us  [swap(): return lax.ppermute(value, ('subj', 'vert'), self.pairs(phase, m))]
    ppermute x18 -> x24, waiting for transfers between devices: 20 us -> 24.9 us  [swap(): return lax.ppermute(value, ('subj', 'vert'), self.pairs(phase, m))]
    slice x11 -> x4, local copies, waits for them, and re-layouts: 4.36 us -> 1.18 us  [the longest x2 1.1 us: reduce(): return (block[:, :width], block[0, width])]
    unnamed x6 -> x14, local copies, waits for them, and re-layouts: 1.49 us -> 3.79 us
    ppermute x4 -> x2, waiting for transfers between devices: 1.96 us -> 0.34 us  [along_vert(): got = lax.ppermute(sent, 'vert', [(0, 1), (1, 0)])]
    concatenate x2 -> x3, other arithmetic: 0.04 us -> 1.55 us  [the longest x1 1.5 us: local(): jnp.concatenate([end[:, inner:inner + k], begin, end[:, :inner], end[:, i...]
  transfers between devices with their start and end apart: 22 -> 26, of which waited for: 9 -> 15; matrix products, arithmetic and copies ran while one was open for 5% -> 4% of each run, Pallas kernels for 0% -> 2%
where the time goes in v1:
time: 91.6 us; the launch traced here: 91.3 us
  starting transfers between devices  33.8 us (37%)
  waiting for transfers between devices  25.3 us (28%)
  Pallas kernels  17.1 us (19%)
  local copies, waits for them, and re-layouts  7.08 us (8%)
  other arithmetic  5.6 us (6%)
  between operations  2.39 us (3%)
    ppermute x24, starting transfers between devices, swap(): return lax.ppermute(value, ('subj', 'vert'), self.pairs(phase, m))  33.2 us
    ppermute x24, waiting for transfers between devices, swap(): return lax.ppermute(value, ('subj', 'vert'), self.pairs(phase, m))  24.9 us
    pallas_call x1, Pallas kernels, align(): pl.pallas_call(functools.partial(align_kernel, n_subjects, n_centres, gro...  15.7 us
    unnamed x14, local copies, waits for them, and re-layouts  3.79 us
  transfers between devices with their start and end apart: 26, of which 15 were waited for; matrix products, arithmetic and copies ran while one was open for 4% of the time, Pallas kernels for 2%

profile of v1, /device:TPU:0, one launch (start us, length us, event | category | flops | bytes accessed | tf_op | source)
XLA Modules:
  0.0 91.3 jit_solution(2904697756123568827)
XLA Ops:
  0.6 1.1 %fusion.30 = (bf16[2,256,128]{2,1,0:T(8,128)(2,1)S(1)}, bf16[2,256,128]{2,1,0:T(8,128)(2,1)S(1)}) fusion(bf16[2,256,2048]{2,1,0:T(8,128)(2,1)} %data_ref.1), kind=kLoop, calls=%fused_computation.115 | loop fusion | bytes 524288 | tf_op jit(solution)/shard_map/slice | solution.py:353
  1.7 0.9 slice_bitcast_fusion
  2.7 0.5 collective-permute-start
  3.2 0.1 add_convert_fusion.side_ref
  3.3 0.7 broadcast_subtract_fusion.pos_ref
  3.9 0.3 collective-permute-done.low_ref.high_ref
  4.3 1.6 %copy-done = bf16[2,256,2048]{2,1,0:T(8,128)(2,1)S(1)} copy-done((bf16[2,256,2048]{2,1,0:T(8,128)(2,1)S(1)}, bf16[2,256,2048]{2,1,0:T(8,128)(2,1)}, u32[]{:S(2)}) %copy-start) | copy-done | bytes 2097176
  5.9 0.7 copy-done.6
  6.5 15.7 %align.1 = (bf16[2,256,2048]{2,1,0:T(8,128)(2,1)}, f32[256,1152]{1,0:T(8,128)S(1)}, f32[256,768]{1,0:T(8,128)S(1)}, f32[2,264,128]{2,1,0:T(8,128)S(1)}, f32[2,26...) custom-call(s32[2]{0:T(128)S(1)} %add_convert_fusion.side_ref, ...), custom_call_target="tpu_custom_call" | custom-call | tf_op jit(solution)/shard_map/align/pallas_call | solution.py:193
  22.3 0.8 copy-done.2
  23.1 0.7 copy-done.4
  23.8 0.7 dynamic-slice_convert_fusion.2
  24.5 2.9 %collective-permute-start.14 = (f16[64,1152]{1,0:T(8,128)(2,1)S(1)}, f16[64,1152]{1,0:T(8,128)(2,1)S(1)}, u32[]{:S(2)}, u32[]{:S(2)}) collective-permute-start(f16[64,1152]{1,0:T(8,128)(2,1)S(1)} %get-tuple-element.42), channel_id=1, source_target_pairs={{0,2},{1,5},{2,0},{3,7},{4,6},{5,1},{6,4},{7,3},{8,10},{9,13},{10,... | collective-permute-start | bytes 442376 | tf_op jit(solution)/shard_map/ppermute | solution.py:315
  27.4 1.5 %collective-permute-start.15 = (f16[64,1152]{1,0:T(8,128)(2,1)S(1)}, f16[64,1152]{1,0:T(8,128)(2,1)S(1)}, u32[]{:S(2)}, u32[]{:S(2)}) collective-permute-start(f16[64,1152]{1,0:T(8,128)(2,1)S(1)} %get-tuple-element.44), channel_id=1, source_target_pairs={{0,4},{1,3},{2,6},{3,1},{4,0},{5,7},{6,2},{7,5},{8,12},{9,11},{10,... | collective-permute-start | bytes 442376 | tf_op jit(solution)/shard_map/ppermute | solution.py:315
  28.9 2.4 %collective-permute-done.14 = f16[64,1152]{1,0:T(8,128)(2,1)S(1)} collective-permute-done((f16[64,1152]{1,0:T(8,128)(2,1)S(1)}, f16[64,1152]{1,0:T(8,128)(2,1)S(1)}, u32[]{:S(2)}, u32[]{:S(2)}) %collective-permute-start.14) | collective-permute-done | bytes 147488 | tf_op jit(solution)/shard_map/ppermute | solution.py:315
  31.3 3.5 %collective-permute-done.15 = f16[64,1152]{1,0:T(8,128)(2,1)S(1)} collective-permute-done((f16[64,1152]{1,0:T(8,128)(2,1)S(1)}, f16[64,1152]{1,0:T(8,128)(2,1)S(1)}, u32[]{:S(2)}, u32[]{:S(2)}) %collective-permute-start.15) | collective-permute-done | bytes 147488 | tf_op jit(solution)/shard_map/ppermute | solution.py:315
  34.8 1.1 %collective-permute-done.16 = f16[64,1152]{1,0:T(8,128)(2,1)S(1)} collective-permute-done((f16[64,1152]{1,0:T(8,128)(2,1)}, f16[64,1152]{1,0:T(8,128)(2,1)S(1)}, u32[]{:S(2)}, u32[]{:S(2)}) %collective-permute-start.16) | collective-permute-done | bytes 147488 | tf_op jit(solution)/shard_map/ppermute | solution.py:315
  35.9 0.2 fusion.28
  36.1 0.2 fusion
  36.4 1.9 %collective-permute-start.17 = (f16[16,1152]{1,0:T(8,128)(2,1)S(1)}, f16[16,1152]{1,0:T(8,128)(2,1)S(1)}, u32[]{:S(2)}, u32[]{:S(2)}) collective-permute-start(f16[16,1152]{1,0:T(8,128)(2,1)S(1)} %get-tuple-element.61), channel_id=1, source_target_pairs={{0,8},{1,17},{2,10},{3,19},{4,12},{5,21},{6,14},{7,23},{8,0},{9,25... | collective-permute-start | bytes 110600 | tf_op jit(solution)/shard_map/ppermute | solution.py:315
  38.3 2.6 %collective-permute-start.18 = (f16[16,1152]{1,0:T(8,128)(2,1)S(1)}, f16[16,1152]{1,0:T(8,128)(2,1)S(1)}, u32[]{:S(2)}, u32[]{:S(2)}) collective-permute-start(f16[16,1152]{1,0:T(8,128)(2,1)S(1)} %get-tuple-element.62), channel_id=1, source_target_pairs={{0,16},{1,9},{2,18},{3,11},{4,20},{5,13},{6,22},{7,15},{8,24},{9,1... | collective-permute-start | bytes 110600 | tf_op jit(solution)/shard_map/ppermute | solution.py:315
  41.0 2.5 %collective-permute-done.18 = f16[16,1152]{1,0:T(8,128)(2,1)S(1)} collective-permute-done((f16[16,1152]{1,0:T(8,128)(2,1)S(1)}, f16[16,1152]{1,0:T(8,128)(2,1)S(1)}, u32[]{:S(2)}, u32[]{:S(2)}) %collective-permute-start.18) | collective-permute-done | bytes 36896 | tf_op jit(solution)/shard_map/ppermute | solution.py:315
  43.5 3.1 %collective-permute-done.19 = f16[16,1152]{1,0:T(8,128)(2,1)S(1)} collective-permute-done((f16[16,1152]{1,0:T(8,128)(2,1)S(1)}, f16[16,1152]{1,0:T(8,128)(2,1)S(1)}, u32[]{:S(2)}, u32[]{:S(2)}) %collective-permute-start.19) | collective-permute-done | bytes 36896 | tf_op jit(solution)/shard_map/ppermute | solution.py:315
  46.6 0.2 exponential_reduce_fusion.11
  46.8 0.1 fusion.21
  46.9 0.5 collective-permute-start.20
  47.3 4.0 %collective-permute-start.22 = (f16[16,1024]{1,0:T(8,128)(2,1)S(1)}, f16[16,1024]{1,0:T(8,128)(2,1)S(1)}, u32[]{:S(2)}, u32[]{:S(2)}) collective-permute-start(f16[16,1024]{1,0:T(8,128)(2,1)S(1)} %fusion.21), channel_id=1, source_target_pairs={{0,8},{1,17},{2,10},{3,19},{4,12},{5,21},{6,14},{7,23},{8,0},{9,25... | collective-permute-start | bytes 98312 | tf_op jit(solution)/shard_map/ppermute | solution.py:315
  51.3 0.6 slice.198
  52.7 1.4 %edges.1 = (bf16[2,256,2048]{2,1,0:T(8,128)(2,1)}, f32[256,1152]{1,0:T(8,128)S(1)}) custom-call(s32[2]{0:T(128)S(1)} %add_convert_fusion.side_ref, f32[2,256,256]{2,1,0:T(8,128)S(1)} %copy-done.3, f32[8,256]{1,0:T(8,128)S(1)} %get-tuple-element.12.hits_ref, ...), custom_call_target="tpu_custom_call", output_to_operand_aliasing={{0}: (6, {})} | custom-call | tf_op jit(solution)/shard_map/edges/pallas_call | solution.py:255
  54.1 1.7 %collective-permute-start.2 = (f16[64,1152]{1,0:T(8,128)(2,1)S(1)}, f16[64,1152]{1,0:T(8,128)(2,1)S(1)}, u32[]{:S(2)}, u32[]{:S(2)}) collective-permute-start(f16[64,1152]{1,0:T(8,128)(2,1)S(1)} %get-tuple-element.45), channel_id=1, source_target_pairs={{0,2},{1,5},{2,0},{3,7},{4,6},{5,1},{6,4},{7,3},{8,10},{9,13},{10,... | collective-permute-start | bytes 442376 | tf_op jit(solution)/shard_map/ppermute | solution.py:315
  55.8 0.6 collective-permute-start.3
  56.5 1.2 %collective-permute-start.4 = (f16[64,1152]{1,0:T(8,128)(2,1)S(1)}, f16[64,1152]{1,0:T(8,128)(2,1)S(1)}, u32[]{:S(2)}, u32[]{:S(2)}) collective-permute-start(f16[64,1152]{1,0:T(8,128)(2,1)S(1)} %get-tuple-element.46), channel_id=1, source_target_pairs={{0,6},{1,7},{2,4},{3,5},{4,2},{5,3},{6,0},{7,1},{8,14},{9,15},{10,... | collective-permute-start | bytes 442376 | tf_op jit(solution)/shard_map/ppermute | solution.py:315
  57.8 1.7 %collective-permute-start.23 = (f16[64,1024]{1,0:T(8,128)(2,1)S(1)}, f16[64,1024]{1,0:T(8,128)(2,1)S(1)}, u32[]{:S(2)}, u32[]{:S(2)}) collective-permute-start(f16[64,1024]{1,0:T(8,128)(2,1)S(1)} %pad_maximum_fusion.2), channel_id=1, source_target_pairs={{0,6},{1,7},{2,4},{3,5},{4,2},{5,3},{6,0},{7,1},{8,14},{9,15},{10,... | collective-permute-start | bytes 393224 | tf_op jit(solution)/shard_map/ppermute | solution.py:315
  59.6 1.4 %collective-permute-start.24 = (f16[64,1024]{1,0:T(8,128)(2,1)S(1)}, f16[64,1024]{1,0:T(8,128)(2,1)S(1)}, u32[]{:S(2)}, u32[]{:S(2)}) collective-permute-start(f16[64,1024]{1,0:T(8,128)(2,1)S(1)} %pad_maximum_fusion.2), channel_id=1, source_target_pairs={{0,4},{1,3},{2,6},{3,1},{4,0},{5,7},{6,2},{7,5},{8,12},{9,11},{10,... | collective-permute-start | bytes 393224 | tf_op jit(solution)/shard_map/ppermute | solution.py:315
  61.0 1.6 %collective-permute-start.25 = (f16[64,1024]{1,0:T(8,128)(2,1)S(1)}, f16[64,1024]{1,0:T(8,128)(2,1)S(1)}, u32[]{:S(2)}, u32[]{:S(2)}) collective-permute-start(f16[64,1024]{1,0:T(8,128)(2,1)S(1)} %pad_maximum_fusion.2), channel_id=1, source_target_pairs={{0,2},{1,5},{2,0},{3,7},{4,6},{5,1},{6,4},{7,3},{8,10},{9,13},{10,... | collective-permute-start | bytes 393224 | tf_op jit(solution)/shard_map/ppermute | solution.py:315
  62.6 3.7 %collective-permute-done.3 = f16[64,1152]{1,0:T(8,128)(2,1)S(1)} collective-permute-done((f16[64,1152]{1,0:T(8,128)(2,1)S(1)}, f16[64,1152]{1,0:T(8,128)(2,1)S(1)}, u32[]{:S(2)}, u32[]{:S(2)}) %collective-permute-start.3) | collective-permute-done | bytes 147488 | tf_op jit(solution)/shard_map/ppermute | solution.py:315
  66.4 0.2 fusion.29
  66.6 0.1 fusion.3
  66.9 0.5 collective-permute-start.5
  67.4 1.0 %collective-permute-start.6 = (f16[16,1152]{1,0:T(8,128)(2,1)S(1)}, f16[16,1152]{1,0:T(8,128)(2,1)S(1)}, u32[]{:S(2)}, u32[]{:S(2)}) collective-permute-start(f16[16,1152]{1,0:T(8,128)(2,1)S(1)} %get-tuple-element.66), channel_id=1, source_target_pairs={{0,16},{1,9},{2,18},{3,11},{4,20},{5,13},{6,22},{7,15},{8,24},{9,1... | collective-permute-start | bytes 110600 | tf_op jit(solution)/shard_map/ppermute | solution.py:315
  68.3 3.0 %collective-permute-start.7 = (f16[16,1152]{1,0:T(8,128)(2,1)S(1)}, f16[16,1152]{1,0:T(8,128)(2,1)S(1)}, u32[]{:S(2)}, u32[]{:S(2)}) collective-permute-start(f16[16,1152]{1,0:T(8,128)(2,1)S(1)} %get-tuple-element.67), channel_id=1, source_target_pairs={{0,24},{1,25},{2,26},{3,27},{4,28},{5,29},{6,30},{7,31},{8,16},{9,... | collective-permute-start | bytes 110600 | tf_op jit(solution)/shard_map/ppermute | solution.py:315
  71.3 0.1 select_select_fusion.2
  71.5 0.8 collective-permute-done.6
  72.3 1.8 %collective-permute-done.7 = f16[16,1152]{1,0:T(8,128)(2,1)S(1)} collective-permute-done((f16[16,1152]{1,0:T(8,128)(2,1)S(1)}, f16[16,1152]{1,0:T(8,128)(2,1)S(1)}, u32[]{:S(2)}, u32[]{:S(2)}) %collective-permute-start.7) | collective-permute-done | bytes 36896 | tf_op jit(solution)/shard_map/ppermute | solution.py:315
  74.1 0.2 exponential_reduce_fusion.15
  74.3 0.1 fusion.25
  74.5 3.0 %collective-permute-start.8 = (f16[16,1024]{1,0:T(8,128)(2,1)S(1)}, f16[16,1024]{1,0:T(8,128)(2,1)S(1)}, u32[]{:S(2)}, u32[]{:S(2)}) collective-permute-start(f16[16,1024]{1,0:T(8,128)(2,1)S(1)} %fusion.25), channel_id=1, source_target_pairs={{0,24},{1,25},{2,26},{3,27},{4,28},{5,29},{6,30},{7,31},{8,16},{9,... | collective-permute-start | bytes 98312 | tf_op jit(solution)/shard_map/ppermute | solution.py:315
  77.5 0.5 collective-permute-start.9
  78.0 0.1 select_select_fusion.3
  78.1 0.2 collective-permute-done.10
  78.4 1.9 %collective-permute-done.8 = f16[16,1024]{1,0:T(8,128)(2,1)S(1)} collective-permute-done((f16[16,1024]{1,0:T(8,128)(2,1)S(1)}, f16[16,1024]{1,0:T(8,128)(2,1)S(1)}, u32[]{:S(2)}, u32[]{:S(2)}) %collective-permute-start.8) | collective-permute-done | bytes 32800 | tf_op jit(solution)/shard_map/ppermute | solution.py:315
  80.2 2.1 %collective-permute-done.9 = f16[16,1024]{1,0:T(8,128)(2,1)S(1)} collective-permute-done((f16[16,1024]{1,0:T(8,128)(2,1)S(1)}, f16[16,1024]{1,0:T(8,128)(2,1)S(1)}, u32[]{:S(2)}, u32[]{:S(2)}) %collective-permute-start.9) | collective-permute-done | bytes 32800 | tf_op jit(solution)/shard_map/ppermute | solution.py:315
  82.4 0.1 collective-permute-start.11
  82.5 0.9 collective-permute-start.12
  83.4 2.6 %collective-permute-start.13 = (f16[64,1024]{1,0:T(8,128)(2,1)S(1)}, f16[64,1024]{1,0:T(8,128)(2,1)S(1)}, u32[]{:S(2)}, u32[]{:S(2)}) collective-permute-start(f16[64,1024]{1,0:T(8,128)(2,1)S(1)} %pad_maximum_fusion.1), channel_id=1, source_target_pairs={{0,2},{1,5},{2,0},{3,7},{4,6},{5,1},{6,4},{7,3},{8,10},{9,13},{10,... | collective-permute-start | bytes 393224 | tf_op jit(solution)/shard_map/ppermute | solution.py:315
  86.0 0.2 convert_multiply_fusion
  86.2 0.5 slice.182
  87.4 1.1 %collective-permute-done.11 = f16[64,1024]{1,0:T(8,128)(2,1)S(1)} collective-permute-done((f16[64,1024]{1,0:T(8,128)(2,1)S(1)}, f16[64,1024]{1,0:T(8,128)(2,1)S(1)}, u32[]{:S(2)}, u32[]{:S(2)}) %collective-permute-start.11) | collective-permute-done | bytes 131104 | tf_op jit(solution)/shard_map/ppermute | solution.py:315
  88.5 0.5 collective-permute-done.12
  88.9 0.3 collective-permute-done.13
  89.2 0.1 select_select_fusion.6
  89.3 0.1 select_select_fusion.7
  89.5 0.2 convert_multiply_fusion.1
  89.8 1.5 %pad_maximum_fusion = f32[256,2048]{1,0:T(8,128)} fusion(f32[256,128]{1,0:T(8,128)S(1)} %get-tuple-element.49, f32[256,768]{1,0:T(8,128)S(1)} %slice.199, f32[256,1024]{1,0:T(8,128)S(1)} %convert_multiply_fusion, f32[256,128]{1,0:T(8,128)S(1)} %get-tuple-element.48), kind=kLoop, calls=%fused_computation | loop fusion | flops 1572864 | bytes 4194304 | tf_op jit(solution)/shard_map/concatenate | solution.py:371
  (51 shorter events, 1.0 us)
Async XLA Ops:
  0.6 3.6 %copy-start.1 = (bf16[256,2048]{1,0:T(8,128)(2,1)S(1)}, bf16[256,2048]{1,0:T(8,128)(2,1)}, u32[]{:S(2)}) copy-start(bf16[256,2048]{1,0:T(8,128)(2,1)} %tmpl_ref.1) | copy-start | bytes 3145732
  2.7 1.6 %collective-permute-start = (bf16[3,256,128]{2,1,0:T(8,128)(2,1)S(1)}, bf16[3,256,128]{2,1,0:T(8,128)(2,1)S(1)}, u32[]{:S(2)}, u32[]{:S(2)}) collective-permute-start(bf16[3,256,128]{2,1,0:T(8,128)(2,1)S(1)} %maximum_select_fusion), channel_id=1, source_target_pairs={{0,1},{1,0},{2,3},{3,2},{4,5},{5,4},{6,7},{7,6},{8,9},{9,8},{10,11... | collective-permute-start | bytes 589832 | tf_op jit(solution)/shard_map/ppermute | solution.py:278
  4.3 1.6 %copy-start = (bf16[2,256,2048]{2,1,0:T(8,128)(2,1)S(1)}, bf16[2,256,2048]{2,1,0:T(8,128)(2,1)}, u32[]{:S(2)}) copy-start(bf16[2,256,2048]{2,1,0:T(8,128)(2,1)} %data_ref.1) | copy-start | bytes 6291460
  5.9 0.7 copy-start.6
  22.3 0.8 copy-start.2
  23.1 0.7 copy-start.4
  23.8 17.1 %copy-start.5 = (f32[2,264,128]{2,1,0:T(8,128)S(1)}, f32[2,264,128]{2,1,0:T(8,128)}, u32[]{:S(2)}) copy-start(f32[2,264,128]{2,1,0:T(8,128)} %copy-done.4) | copy-start | bytes 811012
  24.5 6.8 %collective-permute-start.14 = (f16[64,1152]{1,0:T(8,128)(2,1)S(1)}, f16[64,1152]{1,0:T(8,128)(2,1)S(1)}, u32[]{:S(2)}, u32[]{:S(2)}) collective-permute-start(f16[64,1152]{1,0:T(8,128)(2,1)S(1)} %get-tuple-element.42), channel_id=1, source_target_pairs={{0,2},{1,5},{2,0},{3,7},{4,6},{5,1},{6,4},{7,3},{8,10},{9,13},{10,... | collective-permute-start | bytes 442376 | tf_op jit(solution)/shard_map/ppermute | solution.py:315
  27.4 7.4 %collective-permute-start.15 = (f16[64,1152]{1,0:T(8,128)(2,1)S(1)}, f16[64,1152]{1,0:T(8,128)(2,1)S(1)}, u32[]{:S(2)}, u32[]{:S(2)}) collective-permute-start(f16[64,1152]{1,0:T(8,128)(2,1)S(1)} %get-tuple-element.44), channel_id=1, source_target_pairs={{0,4},{1,3},{2,6},{3,1},{4,0},{5,7},{6,2},{7,5},{8,12},{9,11},{10,... | collective-permute-start | bytes 442376 | tf_op jit(solution)/shard_map/ppermute | solution.py:315
  28.9 7.0 %collective-permute-start.16 = (f16[64,1152]{1,0:T(8,128)(2,1)}, f16[64,1152]{1,0:T(8,128)(2,1)S(1)}, u32[]{:S(2)}, u32[]{:S(2)}) collective-permute-start(f16[64,1152]{1,0:T(8,128)(2,1)} %get-tuple-element.43), channel_id=1, source_target_pairs={{0,6},{1,7},{2,4},{3,5},{4,2},{5,3},{6,0},{7,1},{8,14},{9,15},{10,... | collective-permute-start | bytes 442376 | tf_op jit(solution)/shard_map/ppermute | solution.py:315
  31.3 21.4 %copy-start.3 = (f32[2,256,256]{2,1,0:T(8,128)S(1)}, f32[2,256,256]{2,1,0:T(8,128)}, u32[]{:S(2)}) copy-start(f32[2,256,256]{2,1,0:T(8,128)} %copy-done.2) | copy-start | bytes 1572868
  36.4 4.6 %collective-permute-start.17 = (f16[16,1152]{1,0:T(8,128)(2,1)S(1)}, f16[16,1152]{1,0:T(8,128)(2,1)S(1)}, u32[]{:S(2)}, u32[]{:S(2)}) collective-permute-start(f16[16,1152]{1,0:T(8,128)(2,1)S(1)} %get-tuple-element.61), channel_id=1, source_target_pairs={{0,8},{1,17},{2,10},{3,19},{4,12},{5,21},{6,14},{7,23},{8,0},{9,25... | collective-permute-start | bytes 110600 | tf_op jit(solution)/shard_map/ppermute | solution.py:315
  38.3 5.2 %collective-permute-start.18 = (f16[16,1152]{1,0:T(8,128)(2,1)S(1)}, f16[16,1152]{1,0:T(8,128)(2,1)S(1)}, u32[]{:S(2)}, u32[]{:S(2)}) collective-permute-start(f16[16,1152]{1,0:T(8,128)(2,1)S(1)} %get-tuple-element.62), channel_id=1, source_target_pairs={{0,16},{1,9},{2,18},{3,11},{4,20},{5,13},{6,22},{7,15},{8,24},{9,1... | collective-permute-start | bytes 110600 | tf_op jit(solution)/shard_map/ppermute | solution.py:315
  40.9 5.8 %collective-permute-start.19 = (f16[16,1152]{1,0:T(8,128)(2,1)S(1)}, f16[16,1152]{1,0:T(8,128)(2,1)S(1)}, u32[]{:S(2)}, u32[]{:S(2)}) collective-permute-start(f16[16,1152]{1,0:T(8,128)(2,1)S(1)} %get-tuple-element.63), channel_id=1, source_target_pairs={{0,24},{1,25},{2,26},{3,27},{4,28},{5,29},{6,30},{7,31},{8,16},{9,... | collective-permute-start | bytes 110600 | tf_op jit(solution)/shard_map/ppermute | solution.py:315
  40.9 11.8 %collective-permute-start.1 = (f32[2,264,128]{2,1,0:T(8,128)S(1)}, f32[2,264,128]{2,1,0:T(8,128)S(1)}, u32[]{:S(2)}, u32[]{:S(2)}) collective-permute-start(f32[2,264,128]{2,1,0:T(8,128)S(1)} %broadcast_select_fusion), channel_id=1, source_target_pairs={{0,1},{1,0},{2,3},{3,2},{4,5},{5,4},{6,7},{7,6},{8,9},{9,8},{10,11... | collective-permute-start | bytes 811016 | tf_op jit(solution)/shard_map/ppermute | solution.py:278
  46.9 9.6 %collective-permute-start.20 = (f16[16,1024]{1,0:T(8,128)(2,1)S(1)}, f16[16,1024]{1,0:T(8,128)(2,1)S(1)}, u32[]{:S(2)}, u32[]{:S(2)}) collective-permute-start(f16[16,1024]{1,0:T(8,128)(2,1)S(1)} %fusion.21), channel_id=1, source_target_pairs={{0,24},{1,25},{2,26},{3,27},{4,28},{5,29},{6,30},{7,31},{8,16},{9,... | collective-permute-start | bytes 98312 | tf_op jit(solution)/shard_map/ppermute | solution.py:315
  47.3 10.4 %collective-permute-start.21 = (f16[16,1024]{1,0:T(8,128)(2,1)S(1)}, f16[16,1024]{1,0:T(8,128)(2,1)S(1)}, u32[]{:S(2)}, u32[]{:S(2)}) collective-permute-start(f16[16,1024]{1,0:T(8,128)(2,1)S(1)} %fusion.21), channel_id=1, source_target_pairs={{0,16},{1,9},{2,18},{3,11},{4,20},{5,13},{6,22},{7,15},{8,24},{9,1... | collective-permute-start | bytes 98312 | tf_op jit(solution)/shard_map/ppermute | solution.py:315
  47.3 10.4 %collective-permute-start.22 = (f16[16,1024]{1,0:T(8,128)(2,1)S(1)}, f16[16,1024]{1,0:T(8,128)(2,1)S(1)}, u32[]{:S(2)}, u32[]{:S(2)}) collective-permute-start(f16[16,1024]{1,0:T(8,128)(2,1)S(1)} %fusion.21), channel_id=1, source_target_pairs={{0,8},{1,17},{2,10},{3,19},{4,12},{5,21},{6,14},{7,23},{8,0},{9,25... | collective-permute-start | bytes 98312 | tf_op jit(solution)/shard_map/ppermute | solution.py:315
  54.1 6.8 %collective-permute-start.2 = (f16[64,1152]{1,0:T(8,128)(2,1)S(1)}, f16[64,1152]{1,0:T(8,128)(2,1)S(1)}, u32[]{:S(2)}, u32[]{:S(2)}) collective-permute-start(f16[64,1152]{1,0:T(8,128)(2,1)S(1)} %get-tuple-element.45), channel_id=1, source_target_pairs={{0,2},{1,5},{2,0},{3,7},{4,6},{5,1},{6,4},{7,3},{8,10},{9,13},{10,... | collective-permute-start | bytes 442376 | tf_op jit(solution)/shard_map/ppermute | solution.py:315
  55.8 10.5 %collective-permute-start.3 = (f16[64,1152]{1,0:T(8,128)(2,1)S(1)}, f16[64,1152]{1,0:T(8,128)(2,1)S(1)}, u32[]{:S(2)}, u32[]{:S(2)}) collective-permute-start(f16[64,1152]{1,0:T(8,128)(2,1)S(1)} %get-tuple-element.47), channel_id=1, source_target_pairs={{0,4},{1,3},{2,6},{3,1},{4,0},{5,7},{6,2},{7,5},{8,12},{9,11},{10,... | collective-permute-start | bytes 442376 | tf_op jit(solution)/shard_map/ppermute | solution.py:315
  56.5 9.9 %collective-permute-start.4 = (f16[64,1152]{1,0:T(8,128)(2,1)S(1)}, f16[64,1152]{1,0:T(8,128)(2,1)S(1)}, u32[]{:S(2)}, u32[]{:S(2)}) collective-permute-start(f16[64,1152]{1,0:T(8,128)(2,1)S(1)} %get-tuple-element.46), channel_id=1, source_target_pairs={{0,6},{1,7},{2,4},{3,5},{4,2},{5,3},{6,0},{7,1},{8,14},{9,15},{10,... | collective-permute-start | bytes 442376 | tf_op jit(solution)/shard_map/ppermute | solution.py:315
  57.8 10.5 %collective-permute-start.23 = (f16[64,1024]{1,0:T(8,128)(2,1)S(1)}, f16[64,1024]{1,0:T(8,128)(2,1)S(1)}, u32[]{:S(2)}, u32[]{:S(2)}) collective-permute-start(f16[64,1024]{1,0:T(8,128)(2,1)S(1)} %pad_maximum_fusion.2), channel_id=1, source_target_pairs={{0,6},{1,7},{2,4},{3,5},{4,2},{5,3},{6,0},{7,1},{8,14},{9,15},{10,... | collective-permute-start | bytes 393224 | tf_op jit(solution)/shard_map/ppermute | solution.py:315
  59.6 11.8 %collective-permute-start.24 = (f16[64,1024]{1,0:T(8,128)(2,1)S(1)}, f16[64,1024]{1,0:T(8,128)(2,1)S(1)}, u32[]{:S(2)}, u32[]{:S(2)}) collective-permute-start(f16[64,1024]{1,0:T(8,128)(2,1)S(1)} %pad_maximum_fusion.2), channel_id=1, source_target_pairs={{0,4},{1,3},{2,6},{3,1},{4,0},{5,7},{6,2},{7,5},{8,12},{9,11},{10,... | collective-permute-start | bytes 393224 | tf_op jit(solution)/shard_map/ppermute | solution.py:315
  61.0 10.3 %collective-permute-start.25 = (f16[64,1024]{1,0:T(8,128)(2,1)S(1)}, f16[64,1024]{1,0:T(8,128)(2,1)S(1)}, u32[]{:S(2)}, u32[]{:S(2)}) collective-permute-start(f16[64,1024]{1,0:T(8,128)(2,1)S(1)} %pad_maximum_fusion.2), channel_id=1, source_target_pairs={{0,2},{1,5},{2,0},{3,7},{4,6},{5,1},{6,4},{7,3},{8,10},{9,13},{10,... | collective-permute-start | bytes 393224 | tf_op jit(solution)/shard_map/ppermute | solution.py:315
  66.9 4.6 %collective-permute-start.5 = (f16[16,1152]{1,0:T(8,128)(2,1)S(1)}, f16[16,1152]{1,0:T(8,128)(2,1)S(1)}, u32[]{:S(2)}, u32[]{:S(2)}) collective-permute-start(f16[16,1152]{1,0:T(8,128)(2,1)S(1)} %get-tuple-element.65), channel_id=1, source_target_pairs={{0,8},{1,17},{2,10},{3,19},{4,12},{5,21},{6,14},{7,23},{8,0},{9,25... | collective-permute-start | bytes 110600 | tf_op jit(solution)/shard_map/ppermute | solution.py:315
  67.4 4.9 %collective-permute-start.6 = (f16[16,1152]{1,0:T(8,128)(2,1)S(1)}, f16[16,1152]{1,0:T(8,128)(2,1)S(1)}, u32[]{:S(2)}, u32[]{:S(2)}) collective-permute-start(f16[16,1152]{1,0:T(8,128)(2,1)S(1)} %get-tuple-element.66), channel_id=1, source_target_pairs={{0,16},{1,9},{2,18},{3,11},{4,20},{5,13},{6,22},{7,15},{8,24},{9,1... | collective-permute-start | bytes 110600 | tf_op jit(solution)/shard_map/ppermute | solution.py:315
  68.3 5.8 %collective-permute-start.7 = (f16[16,1152]{1,0:T(8,128)(2,1)S(1)}, f16[16,1152]{1,0:T(8,128)(2,1)S(1)}, u32[]{:S(2)}, u32[]{:S(2)}) collective-permute-start(f16[16,1152]{1,0:T(8,128)(2,1)S(1)} %get-tuple-element.67), channel_id=1, source_target_pairs={{0,24},{1,25},{2,26},{3,27},{4,28},{5,29},{6,30},{7,31},{8,16},{9,... | collective-permute-start | bytes 110600 | tf_op jit(solution)/shard_map/ppermute | solution.py:315
  74.4 4.0 %collective-permute-start.10 = (f16[16,1024]{1,0:T(8,128)(2,1)S(1)}, f16[16,1024]{1,0:T(8,128)(2,1)S(1)}, u32[]{:S(2)}, u32[]{:S(2)}) collective-permute-start(f16[16,1024]{1,0:T(8,128)(2,1)S(1)} %fusion.25), channel_id=1, source_target_pairs={{0,8},{1,17},{2,10},{3,19},{4,12},{5,21},{6,14},{7,23},{8,0},{9,25... | collective-permute-start | bytes 98312 | tf_op jit(solution)/shard_map/ppermute | solution.py:315
  74.5 5.8 %collective-permute-start.8 = (f16[16,1024]{1,0:T(8,128)(2,1)S(1)}, f16[16,1024]{1,0:T(8,128)(2,1)S(1)}, u32[]{:S(2)}, u32[]{:S(2)}) collective-permute-start(f16[16,1024]{1,0:T(8,128)(2,1)S(1)} %fusion.25), channel_id=1, source_target_pairs={{0,24},{1,25},{2,26},{3,27},{4,28},{5,29},{6,30},{7,31},{8,16},{9,... | collective-permute-start | bytes 98312 | tf_op jit(solution)/shard_map/ppermute | solution.py:315
  77.5 4.8 %collective-permute-start.9 = (f16[16,1024]{1,0:T(8,128)(2,1)S(1)}, f16[16,1024]{1,0:T(8,128)(2,1)S(1)}, u32[]{:S(2)}, u32[]{:S(2)}) collective-permute-start(f16[16,1024]{1,0:T(8,128)(2,1)S(1)} %fusion.25), channel_id=1, source_target_pairs={{0,16},{1,9},{2,18},{3,11},{4,20},{5,13},{6,22},{7,15},{8,24},{9,1... | collective-permute-start | bytes 98312 | tf_op jit(solution)/shard_map/ppermute | solution.py:315
  82.4 6.0 %collective-permute-start.11 = (f16[64,1024]{1,0:T(8,128)(2,1)S(1)}, f16[64,1024]{1,0:T(8,128)(2,1)S(1)}, u32[]{:S(2)}, u32[]{:S(2)}) collective-permute-start(f16[64,1024]{1,0:T(8,128)(2,1)S(1)} %pad_maximum_fusion.1), channel_id=1, source_target_pairs={{0,6},{1,7},{2,4},{3,5},{4,2},{5,3},{6,0},{7,1},{8,14},{9,15},{10,... | collective-permute-start | bytes 393224 | tf_op jit(solution)/shard_map/ppermute | solution.py:315
  82.5 6.4 %collective-permute-start.12 = (f16[64,1024]{1,0:T(8,128)(2,1)S(1)}, f16[64,1024]{1,0:T(8,128)(2,1)S(1)}, u32[]{:S(2)}, u32[]{:S(2)}) collective-permute-start(f16[64,1024]{1,0:T(8,128)(2,1)S(1)} %pad_maximum_fusion.1), channel_id=1, source_target_pairs={{0,4},{1,3},{2,6},{3,1},{4,0},{5,7},{6,2},{7,5},{8,12},{9,11},{10,... | collective-permute-start | bytes 393224 | tf_op jit(solution)/shard_map/ppermute | solution.py:315
  83.4 5.8 %collective-permute-start.13 = (f16[64,1024]{1,0:T(8,128)(2,1)S(1)}, f16[64,1024]{1,0:T(8,128)(2,1)S(1)}, u32[]{:S(2)}, u32[]{:S(2)}) collective-permute-start(f16[64,1024]{1,0:T(8,128)(2,1)S(1)} %pad_maximum_fusion.1), channel_id=1, source_target_pairs={{0,2},{1,5},{2,0},{3,7},{4,6},{5,1},{6,4},{7,3},{8,10},{9,13},{10,... | collective-permute-start | bytes 393224 | tf_op jit(solution)/shard_map/ppermute | solution.py:315

commit v2 on v1

--- a/solution.py
+++ b/solution.py
@@ -56,8 +56,9 @@
 
 
 def align_kernel(
-    n_subjects, n_centres, group, side_ref, pos_ref, nb_ref, data_ref, tmpl_ref, low_ref, high_ref,
-    aligned_ref, first_ref, rest_ref, low_out, high_out, edge_out, hits_out, wide, acc, hits, sems,
+    n_subjects, n_centres, group, meta_ref, pos_ref, nb_ref, data_ref, tmpl_ref, low_ref, high_ref,
+    aligned_ref, first_ref, rest_ref, low_out, high_out, low_edge, high_edge, hits_out,
+    wide, acc, hits, sems,
 ):
     k = nb_ref.shape[1]
     span = 2 * k
@@ -79,11 +80,11 @@
     for copy in copies:
         copy.wait()
 
-    @pl.when(side_ref[0] == 0)
+    @pl.when(meta_ref[0] == 0)
     def _():
         wide[:, :, :k] = jnp.zeros((n_subjects + 1, frames, k), BF16)
 
-    @pl.when(side_ref[1] == 0)
+    @pl.when(meta_ref[1] == 0)
     def _():
         wide[:, :, k + own :] = jnp.zeros((n_subjects + 1, frames, k), BF16)
 
@@ -105,7 +106,7 @@
             first = pl.multiple_of((pos // k) * k, k)
             off = pos - first
             keep = lane >= off
-            want = (nb_ref[pl.ds(c, 1), :] + (k + off)) & (span - 1)
+            want = (nb_ref[pl.ds(c, 1), :] + off) & (span - 1)
             pick = jnp.where(spot == want, 1.0, 0.0).astype(BF16)
             members.append((first, keep, pick))
 
@@ -148,8 +149,8 @@
     for i in range(n_subjects):
         low_out[i, frames:, :] = hits[:, :k]
         high_out[i, frames:, :] = hits[:, own + k :]
-    edge_out[:, :, :k] = acc[:, :, k:span]
-    edge_out[:, :, k:] = acc[:, :, own : own + k]
+    low_edge[...] = acc[:, :, k:span]
+    high_edge[...] = acc[:, :, own : own + k]
     hits_out[:, :k] = hits[:, k:span]
     hits_out[:, k:] = hits[:, own : own + k]
     half = own // 2
@@ -182,7 +183,7 @@
     ref[:, width:] = jnp.broadcast_to(power, (ref.shape[0], LANES))
 
 
-def align(data, template, low, high, sides, local_pos, neighbours):
+def align(data, template, low, high, meta, centres, neighbours):
     n_subjects, frames, own = data.shape
     n_centres, k = neighbours.shape
     n_wide = own + 2 * k
@@ -198,40 +199,43 @@
             jax.ShapeDtypeStruct((frames, own // 2 - 2 * k), F32),
             jax.ShapeDtypeStruct((n_subjects, frames + ROWS, k), F32),
             jax.ShapeDtypeStruct((n_subjects, frames + ROWS, k), F32),
-            jax.ShapeDtypeStruct((n_subjects, frames, 2 * k), F32),
+            jax.ShapeDtypeStruct((n_subjects, frames, k), F32),
+            jax.ShapeDtypeStruct((n_subjects, frames, k), F32),
             jax.ShapeDtypeStruct((ROWS, 2 * k), F32),
         ),
         in_specs=[smem, smem, vmem, hbm, hbm, hbm, hbm],
-        out_specs=(vmem,) * 7,
+        out_specs=(vmem,) * 8,
         scratch_shapes=[
             pltpu.VMEM((n_subjects + 1, frames, n_wide), BF16),
             pltpu.VMEM((n_subjects, frames, n_wide), F32),
             pltpu.VMEM((ROWS, n_wide), F32),
             pltpu.SemaphoreType.DMA((n_subjects + 1, 3)),
         ],
-        compiler_params=pltpu.CompilerParams(vmem_limit_bytes=32 * 1024 * 1024),
+        compiler_params=pltpu.CompilerParams(vmem_limit_bytes=24 * 1024 * 1024),
+        cost_estimate=pl.CostEstimate(flops=16_000_000_000, bytes_accessed=8_000_000, transcendentals=0),
         name="align",
-    )(sides, local_pos, neighbours, data, template, low, high)
+    )(meta, centres, neighbours, data, template, low, high)
 
 
 def edges_kernel(
-    n_subjects, side_ref, edge_ref, hits_ref, low_ref, high_ref, rest_ref, before_ref,
+    n_subjects, meta_ref, low_edge, high_edge, hits_ref, low_ref, high_ref, rest_ref, before_ref,
     aligned_ref, out_ref, left, right, sems,
 ):
     k = low_ref.shape[2]
-    frames = edge_ref.shape[1]
+    frames = low_edge.shape[1]
     own = aligned_ref.shape[2]
     inner = rest_ref.shape[1]
     out_ref[:, :inner] = rest_ref[...]
     copies = []
-    for n, (got_ref, block) in enumerate(((low_ref, left), (high_ref, right))):
+    ends = ((low_ref, low_edge, left), (high_ref, high_edge, right))
+    for n, (got_ref, edge_ref, block) in enumerate(ends):
         lanes = slice(n * k, (n + 1) * k)
-        there = side_ref[n] > 0
+        there = meta_ref[n] > 0
         counts = hits_ref[:, lanes] + jnp.where(there, got_ref[0, frames:, :], 0.0)
         inverse = (1.0 / jnp.maximum(counts, 1.0))[:1]
         total = jnp.zeros((frames, k), F32)
         for i in range(n_subjects):
-            mapped = edge_ref[i, :, lanes] + jnp.where(there, got_ref[i, :frames, :], 0.0)
+            mapped = edge_ref[i] + jnp.where(there, got_ref[i, :frames, :], 0.0)
             mapped = mapped * inverse
             block[i] = mapped.astype(BF16)
             total = total + mapped
@@ -246,8 +250,8 @@
         copy.wait()
 
 
-def finish_edges(edges, edge_hits, from_low, from_high, sides, rest, aligned):
-    n_subjects, frames, _ = edges.shape
+def finish_edges(low_edge, high_edge, edge_hits, from_low, from_high, meta, rest, aligned):
+    n_subjects, frames, _ = low_edge.shape
     k = from_low.shape[2]
     vmem = pl.BlockSpec(memory_space=pltpu.VMEM)
     hbm = pl.BlockSpec(memory_space=pl.ANY)
@@ -258,25 +262,26 @@
             jax.ShapeDtypeStruct(aligned.shape, BF16),
             jax.ShapeDtypeStruct((frames, rest.shape[1] + 2 * k + LANES), F32),
         ),
-        in_specs=[smem, vmem, vmem, vmem, vmem, vmem, hbm],
+        in_specs=[smem, vmem, vmem, vmem, vmem, vmem, vmem, hbm],
         out_specs=(hbm, vmem),
-        input_output_aliases={6: 0},
+        input_output_aliases={7: 0},
         scratch_shapes=[
             pltpu.VMEM((n_subjects, frames, k), BF16),
             pltpu.VMEM((n_subjects, frames, k), BF16),
             pltpu.SemaphoreType.DMA((2,)),
         ],
-        compiler_params=pltpu.CompilerParams(vmem_limit_bytes=16 * 1024 * 1024),
+        compiler_params=pltpu.CompilerParams(vmem_limit_bytes=8 * 1024 * 1024),
+        cost_estimate=pl.CostEstimate(flops=1_000_000_000, bytes_accessed=2_000_000, transcendentals=0),
         name="edges",
-    )(sides, edges, edge_hits, from_low, from_high, rest, aligned)
+    )(meta, low_edge, high_edge, edge_hits, from_low, from_high, rest, aligned)
+
+
+def core_swap(value):
+    return lax.ppermute(value, "vert", [(0, 1), (1, 0)])
 
 
 def along_vert(up_value, down_value):
     size = lax.axis_size("vert")
-    if size == 2:
-        sent = jnp.where(lax.axis_index("vert") == 0, up_value, down_value)
-        got = lax.ppermute(sent, "vert", [(0, 1), (1, 0)])
-        return got, got
     up = [(i, i + 1) for i in range(size - 1)]
     down = [(i + 1, i) for i in range(size - 1)]
     return lax.ppermute(up_value, "vert", up), lax.ppermute(down_value, "vert", down)
@@ -328,7 +333,7 @@
             top = functools.reduce(jnp.maximum, powers)
             total = sum(part[:, :width] * jnp.exp2(p - top) for part, p in zip(parts, powers))
             block = jnp.concatenate([total, jnp.broadcast_to(top, (rows, LANES))], axis=1)
-        return block[:, :width], block[0, width]
+        return block[:, :width], block[:, width:]
 
     def gather(self, value):
         for phase in reversed(self.phases):
@@ -349,24 +354,41 @@
     k = neighbours.shape[1]
     n_subjects, frames, own = data.shape
     v = lax.axis_index("vert")
-    sides = jnp.stack([v > 0, v < lax.axis_size("vert") - 1]).astype(jnp.int32)
-    first_edge = jnp.concatenate([data[:, :, :k], template[None, :, :k]], axis=0)
-    last_edge = jnp.concatenate([data[:, :, own - k :], template[None, :, own - k :]], axis=0)
-    low, high = along_vert(last_edge, first_edge)
-    local_pos = centres - v * own
-    aligned, first, rest, low_out, high_out, edges, edge_hits = align(
-        data, template, low, high, sides, local_pos, neighbours
+    verts = lax.axis_size("vert")
+    meta = jnp.stack([v > 0, v < verts - 1]).astype(jnp.int32)
+    if verts == 2:
+        start = jnp.where(v == 0, own - k, 0)
+        facing = (
+            lax.dynamic_slice_in_dim(data, start, k, 2),
+            lax.dynamic_slice_in_dim(template, start, k, 1)[None],
+        )
+        low = high = core_swap(jnp.concatenate(facing, axis=0))
+    else:
+        first_edge = jnp.concatenate([data[:, :, :k], template[None, :, :k]], axis=0)
+        last_edge = jnp.concatenate([data[:, :, own - k :], template[None, :, own - k :]], axis=0)
+        low, high = along_vert(last_edge, first_edge)
+    aligned, first, rest, low_out, high_out, low_edge, high_edge, edge_hits = align(
+        data, template, low, high, meta, centres - v * own, neighbours + k
     )
-    from_low, from_high = along_vert(high_out, low_out)
-    aligned, rest = finish_edges(edges, edge_hits, from_low, from_high, sides, rest, aligned)
+    if verts == 2:
+        from_low = from_high = core_swap(jnp.where(v == 0, high_out, low_out))
+    else:
+        from_low, from_high = along_vert(high_out, low_out)
+    aligned, rest = finish_edges(
+        low_edge, high_edge, edge_hits, from_low, from_high, meta, rest, aligned
+    )
+    first, rest = lax.optimization_barrier((first, rest))
     cube = Hypercube()
     subjects = n_subjects * lax.axis_size("subj")
-    wholes = []
+    pieces = []
     for block in (first, rest):
         total, power = cube.reduce(block)
-        whole = cube.gather(total.astype(jnp.float16))
-        wholes.append(whole.astype(F32) * (jnp.exp2(power - HEADROOM) * (1.0 / subjects)))
-    begin, end = wholes
+        rows = power.shape[0]
+        whole = cube.gather(total.astype(jnp.float16)).astype(F32)
+        scale = jnp.exp2(power[:, :1] - HEADROOM) * (1.0 / subjects)
+        whole = whole.reshape(frames // rows, rows, -1) * scale[None]
+        pieces.append(whole.reshape(frames, -1))
+    begin, end = pieces
     inner = end.shape[1] - 2 * k
     new_template = jnp.concatenate(
         [end[:, inner : inner + k], begin, end[:, :inner], end[:, inner + k :]], axis=1

time: 91.6 us -> 74.6 us (0.81)
  waiting for transfers between devices: 25.3 us -> 9.21 us
  starting transfers between devices: 33.8 us -> 36.4 us
  local copies, waits for them, and re-layouts: 7.08 us -> 4.97 us
  between operations: 2.39 us -> 0.97 us
    ppermute x24, waiting for transfers between devices: 24.9 us -> 7.79 us  [swap(): return lax.ppermute(value, ('subj', 'vert'), self.pairs(phase, m))]
    ppermute x24, starting transfers between devices: 33.2 us -> 35.7 us  [swap(): return lax.ppermute(value, ('subj', 'vert'), self.pairs(phase, m))]
    slice x3 -> x0, local copies, waits for them, and re-layouts: 2.18 us -> none  [the longest x2 1.1 us: reduce(): return (block[:, :width], block[0, width])]
    ppermute x2, waiting for transfers between devices: 0.34 us -> 1.42 us  [core_swap(): return lax.ppermute(value, 'vert', [(0, 1), (1, 0)])]
    unnamed x14 -> x4, local copies, waits for them, and re-layouts: 3.79 us -> 2.82 us
    dynamic_slice x0 -> x1, local copies, waits for them, and re-layouts: none -> 0.92 us  [local(): lax.dynamic_slice_in_dim(data, start, k, 2)]
  transfers between devices with their start and end apart: 26 -> 26, of which waited for: 15 -> 9; matrix products, arithmetic and copies ran while one was open for 4% -> 5% of each run, Pallas kernels for 2% -> 0%
where the time goes in v2:
time: 74.6 us; the launch traced here: 74.3 us
  starting transfers between devices  36.4 us (49%)
  Pallas kernels  17.1 us (23%)
  waiting for transfers between devices  9.21 us (12%)
  other arithmetic  5.68 us (8%)
  local copies, waits for them, and re-layouts  4.97 us (7%)
  between operations  0.97 us (1%)
    ppermute x24, starting transfers between devices, swap(): return lax.ppermute(value, ('subj', 'vert'), self.pairs(phase, m))  35.7 us
    pallas_call x1, Pallas kernels, align(): pl.pallas_call(functools.partial(align_kernel, n_subjects, n_centres, gro...  15.7 us
    ppermute x24, waiting for transfers between devices, swap(): return lax.ppermute(value, ('subj', 'vert'), self.pairs(phase, m))  7.79 us
    unnamed x4, local copies, waits for them, and re-layouts  2.82 us
    concatenate x1, other arithmetic, local(): jnp.concatenate([end[:, inner:inner + k], begin, end[:, :inner], end[:, i...  1.5 us
  transfers between devices with their start and end apart: 26, of which 9 were waited for; matrix products, arithmetic and copies ran while one was open for 5% of the time, Pallas kernels for 0%

profile of v2, /device:TPU:0, one launch (start us, length us, event | category | flops | bytes accessed | tf_op | source)
XLA Modules:
  0.0 74.3 jit_solution(452206349604896810)
XLA Ops:
  0.6 0.9 %constant_dynamic-slice_fusion = bf16[2,256,128]{2,1,0:T(8,128)(2,1)S(1)} fusion(bf16[2,256,2048]{2,1,0:T(8,128)(2,1)} %data_ref.1, s32[]{:T(128)S(6)} %select_n.323), kind=kLoop, calls=%fused_computation.112 | loop fusion | bytes 262148 | tf_op jit(solution)/shard_map/dynamic_slice | solution.py:362
  1.6 0.9 %dynamic-slice_bitcast_fusion = bf16[1,256,128]{2,1,0:T(8,128)(2,1)S(1)} fusion(bf16[256,2048]{1,0:T(8,128)(2,1)} %tmpl_ref.1, s32[]{:T(128)S(6)} %select_n.323), kind=kLoop, calls=%fused_computation.81 | loop fusion | bytes 131076 | tf_op jit(solution)/shard_map/broadcast_in_dim | solution.py:363
  2.4 0.5 collective-permute-start
  3.0 0.7 broadcast_add_fusion.nb_ref
  3.7 0.1 add_convert_fusion.meta_ref
  3.7 0.7 broadcast_subtract_fusion.pos_ref
  4.4 1.6 %copy-done = bf16[2,256,2048]{2,1,0:T(8,128)(2,1)S(1)} copy-done((bf16[2,256,2048]{2,1,0:T(8,128)(2,1)S(1)}, bf16[2,256,2048]{2,1,0:T(8,128)(2,1)}, u32[]{:S(2)}) %copy-start) | copy-done | bytes 2097176
  6.0 1.2 %copy-done.1 = bf16[256,2048]{1,0:T(8,128)(2,1)S(1)} copy-done((bf16[256,2048]{1,0:T(8,128)(2,1)S(1)}, bf16[256,2048]{1,0:T(8,128)(2,1)}, u32[]{:S(2)}) %copy-start.1) | copy-done | bytes 1048600
  7.2 15.7 %align.1 = (bf16[2,256,2048]{2,1,0:T(8,128)(2,1)}, f32[256,1152]{1,0:T(8,128)S(1)}, f32[256,768]{1,0:T(8,128)S(1)}, f32[2,264,128]{2,1,0:T(8,128)S(1)}, f32[2,26...) custom-call(s32[2]{0:T(128)S(1)} %add_convert_fusion.meta_ref, ...), custom_call_target="tpu_custom_call" | custom-call | flops 16000000000 | bytes 8000000 | tf_op jit(solution)/shard_map/align/pallas_call | solution.py:194
  23.0 0.1 collective-permute-start.1
  23.2 1.4 %collective-permute-done.1.low_ref.high_ref = f32[2,264,128]{2,1,0:T(8,128)S(1)} collective-permute-done((f32[2,264,128]{2,1,0:T(8,128)S(1)}, f32[2,264,128]{2,1,0:T(8,128)S(1)}, u32[]{:S(2)}, u32[]{:S(2)}) %collective-permute-start.1) | collective-permute-done | bytes 270368 | tf_op jit(solution)/shard_map/ppermute | solution.py:280
  24.6 1.4 %edges.1 = (bf16[2,256,2048]{2,1,0:T(8,128)(2,1)}, f32[256,1152]{1,0:T(8,128)S(1)}) custom-call(s32[2]{0:T(128)S(1)} %add_convert_fusion.meta_ref, f32[2,256,128]{2,1,0:T(8,128)S(1)} %get-tuple-element.14.low_edge, f32[2,256,128]{2,1,0:T(8,128)S(1)} %get-tuple-element.15.high_edge, ...), custom_call_target="tpu_custom_call", output_to_operand_aliasing={{0}: (7, {})} | custom-call | flops 1000000000 | bytes 2000000 | tf_op jit(solution)/shard_map/edges/pallas_call | solution.py:259
  26.0 0.1 dynamic-slice_convert_fusion.5
  26.0 2.7 %collective-permute-start.2 = (f16[64,1152]{1,0:T(8,128)(2,1)S(1)}, f16[64,1152]{1,0:T(8,128)(2,1)S(1)}, u32[]{:S(2)}, u32[]{:S(2)}) collective-permute-start(f16[64,1152]{1,0:T(8,128)(2,1)S(1)} %get-tuple-element.49), channel_id=1, source_target_pairs={{0,2},{1,5},{2,0},{3,7},{4,6},{5,1},{6,4},{7,3},{8,10},{9,13},{10,... | collective-permute-start | bytes 442376 | tf_op jit(solution)/shard_map/ppermute | solution.py:320
  28.7 1.5 %collective-permute-start.3 = (f16[64,1152]{1,0:T(8,128)(2,1)S(1)}, f16[64,1152]{1,0:T(8,128)(2,1)S(1)}, u32[]{:S(2)}, u32[]{:S(2)}) collective-permute-start(f16[64,1152]{1,0:T(8,128)(2,1)S(1)} %get-tuple-element.51), channel_id=1, source_target_pairs={{0,4},{1,3},{2,6},{3,1},{4,0},{5,7},{6,2},{7,5},{8,12},{9,11},{10,... | collective-permute-start | bytes 442376 | tf_op jit(solution)/shard_map/ppermute | solution.py:320
  30.3 2.0 %collective-permute-start.14 = (f16[64,1152]{1,0:T(8,128)(2,1)S(1)}, f16[64,1152]{1,0:T(8,128)(2,1)S(1)}, u32[]{:S(2)}, u32[]{:S(2)}) collective-permute-start(f16[64,1152]{1,0:T(8,128)(2,1)S(1)} %get-tuple-element.46), channel_id=1, source_target_pairs={{0,2},{1,5},{2,0},{3,7},{4,6},{5,1},{6,4},{7,3},{8,10},{9,13},{10,... | collective-permute-start | bytes 442376 | tf_op jit(solution)/shard_map/ppermute | solution.py:320
  32.4 1.5 %collective-permute-start.15 = (f16[64,1152]{1,0:T(8,128)(2,1)S(1)}, f16[64,1152]{1,0:T(8,128)(2,1)S(1)}, u32[]{:S(2)}, u32[]{:S(2)}) collective-permute-start(f16[64,1152]{1,0:T(8,128)(2,1)S(1)} %get-tuple-element.48), channel_id=1, source_target_pairs={{0,4},{1,3},{2,6},{3,1},{4,0},{5,7},{6,2},{7,5},{8,12},{9,11},{10,... | collective-permute-start | bytes 442376 | tf_op jit(solution)/shard_map/ppermute | solution.py:320
  33.9 2.5 %collective-permute-start.16 = (f16[64,1152]{1,0:T(8,128)(2,1)S(1)}, f16[64,1152]{1,0:T(8,128)(2,1)S(1)}, u32[]{:S(2)}, u32[]{:S(2)}) collective-permute-start(f16[64,1152]{1,0:T(8,128)(2,1)S(1)} %get-tuple-element.47), channel_id=1, source_target_pairs={{0,6},{1,7},{2,4},{3,5},{4,2},{5,3},{6,0},{7,1},{8,14},{9,15},{10,... | collective-permute-start | bytes 442376 | tf_op jit(solution)/shard_map/ppermute | solution.py:320
  36.4 1.8 %collective-permute-done.3 = f16[64,1152]{1,0:T(8,128)(2,1)S(1)} collective-permute-done((f16[64,1152]{1,0:T(8,128)(2,1)S(1)}, f16[64,1152]{1,0:T(8,128)(2,1)S(1)}, u32[]{:S(2)}, u32[]{:S(2)}) %collective-permute-start.3) | collective-permute-done | bytes 147488 | tf_op jit(solution)/shard_map/ppermute | solution.py:320
  38.2 0.2 fusion.29
  38.4 0.1 fusion.3
  38.6 0.1 broadcast_in_dim.12
  38.7 2.5 %collective-permute-start.6 = (f16[16,1152]{1,0:T(8,128)(2,1)S(1)}, f16[16,1152]{1,0:T(8,128)(2,1)S(1)}, u32[]{:S(2)}, u32[]{:S(2)}) collective-permute-start(f16[16,1152]{1,0:T(8,128)(2,1)S(1)} %get-tuple-element.68), channel_id=1, source_target_pairs={{0,16},{1,9},{2,18},{3,11},{4,20},{5,13},{6,22},{7,15},{8,24},{9,1... | collective-permute-start | bytes 110600 | tf_op jit(solution)/shard_map/ppermute | solution.py:320
  41.2 1.3 %collective-permute-start.7 = (f16[16,1152]{1,0:T(8,128)(2,1)S(1)}, f16[16,1152]{1,0:T(8,128)(2,1)S(1)}, u32[]{:S(2)}, u32[]{:S(2)}) collective-permute-start(f16[16,1152]{1,0:T(8,128)(2,1)S(1)} %get-tuple-element.69), channel_id=1, source_target_pairs={{0,24},{1,25},{2,26},{3,27},{4,28},{5,29},{6,30},{7,31},{8,16},{9,... | collective-permute-start | bytes 110600 | tf_op jit(solution)/shard_map/ppermute | solution.py:320
  42.5 0.2 collective-permute-start.5
  42.8 1.1 %collective-permute-done.16 = f16[64,1152]{1,0:T(8,128)(2,1)S(1)} collective-permute-done((f16[64,1152]{1,0:T(8,128)(2,1)S(1)}, f16[64,1152]{1,0:T(8,128)(2,1)S(1)}, u32[]{:S(2)}, u32[]{:S(2)}) %collective-permute-start.16) | collective-permute-done | bytes 147488 | tf_op jit(solution)/shard_map/ppermute | solution.py:320
  44.0 0.2 fusion.28
  44.2 0.2 fusion
  44.3 0.1 broadcast_in_dim.14
  44.4 1.8 %collective-permute-start.17 = (f16[16,1152]{1,0:T(8,128)(2,1)S(1)}, f16[16,1152]{1,0:T(8,128)(2,1)S(1)}, u32[]{:S(2)}, u32[]{:S(2)}) collective-permute-start(f16[16,1152]{1,0:T(8,128)(2,1)S(1)} %get-tuple-element.63), channel_id=1, source_target_pairs={{0,8},{1,17},{2,10},{3,19},{4,12},{5,21},{6,14},{7,23},{8,0},{9,25... | collective-permute-start | bytes 110600 | tf_op jit(solution)/shard_map/ppermute | solution.py:320
  46.2 2.6 %collective-permute-start.18 = (f16[16,1152]{1,0:T(8,128)(2,1)S(1)}, f16[16,1152]{1,0:T(8,128)(2,1)S(1)}, u32[]{:S(2)}, u32[]{:S(2)}) collective-permute-start(f16[16,1152]{1,0:T(8,128)(2,1)S(1)} %get-tuple-element.64), channel_id=1, source_target_pairs={{0,16},{1,9},{2,18},{3,11},{4,20},{5,13},{6,22},{7,15},{8,24},{9,1... | collective-permute-start | bytes 110600 | tf_op jit(solution)/shard_map/ppermute | solution.py:320
  48.8 0.1 collective-permute-start.19
  48.9 0.2 multiply_reduce_fusion.1
  49.1 0.1 fusion.25
  49.2 0.9 %collective-permute-start.10 = (f16[16,1024]{1,0:T(8,128)(2,1)S(1)}, f16[16,1024]{1,0:T(8,128)(2,1)S(1)}, u32[]{:S(2)}, u32[]{:S(2)}) collective-permute-start(f16[16,1024]{1,0:T(8,128)(2,1)S(1)} %fusion.25), channel_id=1, source_target_pairs={{0,8},{1,17},{2,10},{3,19},{4,12},{5,21},{6,14},{7,23},{8,0},{9,25... | collective-permute-start | bytes 98312 | tf_op jit(solution)/shard_map/ppermute | solution.py:320
  50.1 3.0 %collective-permute-start.8 = (f16[16,1024]{1,0:T(8,128)(2,1)S(1)}, f16[16,1024]{1,0:T(8,128)(2,1)S(1)}, u32[]{:S(2)}, u32[]{:S(2)}) collective-permute-start(f16[16,1024]{1,0:T(8,128)(2,1)S(1)} %fusion.25), channel_id=1, source_target_pairs={{0,24},{1,25},{2,26},{3,27},{4,28},{5,29},{6,30},{7,31},{8,16},{9,... | collective-permute-start | bytes 98312 | tf_op jit(solution)/shard_map/ppermute | solution.py:320
  53.1 0.5 collective-permute-start.9
  53.6 1.3 %collective-permute-done.19 = f16[16,1152]{1,0:T(8,128)(2,1)S(1)} collective-permute-done((f16[16,1152]{1,0:T(8,128)(2,1)S(1)}, f16[16,1152]{1,0:T(8,128)(2,1)S(1)}, u32[]{:S(2)}, u32[]{:S(2)}) %collective-permute-start.19) | collective-permute-done | bytes 36896 | tf_op jit(solution)/shard_map/ppermute | solution.py:320
  54.9 0.2 multiply_reduce_fusion
  55.1 0.1 fusion.21
  55.2 1.7 %collective-permute-start.20 = (f16[16,1024]{1,0:T(8,128)(2,1)S(1)}, f16[16,1024]{1,0:T(8,128)(2,1)S(1)}, u32[]{:S(2)}, u32[]{:S(2)}) collective-permute-start(f16[16,1024]{1,0:T(8,128)(2,1)S(1)} %fusion.21), channel_id=1, source_target_pairs={{0,24},{1,25},{2,26},{3,27},{4,28},{5,29},{6,30},{7,31},{8,16},{9,... | collective-permute-start | bytes 98312 | tf_op jit(solution)/shard_map/ppermute | solution.py:320
  57.0 0.1 mul.311
  57.1 0.1 mul.281
  57.1 2.8 %collective-permute-start.22 = (f16[16,1024]{1,0:T(8,128)(2,1)S(1)}, f16[16,1024]{1,0:T(8,128)(2,1)S(1)}, u32[]{:S(2)}, u32[]{:S(2)}) collective-permute-start(f16[16,1024]{1,0:T(8,128)(2,1)S(1)} %fusion.21), channel_id=1, source_target_pairs={{0,8},{1,17},{2,10},{3,19},{4,12},{5,21},{6,14},{7,23},{8,0},{9,25... | collective-permute-start | bytes 98312 | tf_op jit(solution)/shard_map/ppermute | solution.py:320
  59.9 0.1 select_select_fusion.15
  60.0 0.9 %collective-permute-start.11 = (f16[64,1024]{1,0:T(8,128)(2,1)S(1)}, f16[64,1024]{1,0:T(8,128)(2,1)S(1)}, u32[]{:S(2)}, u32[]{:S(2)}) collective-permute-start(f16[64,1024]{1,0:T(8,128)(2,1)S(1)} %pad_maximum_fusion.2), channel_id=1, source_target_pairs={{0,6},{1,7},{2,4},{3,5},{4,2},{5,3},{6,0},{7,1},{8,14},{9,15},{10,... | collective-permute-start | bytes 393224 | tf_op jit(solution)/shard_map/ppermute | solution.py:320
  61.0 2.1 %collective-permute-start.12 = (f16[64,1024]{1,0:T(8,128)(2,1)S(1)}, f16[64,1024]{1,0:T(8,128)(2,1)S(1)}, u32[]{:S(2)}, u32[]{:S(2)}) collective-permute-start(f16[64,1024]{1,0:T(8,128)(2,1)S(1)} %pad_maximum_fusion.2), channel_id=1, source_target_pairs={{0,4},{1,3},{2,6},{3,1},{4,0},{5,7},{6,2},{7,5},{8,12},{9,11},{10,... | collective-permute-start | bytes 393224 | tf_op jit(solution)/shard_map/ppermute | solution.py:320
  63.1 0.5 collective-permute-start.13
  63.6 0.1 select_select_fusion.11
  63.7 1.0 %collective-permute-start.23 = (f16[64,1024]{1,0:T(8,128)(2,1)S(1)}, f16[64,1024]{1,0:T(8,128)(2,1)S(1)}, u32[]{:S(2)}, u32[]{:S(2)}) collective-permute-start(f16[64,1024]{1,0:T(8,128)(2,1)S(1)} %pad_maximum_fusion.3), channel_id=1, source_target_pairs={{0,6},{1,7},{2,4},{3,5},{4,2},{5,3},{6,0},{7,1},{8,14},{9,15},{10,... | collective-permute-start | bytes 393224 | tf_op jit(solution)/shard_map/ppermute | solution.py:320
  64.7 2.0 %collective-permute-start.24 = (f16[64,1024]{1,0:T(8,128)(2,1)S(1)}, f16[64,1024]{1,0:T(8,128)(2,1)S(1)}, u32[]{:S(2)}, u32[]{:S(2)}) collective-permute-start(f16[64,1024]{1,0:T(8,128)(2,1)S(1)} %pad_maximum_fusion.3), channel_id=1, source_target_pairs={{0,4},{1,3},{2,6},{3,1},{4,0},{5,7},{6,2},{7,5},{8,12},{9,11},{10,... | collective-permute-start | bytes 393224 | tf_op jit(solution)/shard_map/ppermute | solution.py:320
  66.8 0.6 collective-permute-done.11
  67.4 1.5 %collective-permute-start.25 = (f16[64,1024]{1,0:T(8,128)(2,1)S(1)}, f16[64,1024]{1,0:T(8,128)(2,1)S(1)}, u32[]{:S(2)}, u32[]{:S(2)}) collective-permute-start(f16[64,1024]{1,0:T(8,128)(2,1)S(1)} %pad_maximum_fusion.3), channel_id=1, source_target_pairs={{0,2},{1,5},{2,0},{3,7},{4,6},{5,1},{6,4},{7,3},{8,10},{9,13},{10,... | collective-permute-start | bytes 393224 | tf_op jit(solution)/shard_map/ppermute | solution.py:320
  68.9 0.2 collective-permute-done.12
  69.1 0.1 select_select_fusion.6
  69.2 0.1 select_select_fusion.7
  69.4 0.2 convert_multiply_fusion.1
  69.6 1.0 %collective-permute-done.23 = f16[64,1024]{1,0:T(8,128)(2,1)S(1)} collective-permute-done((f16[64,1024]{1,0:T(8,128)(2,1)S(1)}, f16[64,1024]{1,0:T(8,128)(2,1)S(1)}, u32[]{:S(2)}, u32[]{:S(2)}) %collective-permute-start.23) | collective-permute-done | bytes 131104 | tf_op jit(solution)/shard_map/ppermute | solution.py:320
  70.6 1.3 %collective-permute-done.24 = f16[64,1024]{1,0:T(8,128)(2,1)S(1)} collective-permute-done((f16[64,1024]{1,0:T(8,128)(2,1)S(1)}, f16[64,1024]{1,0:T(8,128)(2,1)S(1)}, u32[]{:S(2)}, u32[]{:S(2)}) %collective-permute-start.24) | collective-permute-done | bytes 131104 | tf_op jit(solution)/shard_map/ppermute | solution.py:320
  71.9 0.5 collective-permute-done.25
  72.4 0.1 select_select_fusion.2
  72.5 0.1 select_select_fusion.3
  72.6 0.2 convert_multiply_fusion
  72.8 1.5 %pad_maximum_fusion = f32[256,2048]{1,0:T(8,128)} fusion(f32[256,128]{1,0:T(8,128)S(1)} %get-tuple-element.53, f32[256,768]{1,0:T(8,128)S(1)} %slice.171, f32[256,1024]{1,0:T(8,128)S(1)} %convert_multiply_fusion, f32[256,128]{1,0:T(8,128)S(1)} %get-tuple-element.52), kind=kLoop, calls=%fused_computation | loop fusion | flops 1572864 | bytes 4194304 | tf_op jit(solution)/shard_map/concatenate | solution.py:393
  (44 shorter events, 0.6 us)
Async XLA Ops:
  2.4 2.0 %collective-permute-start = (bf16[3,256,128]{2,1,0:T(8,128)(2,1)S(1)}, bf16[3,256,128]{2,1,0:T(8,128)(2,1)S(1)}, u32[]{:S(2)}, u32[]{:S(2)}) collective-permute-start(bf16[3,256,128]{2,1,0:T(8,128)(2,1)S(1)} %pad_maximum_fusion.1), channel_id=1, source_target_pairs={{0,1},{1,0},{2,3},{3,2},{4,5},{5,4},{6,7},{7,6},{8,9},{9,8},{10,11... | collective-permute-start | bytes 589832 | tf_op jit(solution)/shard_map/ppermute | solution.py:280
  4.4 1.6 %copy-start = (bf16[2,256,2048]{2,1,0:T(8,128)(2,1)S(1)}, bf16[2,256,2048]{2,1,0:T(8,128)(2,1)}, u32[]{:S(2)}) copy-start(bf16[2,256,2048]{2,1,0:T(8,128)(2,1)} %data_ref.1) | copy-start | bytes 6291460
  6.0 1.2 %copy-start.1 = (bf16[256,2048]{1,0:T(8,128)(2,1)S(1)}, bf16[256,2048]{1,0:T(8,128)(2,1)}, u32[]{:S(2)}) copy-start(bf16[256,2048]{1,0:T(8,128)(2,1)} %tmpl_ref.1) | copy-start | bytes 3145732
  23.0 1.6 %collective-permute-start.1 = (f32[2,264,128]{2,1,0:T(8,128)S(1)}, f32[2,264,128]{2,1,0:T(8,128)S(1)}, u32[]{:S(2)}, u32[]{:S(2)}) collective-permute-start(f32[2,264,128]{2,1,0:T(8,128)S(1)} %broadcast_select_fusion), channel_id=1, source_target_pairs={{0,1},{1,0},{2,3},{3,2},{4,5},{5,4},{6,7},{7,6},{8,9},{9,8},{10,11... | collective-permute-start | bytes 811016 | tf_op jit(solution)/shard_map/ppermute | solution.py:280
  26.0 7.8 %collective-permute-start.2 = (f16[64,1152]{1,0:T(8,128)(2,1)S(1)}, f16[64,1152]{1,0:T(8,128)(2,1)S(1)}, u32[]{:S(2)}, u32[]{:S(2)}) collective-permute-start(f16[64,1152]{1,0:T(8,128)(2,1)S(1)} %get-tuple-element.49), channel_id=1, source_target_pairs={{0,2},{1,5},{2,0},{3,7},{4,6},{5,1},{6,4},{7,3},{8,10},{9,13},{10,... | collective-permute-start | bytes 442376 | tf_op jit(solution)/shard_map/ppermute | solution.py:320
  28.7 9.4 %collective-permute-start.3 = (f16[64,1152]{1,0:T(8,128)(2,1)S(1)}, f16[64,1152]{1,0:T(8,128)(2,1)S(1)}, u32[]{:S(2)}, u32[]{:S(2)}) collective-permute-start(f16[64,1152]{1,0:T(8,128)(2,1)S(1)} %get-tuple-element.51), channel_id=1, source_target_pairs={{0,4},{1,3},{2,6},{3,1},{4,0},{5,7},{6,2},{7,5},{8,12},{9,11},{10,... | collective-permute-start | bytes 442376 | tf_op jit(solution)/shard_map/ppermute | solution.py:320
  30.3 7.9 %collective-permute-start.4 = (f16[64,1152]{1,0:T(8,128)(2,1)S(1)}, f16[64,1152]{1,0:T(8,128)(2,1)S(1)}, u32[]{:S(2)}, u32[]{:S(2)}) collective-permute-start(f16[64,1152]{1,0:T(8,128)(2,1)S(1)} %get-tuple-element.50), channel_id=1, source_target_pairs={{0,6},{1,7},{2,4},{3,5},{4,2},{5,3},{6,0},{7,1},{8,14},{9,15},{10,... | collective-permute-start | bytes 442376 | tf_op jit(solution)/shard_map/ppermute | solution.py:320
  30.3 12.2 %collective-permute-start.14 = (f16[64,1152]{1,0:T(8,128)(2,1)S(1)}, f16[64,1152]{1,0:T(8,128)(2,1)S(1)}, u32[]{:S(2)}, u32[]{:S(2)}) collective-permute-start(f16[64,1152]{1,0:T(8,128)(2,1)S(1)} %get-tuple-element.46), channel_id=1, source_target_pairs={{0,2},{1,5},{2,0},{3,7},{4,6},{5,1},{6,4},{7,3},{8,10},{9,13},{10,... | collective-permute-start | bytes 442376 | tf_op jit(solution)/shard_map/ppermute | solution.py:320
  32.4 10.4 %collective-permute-start.15 = (f16[64,1152]{1,0:T(8,128)(2,1)S(1)}, f16[64,1152]{1,0:T(8,128)(2,1)S(1)}, u32[]{:S(2)}, u32[]{:S(2)}) collective-permute-start(f16[64,1152]{1,0:T(8,128)(2,1)S(1)} %get-tuple-element.48), channel_id=1, source_target_pairs={{0,4},{1,3},{2,6},{3,1},{4,0},{5,7},{6,2},{7,5},{8,12},{9,11},{10,... | collective-permute-start | bytes 442376 | tf_op jit(solution)/shard_map/ppermute | solution.py:320
  33.9 10.1 %collective-permute-start.16 = (f16[64,1152]{1,0:T(8,128)(2,1)S(1)}, f16[64,1152]{1,0:T(8,128)(2,1)S(1)}, u32[]{:S(2)}, u32[]{:S(2)}) collective-permute-start(f16[64,1152]{1,0:T(8,128)(2,1)S(1)} %get-tuple-element.47), channel_id=1, source_target_pairs={{0,6},{1,7},{2,4},{3,5},{4,2},{5,3},{6,0},{7,1},{8,14},{9,15},{10,... | collective-permute-start | bytes 442376 | tf_op jit(solution)/shard_map/ppermute | solution.py:320
  38.7 10.1 %collective-permute-start.6 = (f16[16,1152]{1,0:T(8,128)(2,1)S(1)}, f16[16,1152]{1,0:T(8,128)(2,1)S(1)}, u32[]{:S(2)}, u32[]{:S(2)}) collective-permute-start(f16[16,1152]{1,0:T(8,128)(2,1)S(1)} %get-tuple-element.68), channel_id=1, source_target_pairs={{0,16},{1,9},{2,18},{3,11},{4,20},{5,13},{6,22},{7,15},{8,24},{9,1... | collective-permute-start | bytes 110600 | tf_op jit(solution)/shard_map/ppermute | solution.py:320
  41.2 7.7 %collective-permute-start.7 = (f16[16,1152]{1,0:T(8,128)(2,1)S(1)}, f16[16,1152]{1,0:T(8,128)(2,1)S(1)}, u32[]{:S(2)}, u32[]{:S(2)}) collective-permute-start(f16[16,1152]{1,0:T(8,128)(2,1)S(1)} %get-tuple-element.69), channel_id=1, source_target_pairs={{0,24},{1,25},{2,26},{3,27},{4,28},{5,29},{6,30},{7,31},{8,16},{9,... | collective-permute-start | bytes 110600 | tf_op jit(solution)/shard_map/ppermute | solution.py:320
  42.5 6.4 %collective-permute-start.5 = (f16[16,1152]{1,0:T(8,128)(2,1)S(1)}, f16[16,1152]{1,0:T(8,128)(2,1)S(1)}, u32[]{:S(2)}, u32[]{:S(2)}) collective-permute-start(f16[16,1152]{1,0:T(8,128)(2,1)S(1)} %get-tuple-element.67), channel_id=1, source_target_pairs={{0,8},{1,17},{2,10},{3,19},{4,12},{5,21},{6,14},{7,23},{8,0},{9,25... | collective-permute-start | bytes 110600 | tf_op jit(solution)/shard_map/ppermute | solution.py:320
  44.4 8.7 %collective-permute-start.17 = (f16[16,1152]{1,0:T(8,128)(2,1)S(1)}, f16[16,1152]{1,0:T(8,128)(2,1)S(1)}, u32[]{:S(2)}, u32[]{:S(2)}) collective-permute-start(f16[16,1152]{1,0:T(8,128)(2,1)S(1)} %get-tuple-element.63), channel_id=1, source_target_pairs={{0,8},{1,17},{2,10},{3,19},{4,12},{5,21},{6,14},{7,23},{8,0},{9,25... | collective-permute-start | bytes 110600 | tf_op jit(solution)/shard_map/ppermute | solution.py:320
  46.2 7.4 %collective-permute-start.18 = (f16[16,1152]{1,0:T(8,128)(2,1)S(1)}, f16[16,1152]{1,0:T(8,128)(2,1)S(1)}, u32[]{:S(2)}, u32[]{:S(2)}) collective-permute-start(f16[16,1152]{1,0:T(8,128)(2,1)S(1)} %get-tuple-element.64), channel_id=1, source_target_pairs={{0,16},{1,9},{2,18},{3,11},{4,20},{5,13},{6,22},{7,15},{8,24},{9,1... | collective-permute-start | bytes 110600 | tf_op jit(solution)/shard_map/ppermute | solution.py:320
  48.8 6.1 %collective-permute-start.19 = (f16[16,1152]{1,0:T(8,128)(2,1)S(1)}, f16[16,1152]{1,0:T(8,128)(2,1)S(1)}, u32[]{:S(2)}, u32[]{:S(2)}) collective-permute-start(f16[16,1152]{1,0:T(8,128)(2,1)S(1)} %get-tuple-element.65), channel_id=1, source_target_pairs={{0,24},{1,25},{2,26},{3,27},{4,28},{5,29},{6,30},{7,31},{8,16},{9,... | collective-permute-start | bytes 110600 | tf_op jit(solution)/shard_map/ppermute | solution.py:320
  49.2 7.9 %collective-permute-start.10 = (f16[16,1024]{1,0:T(8,128)(2,1)S(1)}, f16[16,1024]{1,0:T(8,128)(2,1)S(1)}, u32[]{:S(2)}, u32[]{:S(2)}) collective-permute-start(f16[16,1024]{1,0:T(8,128)(2,1)S(1)} %fusion.25), channel_id=1, source_target_pairs={{0,8},{1,17},{2,10},{3,19},{4,12},{5,21},{6,14},{7,23},{8,0},{9,25... | collective-permute-start | bytes 98312 | tf_op jit(solution)/shard_map/ppermute | solution.py:320
  50.1 9.8 %collective-permute-start.8 = (f16[16,1024]{1,0:T(8,128)(2,1)S(1)}, f16[16,1024]{1,0:T(8,128)(2,1)S(1)}, u32[]{:S(2)}, u32[]{:S(2)}) collective-permute-start(f16[16,1024]{1,0:T(8,128)(2,1)S(1)} %fusion.25), channel_id=1, source_target_pairs={{0,24},{1,25},{2,26},{3,27},{4,28},{5,29},{6,30},{7,31},{8,16},{9,... | collective-permute-start | bytes 98312 | tf_op jit(solution)/shard_map/ppermute | solution.py:320
  53.1 6.8 %collective-permute-start.9 = (f16[16,1024]{1,0:T(8,128)(2,1)S(1)}, f16[16,1024]{1,0:T(8,128)(2,1)S(1)}, u32[]{:S(2)}, u32[]{:S(2)}) collective-permute-start(f16[16,1024]{1,0:T(8,128)(2,1)S(1)} %fusion.25), channel_id=1, source_target_pairs={{0,16},{1,9},{2,18},{3,11},{4,20},{5,13},{6,22},{7,15},{8,24},{9,1... | collective-permute-start | bytes 98312 | tf_op jit(solution)/shard_map/ppermute | solution.py:320
  55.2 7.8 %collective-permute-start.20 = (f16[16,1024]{1,0:T(8,128)(2,1)S(1)}, f16[16,1024]{1,0:T(8,128)(2,1)S(1)}, u32[]{:S(2)}, u32[]{:S(2)}) collective-permute-start(f16[16,1024]{1,0:T(8,128)(2,1)S(1)} %fusion.21), channel_id=1, source_target_pairs={{0,24},{1,25},{2,26},{3,27},{4,28},{5,29},{6,30},{7,31},{8,16},{9,... | collective-permute-start | bytes 98312 | tf_op jit(solution)/shard_map/ppermute | solution.py:320
  57.0 6.6 %collective-permute-start.21 = (f16[16,1024]{1,0:T(8,128)(2,1)S(1)}, f16[16,1024]{1,0:T(8,128)(2,1)S(1)}, u32[]{:S(2)}, u32[]{:S(2)}) collective-permute-start(f16[16,1024]{1,0:T(8,128)(2,1)S(1)} %fusion.21), channel_id=1, source_target_pairs={{0,16},{1,9},{2,18},{3,11},{4,20},{5,13},{6,22},{7,15},{8,24},{9,1... | collective-permute-start | bytes 98312 | tf_op jit(solution)/shard_map/ppermute | solution.py:320
  57.1 6.5 %collective-permute-start.22 = (f16[16,1024]{1,0:T(8,128)(2,1)S(1)}, f16[16,1024]{1,0:T(8,128)(2,1)S(1)}, u32[]{:S(2)}, u32[]{:S(2)}) collective-permute-start(f16[16,1024]{1,0:T(8,128)(2,1)S(1)} %fusion.21), channel_id=1, source_target_pairs={{0,8},{1,17},{2,10},{3,19},{4,12},{5,21},{6,14},{7,23},{8,0},{9,25... | collective-permute-start | bytes 98312 | tf_op jit(solution)/shard_map/ppermute | solution.py:320
  60.0 7.3 %collective-permute-start.11 = (f16[64,1024]{1,0:T(8,128)(2,1)S(1)}, f16[64,1024]{1,0:T(8,128)(2,1)S(1)}, u32[]{:S(2)}, u32[]{:S(2)}) collective-permute-start(f16[64,1024]{1,0:T(8,128)(2,1)S(1)} %pad_maximum_fusion.2), channel_id=1, source_target_pairs={{0,6},{1,7},{2,4},{3,5},{4,2},{5,3},{6,0},{7,1},{8,14},{9,15},{10,... | collective-permute-start | bytes 393224 | tf_op jit(solution)/shard_map/ppermute | solution.py:320
  61.0 8.1 %collective-permute-start.12 = (f16[64,1024]{1,0:T(8,128)(2,1)S(1)}, f16[64,1024]{1,0:T(8,128)(2,1)S(1)}, u32[]{:S(2)}, u32[]{:S(2)}) collective-permute-start(f16[64,1024]{1,0:T(8,128)(2,1)S(1)} %pad_maximum_fusion.2), channel_id=1, source_target_pairs={{0,4},{1,3},{2,6},{3,1},{4,0},{5,7},{6,2},{7,5},{8,12},{9,11},{10,... | collective-permute-start | bytes 393224 | tf_op jit(solution)/shard_map/ppermute | solution.py:320
  63.1 6.0 %collective-permute-start.13 = (f16[64,1024]{1,0:T(8,128)(2,1)S(1)}, f16[64,1024]{1,0:T(8,128)(2,1)S(1)}, u32[]{:S(2)}, u32[]{:S(2)}) collective-permute-start(f16[64,1024]{1,0:T(8,128)(2,1)S(1)} %pad_maximum_fusion.2), channel_id=1, source_target_pairs={{0,2},{1,5},{2,0},{3,7},{4,6},{5,1},{6,4},{7,3},{8,10},{9,13},{10,... | collective-permute-start | bytes 393224 | tf_op jit(solution)/shard_map/ppermute | solution.py:320
  63.7 6.9 %collective-permute-start.23 = (f16[64,1024]{1,0:T(8,128)(2,1)S(1)}, f16[64,1024]{1,0:T(8,128)(2,1)S(1)}, u32[]{:S(2)}, u32[]{:S(2)}) collective-permute-start(f16[64,1024]{1,0:T(8,128)(2,1)S(1)} %pad_maximum_fusion.3), channel_id=1, source_target_pairs={{0,6},{1,7},{2,4},{3,5},{4,2},{5,3},{6,0},{7,1},{8,14},{9,15},{10,... | collective-permute-start | bytes 393224 | tf_op jit(solution)/shard_map/ppermute | solution.py:320
  64.7 7.1 %collective-permute-start.24 = (f16[64,1024]{1,0:T(8,128)(2,1)S(1)}, f16[64,1024]{1,0:T(8,128)(2,1)S(1)}, u32[]{:S(2)}, u32[]{:S(2)}) collective-permute-start(f16[64,1024]{1,0:T(8,128)(2,1)S(1)} %pad_maximum_fusion.3), channel_id=1, source_target_pairs={{0,4},{1,3},{2,6},{3,1},{4,0},{5,7},{6,2},{7,5},{8,12},{9,11},{10,... | collective-permute-start | bytes 393224 | tf_op jit(solution)/shard_map/ppermute | solution.py:320
  67.4 5.0 %collective-permute-start.25 = (f16[64,1024]{1,0:T(8,128)(2,1)S(1)}, f16[64,1024]{1,0:T(8,128)(2,1)S(1)}, u32[]{:S(2)}, u32[]{:S(2)}) collective-permute-start(f16[64,1024]{1,0:T(8,128)(2,1)S(1)} %pad_maximum_fusion.3), channel_id=1, source_target_pairs={{0,2},{1,5},{2,0},{3,7},{4,6},{5,1},{6,4},{7,3},{8,10},{9,13},{10,... | collective-permute-start | bytes 393224 | tf_op jit(solution)/shard_map/ppermute | solution.py:320

commit v3 on v2

--- a/solution.py
+++ b/solution.py
@@ -12,6 +12,9 @@
 LANES = 128
 ROWS = 8
 HEADROOM = 10.0
+ORDER = {-2: (1,), 2: (1,), -4: (3, 2, 1), 4: (3, 2, 1)}
+FIRST = 8
+PARTS = 4
 BF16 = jnp.bfloat16
 F32 = jnp.float32
 
@@ -58,7 +61,7 @@
 def align_kernel(
     n_subjects, n_centres, group, meta_ref, pos_ref, nb_ref, data_ref, tmpl_ref, low_ref, high_ref,
     aligned_ref, first_ref, rest_ref, low_out, high_out, low_edge, high_edge, hits_out,
-    wide, acc, hits, sems,
+    wide, acc, hits, rounded, sems, out_sems,
 ):
     k = nb_ref.shape[1]
     span = 2 * k
@@ -130,9 +133,14 @@
             zs += [crosses[:, i * k : (i + 1) * k] for i in range(n_subjects)]
         zs = polar_factors_t(zs)
         spreads = []
-        for n, z in enumerate(zs):
-            pick = members[n // n_subjects][2]
-            spreads.append(dot(pick, jnp.concatenate(split(z), axis=1)).astype(BF16))
+        for member, (_, _, pick) in enumerate(members):
+            mine = [split(z) for z in zs[member * n_subjects : (member + 1) * n_subjects]]
+            stacked = jnp.concatenate(
+                [jnp.concatenate([part[n] for part in mine], axis=1) for n in (0, 1)], axis=0
+            )
+            spread = dot(jnp.concatenate([pick, pick], axis=1), stacked)
+            for i in range(n_subjects):
+                spreads.append(jnp.concatenate(split(spread[:, i * k : (i + 1) * k]), axis=1))
         outs = [
             dot_t(jnp.concatenate([x, x], axis=1), spread) for x, spread in zip(xs, spreads)
         ]
@@ -153,7 +161,7 @@
     high_edge[...] = acc[:, :, own : own + k]
     hits_out[:, :k] = hits[:, k:span]
     hits_out[:, k:] = hits[:, own : own + k]
-    half = own // 2
+    half = first_ref.shape[1] - LANES
     hits[...] = 1.0 / jnp.maximum(hits[...], 1.0)
     scale = hits[:, span:own]
 
@@ -163,17 +171,30 @@
         total = jnp.zeros((2 * ROWS, own - span), F32)
         for i in range(n_subjects):
             mapped = acc[i, rows, span:own] * both
-            aligned_ref[i, rows, k : own - k] = mapped.astype(BF16)
+            rounded[i, rows, :] = mapped.astype(BF16)
             total = total + mapped
         first_ref[rows, :half] = total[:, :half]
         rest_ref[rows, :] = total[:, half:]
         tops = jnp.abs(total[:, :half])
-        while tops.shape[1] > k:
-            tops = jnp.maximum(tops[:, : tops.shape[1] // 2], tops[:, tops.shape[1] // 2 :])
-        return jnp.maximum(top, tops)
-
-    top = lax.fori_loop(0, frames // (2 * ROWS), one_rows, jnp.zeros((2 * ROWS, k), F32))
+        for at in range(0, half, k):
+            top = jnp.maximum(top, tops[:, at : at + k])
+        return top
+
+    top = jnp.zeros((2 * ROWS, k), F32)
+    steps = frames // (2 * ROWS)
+    copies = []
+    for part in range(PARTS):
+        top = lax.fori_loop(part * steps // PARTS, (part + 1) * steps // PARTS, one_rows, top)
+        rows = pl.ds(part * frames // PARTS, frames // PARTS)
+        copies.append(
+            pltpu.make_async_copy(
+                rounded.at[:, rows, :], aligned_ref.at[:, rows, pl.ds(k, own - span)], out_sems.at[part]
+            )
+        )
+        copies[-1].start()
     scale_out(first_ref, jnp.max(top, keepdims=True))
+    for copy in copies:
+        copy.wait()
 
 
 def scale_out(ref, top):
@@ -188,6 +209,7 @@
     n_centres, k = neighbours.shape
     n_wide = own + 2 * k
     group = math.gcd(n_centres, 8)
+    begin = own // 16 * FIRST
     vmem = pl.BlockSpec(memory_space=pltpu.VMEM)
     hbm = pl.BlockSpec(memory_space=pl.ANY)
     smem = pl.BlockSpec(memory_space=pltpu.SMEM)
@@ -195,8 +217,8 @@
         functools.partial(align_kernel, n_subjects, n_centres, group),
         out_shape=(
             jax.ShapeDtypeStruct((n_subjects, frames, own), BF16),
-            jax.ShapeDtypeStruct((frames, own // 2 + LANES), F32),
-            jax.ShapeDtypeStruct((frames, own // 2 - 2 * k), F32),
+            jax.ShapeDtypeStruct((frames, begin + LANES), F32),
+            jax.ShapeDtypeStruct((frames, own - begin - 2 * k), F32),
             jax.ShapeDtypeStruct((n_subjects, frames + ROWS, k), F32),
             jax.ShapeDtypeStruct((n_subjects, frames + ROWS, k), F32),
             jax.ShapeDtypeStruct((n_subjects, frames, k), F32),
@@ -204,12 +226,14 @@
             jax.ShapeDtypeStruct((ROWS, 2 * k), F32),
         ),
         in_specs=[smem, smem, vmem, hbm, hbm, hbm, hbm],
-        out_specs=(vmem,) * 8,
+        out_specs=(hbm,) + (vmem,) * 7,
         scratch_shapes=[
             pltpu.VMEM((n_subjects + 1, frames, n_wide), BF16),
             pltpu.VMEM((n_subjects, frames, n_wide), F32),
             pltpu.VMEM((ROWS, n_wide), F32),
+            pltpu.VMEM((n_subjects, frames, own - 2 * k), BF16),
             pltpu.SemaphoreType.DMA((n_subjects + 1, 3)),
+            pltpu.SemaphoreType.DMA((PARTS,)),
         ],
         compiler_params=pltpu.CompilerParams(vmem_limit_bytes=24 * 1024 * 1024),
         cost_estimate=pl.CostEstimate(flops=16_000_000_000, bytes_accessed=8_000_000, transcendentals=0),
@@ -291,9 +315,9 @@
     def __init__(self):
         self.size = lax.axis_size("subj")
         self.verts = lax.axis_size("vert")
-        n_bits = self.size.bit_length() - 1
-        bits = list(range(n_bits))
-        self.phases = [bits[i : i + 2] for i in range(0, n_bits, 2)]
+        bits = list(range(self.size.bit_length() - 1))
+        self.phases = [bits[i : i + 2] for i in range(0, len(bits), 2)]
+        self.whole = []
 
     def order(self, phase, v):
         return phase if v % 2 == 0 else phase[::-1]
@@ -319,27 +343,36 @@
     def swap(self, value, phase, m):
         return lax.ppermute(value, ("subj", "vert"), self.pairs(phase, m))
 
+    def combine(self, parts):
+        width = parts[0].shape[1] - LANES
+        powers = [part[:, width : width + 1] for part in parts]
+        top = functools.reduce(jnp.maximum, powers)
+        total = sum(part[:, :width] * jnp.exp2(p - top) for part, p in zip(parts, powers))
+        return jnp.concatenate([total, jnp.broadcast_to(top, (total.shape[0], LANES))], axis=1)
+
     def reduce(self, block):
-        width = block.shape[1] - LANES
         for phase in self.phases:
             count = 1 << len(phase)
             rows = block.shape[0] // count
             j = self.mine(phase)
             parts = [lax.dynamic_slice_in_dim(block, j * rows, rows)]
-            for m in range(1, count):
+            for m in ORDER[-count]:
                 sent = lax.dynamic_slice_in_dim(block, (j ^ m) * rows, rows).astype(jnp.float16)
                 parts.append(self.swap(sent, phase, m).astype(F32))
-            powers = [part[:, width : width + 1] for part in parts]
-            top = functools.reduce(jnp.maximum, powers)
-            total = sum(part[:, :width] * jnp.exp2(p - top) for part, p in zip(parts, powers))
-            block = jnp.concatenate([total, jnp.broadcast_to(top, (rows, LANES))], axis=1)
+            block = self.combine(parts)
+        for bit in self.whole:
+            sent = block.astype(jnp.float16)
+            got = self.swap(sent, [bit], 1)
+            block = self.combine([sent.astype(F32), got.astype(F32)])
+        width = block.shape[1] - LANES
         return block[:, :width], block[:, width:]
 
     def gather(self, value):
         for phase in reversed(self.phases):
             count = 1 << len(phase)
             j = self.mine(phase)
-            parts = [value] + [self.swap(value, phase, m) for m in range(1, count)]
+            got = {m: self.swap(value, phase, m) for m in ORDER[count]}
+            parts = [value] + [got[m] for m in range(1, count)]
             placed = []
             for q in range(count):
                 chosen = parts[0]
@@ -368,7 +401,7 @@
         last_edge = jnp.concatenate([data[:, :, own - k :], template[None, :, own - k :]], axis=0)
         low, high = along_vert(last_edge, first_edge)
     aligned, first, rest, low_out, high_out, low_edge, high_edge, edge_hits = align(
-        data, template, low, high, meta, centres - v * own, neighbours + k
+        pltpu.with_memory_space_constraint(data, pltpu.HBM), pltpu.with_memory_space_constraint(template, pltpu.HBM), low, high, meta, centres - v * own, neighbours + k
     )
     if verts == 2:
         from_low = from_high = core_swap(jnp.where(v == 0, high_out, low_out))

time: 74.6 us -> 70.9 us (0.950)
  local copies, waits for them, and re-layouts: 4.97 us -> 2.15 us
  waiting for transfers between devices: 9.21 us -> 7.33 us
    unnamed x4 -> x0, local copies, waits for them, and re-layouts: 2.82 us -> none
    ppermute x24, waiting for transfers between devices: 7.79 us -> 5.91 us  [swap(): return lax.ppermute(value, ('subj', 'vert'), self.pairs(phase, m))]
  transfers between devices with their start and end apart: 26 -> 26, of which waited for: 9 -> 7; matrix products, arithmetic and copies ran while one was open for 5% -> 6% of each run, Pallas kernels for 0% -> 0%
where the time goes in v3:
time: 70.9 us; the launch traced here: 70.6 us
  starting transfers between devices  37.1 us (52%)
  Pallas kernels  17.4 us (25%)
  waiting for transfers between devices  7.33 us (10%)
  other arithmetic  5.68 us (8%)
  local copies, waits for them, and re-layouts  2.15 us (3%)
  between operations  1 us (1%)
    ppermute x24, starting transfers between devices, swap(): return lax.ppermute(value, ('subj', 'vert'), self.pairs(phase, m))  36.4 us
    pallas_call x1, Pallas kernels, align(): pl.pallas_call(functools.partial(align_kernel, n_subjects, n_centres, gro...  16 us
    ppermute x24, waiting for transfers between devices, swap(): return lax.ppermute(value, ('subj', 'vert'), self.pairs(phase, m))  5.91 us
    concatenate x1, other arithmetic, local(): jnp.concatenate([end[:, inner:inner + k], begin, end[:, :inner], end[:, i...  1.5 us
  transfers between devices with their start and end apart: 26, of which 7 were waited for; matrix products, arithmetic and copies ran while one was open for 6% of the time, Pallas kernels for 0%

profile of v3, /device:TPU:0, one launch (start us, length us, event | category | flops | bytes accessed | tf_op | source)
XLA Modules:
  0.0 70.6 jit_solution(16002640738092823576)
XLA Ops:
  0.6 0.9 %constant_dynamic-slice_fusion = bf16[2,256,128]{2,1,0:T(8,128)(2,1)S(1)} fusion(bf16[2,256,2048]{2,1,0:T(8,128)(2,1)} %data_ref.1, s32[]{:T(128)S(6)} %select_n.323), kind=kLoop, calls=%fused_computation.112 | loop fusion | bytes 262148 | tf_op jit(solution)/shard_map/dynamic_slice | solution.py:395
  1.6 0.9 %dynamic-slice_bitcast_fusion = bf16[1,256,128]{2,1,0:T(8,128)(2,1)S(1)} fusion(bf16[256,2048]{1,0:T(8,128)(2,1)} %tmpl_ref.1, s32[]{:T(128)S(6)} %select_n.323), kind=kLoop, calls=%fused_computation.81 | loop fusion | bytes 131076 | tf_op jit(solution)/shard_map/broadcast_in_dim | solution.py:396
  2.4 0.5 collective-permute-start
  3.0 0.7 broadcast_add_fusion.nb_ref
  3.7 0.1 add_convert_fusion.meta_ref
  3.7 0.7 broadcast_subtract_fusion.pos_ref
  4.4 16.0 %align.1 = (bf16[2,256,2048]{2,1,0:T(8,128)(2,1)}, f32[256,1152]{1,0:T(8,128)S(1)}, f32[256,768]{1,0:T(8,128)S(1)}, f32[2,264,128]{2,1,0:T(8,128)S(1)}, f32[2,26...) custom-call(s32[2]{0:T(128)S(1)} %add_convert_fusion.meta_ref, ...), custom_call_target="tpu_custom_call" | custom-call | flops 16000000000 | bytes 8000000 | tf_op jit(solution)/shard_map/align/pallas_call | solution.py:216
  20.5 0.1 collective-permute-start.1
  20.7 1.4 %collective-permute-done.1.low_ref.high_ref = f32[2,264,128]{2,1,0:T(8,128)S(1)} collective-permute-done((f32[2,264,128]{2,1,0:T(8,128)S(1)}, f32[2,264,128]{2,1,0:T(8,128)S(1)}, u32[]{:S(2)}, u32[]{:S(2)}) %collective-permute-start.1) | collective-permute-done | bytes 270368 | tf_op jit(solution)/shard_map/ppermute | solution.py:304
  22.1 1.4 %edges.1 = (bf16[2,256,2048]{2,1,0:T(8,128)(2,1)}, f32[256,1152]{1,0:T(8,128)S(1)}) custom-call(s32[2]{0:T(128)S(1)} %add_convert_fusion.meta_ref, f32[2,256,128]{2,1,0:T(8,128)S(1)} %get-tuple-element.14.low_edge, f32[2,256,128]{2,1,0:T(8,128)S(1)} %get-tuple-element.15.high_edge, ...), custom_call_target="tpu_custom_call", output_to_operand_aliasing={{0}: (7, {})} | custom-call | flops 1000000000 | bytes 2000000 | tf_op jit(solution)/shard_map/edges/pallas_call | solution.py:283
  23.5 0.1 dynamic-slice_convert_fusion.5
  23.5 3.7 %collective-permute-start.2 = (f16[64,1152]{1,0:T(8,128)(2,1)S(1)}, f16[64,1152]{1,0:T(8,128)(2,1)S(1)}, u32[]{:S(2)}, u32[]{:S(2)}) collective-permute-start(f16[64,1152]{1,0:T(8,128)(2,1)S(1)} %get-tuple-element.49), channel_id=1, source_target_pairs={{0,6},{1,7},{2,4},{3,5},{4,2},{5,3},{6,0},{7,1},{8,14},{9,15},{10,... | collective-permute-start | bytes 442376 | tf_op jit(solution)/shard_map/ppermute | solution.py:344
  27.2 0.5 collective-permute-start.3
  27.7 0.1 collective-permute-start.4
  27.9 2.9 %collective-permute-start.14 = (f16[64,1152]{1,0:T(8,128)(2,1)S(1)}, f16[64,1152]{1,0:T(8,128)(2,1)S(1)}, u32[]{:S(2)}, u32[]{:S(2)}) collective-permute-start(f16[64,1152]{1,0:T(8,128)(2,1)S(1)} %get-tuple-element.46), channel_id=1, source_target_pairs={{0,6},{1,7},{2,4},{3,5},{4,2},{5,3},{6,0},{7,1},{8,14},{9,15},{10,... | collective-permute-start | bytes 442376 | tf_op jit(solution)/shard_map/ppermute | solution.py:344
  30.8 0.5 collective-permute-start.15
  31.3 0.6 collective-permute-done.2
  31.9 1.9 %collective-permute-start.16 = (f16[64,1152]{1,0:T(8,128)(2,1)S(1)}, f16[64,1152]{1,0:T(8,128)(2,1)S(1)}, u32[]{:S(2)}, u32[]{:S(2)}) collective-permute-start(f16[64,1152]{1,0:T(8,128)(2,1)S(1)} %get-tuple-element.47), channel_id=1, source_target_pairs={{0,2},{1,5},{2,0},{3,7},{4,6},{5,1},{6,4},{7,3},{8,10},{9,13},{10,... | collective-permute-start | bytes 442376 | tf_op jit(solution)/shard_map/ppermute | solution.py:344
  33.8 1.7 %collective-permute-done.3 = f16[64,1152]{1,0:T(8,128)(2,1)S(1)} collective-permute-done((f16[64,1152]{1,0:T(8,128)(2,1)S(1)}, f16[64,1152]{1,0:T(8,128)(2,1)S(1)}, u32[]{:S(2)}, u32[]{:S(2)}) %collective-permute-start.3) | collective-permute-done | bytes 147488 | tf_op jit(solution)/shard_map/ppermute | solution.py:344
  35.5 0.0 collective-permute-done.4
  35.6 0.2 fusion.29
  35.8 0.1 fusion.3
  36.0 0.1 broadcast_in_dim.12
  36.1 2.6 %collective-permute-start.6 = (f16[16,1152]{1,0:T(8,128)(2,1)S(1)}, f16[16,1152]{1,0:T(8,128)(2,1)S(1)}, u32[]{:S(2)}, u32[]{:S(2)}) collective-permute-start(f16[16,1152]{1,0:T(8,128)(2,1)S(1)} %get-tuple-element.68), channel_id=1, source_target_pairs={{0,16},{1,9},{2,18},{3,11},{4,20},{5,13},{6,22},{7,15},{8,24},{9,1... | collective-permute-start | bytes 110600 | tf_op jit(solution)/shard_map/ppermute | solution.py:344
  38.7 1.6 %collective-permute-start.7 = (f16[16,1152]{1,0:T(8,128)(2,1)S(1)}, f16[16,1152]{1,0:T(8,128)(2,1)S(1)}, u32[]{:S(2)}, u32[]{:S(2)}) collective-permute-start(f16[16,1152]{1,0:T(8,128)(2,1)S(1)} %get-tuple-element.69), channel_id=1, source_target_pairs={{0,8},{1,17},{2,10},{3,19},{4,12},{5,21},{6,14},{7,23},{8,0},{9,25... | collective-permute-start | bytes 110600 | tf_op jit(solution)/shard_map/ppermute | solution.py:344
  40.3 2.0 %collective-permute-start.5 = (f16[16,1152]{1,0:T(8,128)(2,1)S(1)}, f16[16,1152]{1,0:T(8,128)(2,1)S(1)}, u32[]{:S(2)}, u32[]{:S(2)}) collective-permute-start(f16[16,1152]{1,0:T(8,128)(2,1)S(1)} %get-tuple-element.67), channel_id=1, source_target_pairs={{0,24},{1,25},{2,26},{3,27},{4,28},{5,29},{6,30},{7,31},{8,16},{9,... | collective-permute-start | bytes 110600 | tf_op jit(solution)/shard_map/ppermute | solution.py:344
  42.4 0.2 fusion.28
  42.6 0.2 fusion
  42.7 0.1 broadcast_in_dim.14
  42.8 2.7 %collective-permute-start.17 = (f16[16,1152]{1,0:T(8,128)(2,1)S(1)}, f16[16,1152]{1,0:T(8,128)(2,1)S(1)}, u32[]{:S(2)}, u32[]{:S(2)}) collective-permute-start(f16[16,1152]{1,0:T(8,128)(2,1)S(1)} %get-tuple-element.63), channel_id=1, source_target_pairs={{0,24},{1,25},{2,26},{3,27},{4,28},{5,29},{6,30},{7,31},{8,16},{9,... | collective-permute-start | bytes 110600 | tf_op jit(solution)/shard_map/ppermute | solution.py:344
  45.5 1.8 %collective-permute-start.19 = (f16[16,1152]{1,0:T(8,128)(2,1)S(1)}, f16[16,1152]{1,0:T(8,128)(2,1)S(1)}, u32[]{:S(2)}, u32[]{:S(2)}) collective-permute-start(f16[16,1152]{1,0:T(8,128)(2,1)S(1)} %get-tuple-element.65), channel_id=1, source_target_pairs={{0,8},{1,17},{2,10},{3,19},{4,12},{5,21},{6,14},{7,23},{8,0},{9,25... | collective-permute-start | bytes 110600 | tf_op jit(solution)/shard_map/ppermute | solution.py:344
  47.3 0.2 multiply_reduce_fusion.1
  47.5 0.1 fusion.25
  47.6 0.3 collective-permute-start.10
  48.0 2.4 %collective-permute-start.8 = (f16[16,1024]{1,0:T(8,128)(2,1)S(1)}, f16[16,1024]{1,0:T(8,128)(2,1)S(1)}, u32[]{:S(2)}, u32[]{:S(2)}) collective-permute-start(f16[16,1024]{1,0:T(8,128)(2,1)S(1)} %fusion.25), channel_id=1, source_target_pairs={{0,24},{1,25},{2,26},{3,27},{4,28},{5,29},{6,30},{7,31},{8,16},{9,... | collective-permute-start | bytes 98312 | tf_op jit(solution)/shard_map/ppermute | solution.py:344
  50.4 0.8 %collective-permute-start.9 = (f16[16,1024]{1,0:T(8,128)(2,1)S(1)}, f16[16,1024]{1,0:T(8,128)(2,1)S(1)}, u32[]{:S(2)}, u32[]{:S(2)}) collective-permute-start(f16[16,1024]{1,0:T(8,128)(2,1)S(1)} %fusion.25), channel_id=1, source_target_pairs={{0,16},{1,9},{2,18},{3,11},{4,20},{5,13},{6,22},{7,15},{8,24},{9,1... | collective-permute-start | bytes 98312 | tf_op jit(solution)/shard_map/ppermute | solution.py:344
  51.3 0.2 multiply_reduce_fusion
  51.5 0.1 fusion.21
  51.6 2.7 %collective-permute-start.20 = (f16[16,1024]{1,0:T(8,128)(2,1)S(1)}, f16[16,1024]{1,0:T(8,128)(2,1)S(1)}, u32[]{:S(2)}, u32[]{:S(2)}) collective-permute-start(f16[16,1024]{1,0:T(8,128)(2,1)S(1)} %fusion.21), channel_id=1, source_target_pairs={{0,24},{1,25},{2,26},{3,27},{4,28},{5,29},{6,30},{7,31},{8,16},{9,... | collective-permute-start | bytes 98312 | tf_op jit(solution)/shard_map/ppermute | solution.py:344
  54.3 0.0 collective-permute-start.21
  54.3 0.1 mul.311
  54.3 0.1 mul.281
  54.4 1.8 %collective-permute-start.22 = (f16[16,1024]{1,0:T(8,128)(2,1)S(1)}, f16[16,1024]{1,0:T(8,128)(2,1)S(1)}, u32[]{:S(2)}, u32[]{:S(2)}) collective-permute-start(f16[16,1024]{1,0:T(8,128)(2,1)S(1)} %fusion.21), channel_id=1, source_target_pairs={{0,8},{1,17},{2,10},{3,19},{4,12},{5,21},{6,14},{7,23},{8,0},{9,25... | collective-permute-start | bytes 98312 | tf_op jit(solution)/shard_map/ppermute | solution.py:344
  56.3 0.1 select_select_fusion.15
  56.4 2.6 %collective-permute-start.11 = (f16[64,1024]{1,0:T(8,128)(2,1)S(1)}, f16[64,1024]{1,0:T(8,128)(2,1)S(1)}, u32[]{:S(2)}, u32[]{:S(2)}) collective-permute-start(f16[64,1024]{1,0:T(8,128)(2,1)S(1)} %pad_maximum_fusion.2), channel_id=1, source_target_pairs={{0,6},{1,7},{2,4},{3,5},{4,2},{5,3},{6,0},{7,1},{8,14},{9,15},{10,... | collective-permute-start | bytes 393224 | tf_op jit(solution)/shard_map/ppermute | solution.py:344
  58.9 0.4 collective-permute-start.12
  59.4 0.5 collective-permute-start.13
  59.9 0.1 select_select_fusion.11
  60.1 2.6 %collective-permute-start.23 = (f16[64,1024]{1,0:T(8,128)(2,1)S(1)}, f16[64,1024]{1,0:T(8,128)(2,1)S(1)}, u32[]{:S(2)}, u32[]{:S(2)}) collective-permute-start(f16[64,1024]{1,0:T(8,128)(2,1)S(1)} %pad_maximum_fusion.3), channel_id=1, source_target_pairs={{0,6},{1,7},{2,4},{3,5},{4,2},{5,3},{6,0},{7,1},{8,14},{9,15},{10,... | collective-permute-start | bytes 393224 | tf_op jit(solution)/shard_map/ppermute | solution.py:344
  62.6 0.4 collective-permute-start.24
  63.1 0.6 collective-permute-done.11
  63.7 1.5 %collective-permute-start.25 = (f16[64,1024]{1,0:T(8,128)(2,1)S(1)}, f16[64,1024]{1,0:T(8,128)(2,1)S(1)}, u32[]{:S(2)}, u32[]{:S(2)}) collective-permute-start(f16[64,1024]{1,0:T(8,128)(2,1)S(1)} %pad_maximum_fusion.3), channel_id=1, source_target_pairs={{0,2},{1,5},{2,0},{3,7},{4,6},{5,1},{6,4},{7,3},{8,10},{9,13},{10,... | collective-permute-start | bytes 393224 | tf_op jit(solution)/shard_map/ppermute | solution.py:344
  65.2 0.7 collective-permute-done.12
  65.9 0.1 select_select_fusion.6
  66.0 0.1 select_select_fusion.7
  66.2 0.2 convert_multiply_fusion.1
  66.3 0.1 slice.171
  66.4 0.9 %collective-permute-done.23 = f16[64,1024]{1,0:T(8,128)(2,1)S(1)} collective-permute-done((f16[64,1024]{1,0:T(8,128)(2,1)S(1)}, f16[64,1024]{1,0:T(8,128)(2,1)S(1)}, u32[]{:S(2)}, u32[]{:S(2)}) %collective-permute-start.23) | collective-permute-done | bytes 131104 | tf_op jit(solution)/shard_map/ppermute | solution.py:344
  67.3 1.4 %collective-permute-done.24 = f16[64,1024]{1,0:T(8,128)(2,1)S(1)} collective-permute-done((f16[64,1024]{1,0:T(8,128)(2,1)S(1)}, f16[64,1024]{1,0:T(8,128)(2,1)S(1)}, u32[]{:S(2)}, u32[]{:S(2)}) %collective-permute-start.24) | collective-permute-done | bytes 131104 | tf_op jit(solution)/shard_map/ppermute | solution.py:344
  68.7 0.0 collective-permute-done.25
  68.7 0.1 select_select_fusion.2
  68.8 0.1 select_select_fusion.3
  69.0 0.2 convert_multiply_fusion
  69.1 1.5 %pad_maximum_fusion = f32[256,2048]{1,0:T(8,128)} fusion(f32[256,128]{1,0:T(8,128)S(1)} %get-tuple-element.53, f32[256,768]{1,0:T(8,128)S(1)} %slice.171, f32[256,1024]{1,0:T(8,128)S(1)} %convert_multiply_fusion, f32[256,128]{1,0:T(8,128)S(1)} %get-tuple-element.52), kind=kLoop, calls=%fused_computation | loop fusion | flops 1572864 | bytes 4194304 | tf_op jit(solution)/shard_map/concatenate | solution.py:426
  (40 shorter events, 0.5 us)
Async XLA Ops:
  2.4 2.0 %collective-permute-start = (bf16[3,256,128]{2,1,0:T(8,128)(2,1)S(1)}, bf16[3,256,128]{2,1,0:T(8,128)(2,1)S(1)}, u32[]{:S(2)}, u32[]{:S(2)}) collective-permute-start(bf16[3,256,128]{2,1,0:T(8,128)(2,1)S(1)} %pad_maximum_fusion.1), channel_id=1, source_target_pairs={{0,1},{1,0},{2,3},{3,2},{4,5},{5,4},{6,7},{7,6},{8,9},{9,8},{10,11... | collective-permute-start | bytes 589832 | tf_op jit(solution)/shard_map/ppermute | solution.py:304
  20.5 1.6 %collective-permute-start.1 = (f32[2,264,128]{2,1,0:T(8,128)S(1)}, f32[2,264,128]{2,1,0:T(8,128)S(1)}, u32[]{:S(2)}, u32[]{:S(2)}) collective-permute-start(f32[2,264,128]{2,1,0:T(8,128)S(1)} %broadcast_select_fusion), channel_id=1, source_target_pairs={{0,1},{1,0},{2,3},{3,2},{4,5},{5,4},{6,7},{7,6},{8,9},{9,8},{10,11... | collective-permute-start | bytes 811016 | tf_op jit(solution)/shard_map/ppermute | solution.py:304
  23.5 8.4 %collective-permute-start.2 = (f16[64,1152]{1,0:T(8,128)(2,1)S(1)}, f16[64,1152]{1,0:T(8,128)(2,1)S(1)}, u32[]{:S(2)}, u32[]{:S(2)}) collective-permute-start(f16[64,1152]{1,0:T(8,128)(2,1)S(1)} %get-tuple-element.49), channel_id=1, source_target_pairs={{0,6},{1,7},{2,4},{3,5},{4,2},{5,3},{6,0},{7,1},{8,14},{9,15},{10,... | collective-permute-start | bytes 442376 | tf_op jit(solution)/shard_map/ppermute | solution.py:344
  27.2 8.3 %collective-permute-start.3 = (f16[64,1152]{1,0:T(8,128)(2,1)S(1)}, f16[64,1152]{1,0:T(8,128)(2,1)S(1)}, u32[]{:S(2)}, u32[]{:S(2)}) collective-permute-start(f16[64,1152]{1,0:T(8,128)(2,1)S(1)} %get-tuple-element.51), channel_id=1, source_target_pairs={{0,4},{1,3},{2,6},{3,1},{4,0},{5,7},{6,2},{7,5},{8,12},{9,11},{10,... | collective-permute-start | bytes 442376 | tf_op jit(solution)/shard_map/ppermute | solution.py:344
  27.7 7.9 %collective-permute-start.4 = (f16[64,1152]{1,0:T(8,128)(2,1)S(1)}, f16[64,1152]{1,0:T(8,128)(2,1)S(1)}, u32[]{:S(2)}, u32[]{:S(2)}) collective-permute-start(f16[64,1152]{1,0:T(8,128)(2,1)S(1)} %get-tuple-element.50), channel_id=1, source_target_pairs={{0,2},{1,5},{2,0},{3,7},{4,6},{5,1},{6,4},{7,3},{8,10},{9,13},{10,... | collective-permute-start | bytes 442376 | tf_op jit(solution)/shard_map/ppermute | solution.py:344
  27.9 12.4 %collective-permute-start.14 = (f16[64,1152]{1,0:T(8,128)(2,1)S(1)}, f16[64,1152]{1,0:T(8,128)(2,1)S(1)}, u32[]{:S(2)}, u32[]{:S(2)}) collective-permute-start(f16[64,1152]{1,0:T(8,128)(2,1)S(1)} %get-tuple-element.46), channel_id=1, source_target_pairs={{0,6},{1,7},{2,4},{3,5},{4,2},{5,3},{6,0},{7,1},{8,14},{9,15},{10,... | collective-permute-start | bytes 442376 | tf_op jit(solution)/shard_map/ppermute | solution.py:344
  30.8 11.5 %collective-permute-start.15 = (f16[64,1152]{1,0:T(8,128)(2,1)S(1)}, f16[64,1152]{1,0:T(8,128)(2,1)S(1)}, u32[]{:S(2)}, u32[]{:S(2)}) collective-permute-start(f16[64,1152]{1,0:T(8,128)(2,1)S(1)} %get-tuple-element.48), channel_id=1, source_target_pairs={{0,4},{1,3},{2,6},{3,1},{4,0},{5,7},{6,2},{7,5},{8,12},{9,11},{10,... | collective-permute-start | bytes 442376 | tf_op jit(solution)/shard_map/ppermute | solution.py:344
  31.9 10.4 %collective-permute-start.16 = (f16[64,1152]{1,0:T(8,128)(2,1)S(1)}, f16[64,1152]{1,0:T(8,128)(2,1)S(1)}, u32[]{:S(2)}, u32[]{:S(2)}) collective-permute-start(f16[64,1152]{1,0:T(8,128)(2,1)S(1)} %get-tuple-element.47), channel_id=1, source_target_pairs={{0,2},{1,5},{2,0},{3,7},{4,6},{5,1},{6,4},{7,3},{8,10},{9,13},{10,... | collective-permute-start | bytes 442376 | tf_op jit(solution)/shard_map/ppermute | solution.py:344
  36.1 9.5 %collective-permute-start.6 = (f16[16,1152]{1,0:T(8,128)(2,1)S(1)}, f16[16,1152]{1,0:T(8,128)(2,1)S(1)}, u32[]{:S(2)}, u32[]{:S(2)}) collective-permute-start(f16[16,1152]{1,0:T(8,128)(2,1)S(1)} %get-tuple-element.68), channel_id=1, source_target_pairs={{0,16},{1,9},{2,18},{3,11},{4,20},{5,13},{6,22},{7,15},{8,24},{9,1... | collective-permute-start | bytes 110600 | tf_op jit(solution)/shard_map/ppermute | solution.py:344
  38.7 8.6 %collective-permute-start.7 = (f16[16,1152]{1,0:T(8,128)(2,1)S(1)}, f16[16,1152]{1,0:T(8,128)(2,1)S(1)}, u32[]{:S(2)}, u32[]{:S(2)}) collective-permute-start(f16[16,1152]{1,0:T(8,128)(2,1)S(1)} %get-tuple-element.69), channel_id=1, source_target_pairs={{0,8},{1,17},{2,10},{3,19},{4,12},{5,21},{6,14},{7,23},{8,0},{9,25... | collective-permute-start | bytes 110600 | tf_op jit(solution)/shard_map/ppermute | solution.py:344
  40.3 7.0 %collective-permute-start.5 = (f16[16,1152]{1,0:T(8,128)(2,1)S(1)}, f16[16,1152]{1,0:T(8,128)(2,1)S(1)}, u32[]{:S(2)}, u32[]{:S(2)}) collective-permute-start(f16[16,1152]{1,0:T(8,128)(2,1)S(1)} %get-tuple-element.67), channel_id=1, source_target_pairs={{0,24},{1,25},{2,26},{3,27},{4,28},{5,29},{6,30},{7,31},{8,16},{9,... | collective-permute-start | bytes 110600 | tf_op jit(solution)/shard_map/ppermute | solution.py:344
  42.8 7.6 %collective-permute-start.17 = (f16[16,1152]{1,0:T(8,128)(2,1)S(1)}, f16[16,1152]{1,0:T(8,128)(2,1)S(1)}, u32[]{:S(2)}, u32[]{:S(2)}) collective-permute-start(f16[16,1152]{1,0:T(8,128)(2,1)S(1)} %get-tuple-element.63), channel_id=1, source_target_pairs={{0,24},{1,25},{2,26},{3,27},{4,28},{5,29},{6,30},{7,31},{8,16},{9,... | collective-permute-start | bytes 110600 | tf_op jit(solution)/shard_map/ppermute | solution.py:344
  45.5 5.7 %collective-permute-start.18 = (f16[16,1152]{1,0:T(8,128)(2,1)S(1)}, f16[16,1152]{1,0:T(8,128)(2,1)S(1)}, u32[]{:S(2)}, u32[]{:S(2)}) collective-permute-start(f16[16,1152]{1,0:T(8,128)(2,1)S(1)} %get-tuple-element.64), channel_id=1, source_target_pairs={{0,16},{1,9},{2,18},{3,11},{4,20},{5,13},{6,22},{7,15},{8,24},{9,1... | collective-permute-start | bytes 110600 | tf_op jit(solution)/shard_map/ppermute | solution.py:344
  45.5 5.7 %collective-permute-start.19 = (f16[16,1152]{1,0:T(8,128)(2,1)S(1)}, f16[16,1152]{1,0:T(8,128)(2,1)S(1)}, u32[]{:S(2)}, u32[]{:S(2)}) collective-permute-start(f16[16,1152]{1,0:T(8,128)(2,1)S(1)} %get-tuple-element.65), channel_id=1, source_target_pairs={{0,8},{1,17},{2,10},{3,19},{4,12},{5,21},{6,14},{7,23},{8,0},{9,25... | collective-permute-start | bytes 110600 | tf_op jit(solution)/shard_map/ppermute | solution.py:344
  47.6 6.8 %collective-permute-start.10 = (f16[16,1024]{1,0:T(8,128)(2,1)S(1)}, f16[16,1024]{1,0:T(8,128)(2,1)S(1)}, u32[]{:S(2)}, u32[]{:S(2)}) collective-permute-start(f16[16,1024]{1,0:T(8,128)(2,1)S(1)} %fusion.25), channel_id=1, source_target_pairs={{0,8},{1,17},{2,10},{3,19},{4,12},{5,21},{6,14},{7,23},{8,0},{9,25... | collective-permute-start | bytes 98312 | tf_op jit(solution)/shard_map/ppermute | solution.py:344
  48.0 8.3 %collective-permute-start.8 = (f16[16,1024]{1,0:T(8,128)(2,1)S(1)}, f16[16,1024]{1,0:T(8,128)(2,1)S(1)}, u32[]{:S(2)}, u32[]{:S(2)}) collective-permute-start(f16[16,1024]{1,0:T(8,128)(2,1)S(1)} %fusion.25), channel_id=1, source_target_pairs={{0,24},{1,25},{2,26},{3,27},{4,28},{5,29},{6,30},{7,31},{8,16},{9,... | collective-permute-start | bytes 98312 | tf_op jit(solution)/shard_map/ppermute | solution.py:344
  50.4 5.8 %collective-permute-start.9 = (f16[16,1024]{1,0:T(8,128)(2,1)S(1)}, f16[16,1024]{1,0:T(8,128)(2,1)S(1)}, u32[]{:S(2)}, u32[]{:S(2)}) collective-permute-start(f16[16,1024]{1,0:T(8,128)(2,1)S(1)} %fusion.25), channel_id=1, source_target_pairs={{0,16},{1,9},{2,18},{3,11},{4,20},{5,13},{6,22},{7,15},{8,24},{9,1... | collective-permute-start | bytes 98312 | tf_op jit(solution)/shard_map/ppermute | solution.py:344
  51.6 7.8 %collective-permute-start.20 = (f16[16,1024]{1,0:T(8,128)(2,1)S(1)}, f16[16,1024]{1,0:T(8,128)(2,1)S(1)}, u32[]{:S(2)}, u32[]{:S(2)}) collective-permute-start(f16[16,1024]{1,0:T(8,128)(2,1)S(1)} %fusion.21), channel_id=1, source_target_pairs={{0,24},{1,25},{2,26},{3,27},{4,28},{5,29},{6,30},{7,31},{8,16},{9,... | collective-permute-start | bytes 98312 | tf_op jit(solution)/shard_map/ppermute | solution.py:344
  54.3 5.7 %collective-permute-start.21 = (f16[16,1024]{1,0:T(8,128)(2,1)S(1)}, f16[16,1024]{1,0:T(8,128)(2,1)S(1)}, u32[]{:S(2)}, u32[]{:S(2)}) collective-permute-start(f16[16,1024]{1,0:T(8,128)(2,1)S(1)} %fusion.21), channel_id=1, source_target_pairs={{0,16},{1,9},{2,18},{3,11},{4,20},{5,13},{6,22},{7,15},{8,24},{9,1... | collective-permute-start | bytes 98312 | tf_op jit(solution)/shard_map/ppermute | solution.py:344
  54.4 5.5 %collective-permute-start.22 = (f16[16,1024]{1,0:T(8,128)(2,1)S(1)}, f16[16,1024]{1,0:T(8,128)(2,1)S(1)}, u32[]{:S(2)}, u32[]{:S(2)}) collective-permute-start(f16[16,1024]{1,0:T(8,128)(2,1)S(1)} %fusion.21), channel_id=1, source_target_pairs={{0,8},{1,17},{2,10},{3,19},{4,12},{5,21},{6,14},{7,23},{8,0},{9,25... | collective-permute-start | bytes 98312 | tf_op jit(solution)/shard_map/ppermute | solution.py:344
  56.4 7.3 %collective-permute-start.11 = (f16[64,1024]{1,0:T(8,128)(2,1)S(1)}, f16[64,1024]{1,0:T(8,128)(2,1)S(1)}, u32[]{:S(2)}, u32[]{:S(2)}) collective-permute-start(f16[64,1024]{1,0:T(8,128)(2,1)S(1)} %pad_maximum_fusion.2), channel_id=1, source_target_pairs={{0,6},{1,7},{2,4},{3,5},{4,2},{5,3},{6,0},{7,1},{8,14},{9,15},{10,... | collective-permute-start | bytes 393224 | tf_op jit(solution)/shard_map/ppermute | solution.py:344
  58.9 6.9 %collective-permute-start.12 = (f16[64,1024]{1,0:T(8,128)(2,1)S(1)}, f16[64,1024]{1,0:T(8,128)(2,1)S(1)}, u32[]{:S(2)}, u32[]{:S(2)}) collective-permute-start(f16[64,1024]{1,0:T(8,128)(2,1)S(1)} %pad_maximum_fusion.2), channel_id=1, source_target_pairs={{0,4},{1,3},{2,6},{3,1},{4,0},{5,7},{6,2},{7,5},{8,12},{9,11},{10,... | collective-permute-start | bytes 393224 | tf_op jit(solution)/shard_map/ppermute | solution.py:344
  59.4 6.5 %collective-permute-start.13 = (f16[64,1024]{1,0:T(8,128)(2,1)S(1)}, f16[64,1024]{1,0:T(8,128)(2,1)S(1)}, u32[]{:S(2)}, u32[]{:S(2)}) collective-permute-start(f16[64,1024]{1,0:T(8,128)(2,1)S(1)} %pad_maximum_fusion.2), channel_id=1, source_target_pairs={{0,2},{1,5},{2,0},{3,7},{4,6},{5,1},{6,4},{7,3},{8,10},{9,13},{10,... | collective-permute-start | bytes 393224 | tf_op jit(solution)/shard_map/ppermute | solution.py:344
  60.1 7.3 %collective-permute-start.23 = (f16[64,1024]{1,0:T(8,128)(2,1)S(1)}, f16[64,1024]{1,0:T(8,128)(2,1)S(1)}, u32[]{:S(2)}, u32[]{:S(2)}) collective-permute-start(f16[64,1024]{1,0:T(8,128)(2,1)S(1)} %pad_maximum_fusion.3), channel_id=1, source_target_pairs={{0,6},{1,7},{2,4},{3,5},{4,2},{5,3},{6,0},{7,1},{8,14},{9,15},{10,... | collective-permute-start | bytes 393224 | tf_op jit(solution)/shard_map/ppermute | solution.py:344
  62.6 6.0 %collective-permute-start.24 = (f16[64,1024]{1,0:T(8,128)(2,1)S(1)}, f16[64,1024]{1,0:T(8,128)(2,1)S(1)}, u32[]{:S(2)}, u32[]{:S(2)}) collective-permute-start(f16[64,1024]{1,0:T(8,128)(2,1)S(1)} %pad_maximum_fusion.3), channel_id=1, source_target_pairs={{0,4},{1,3},{2,6},{3,1},{4,0},{5,7},{6,2},{7,5},{8,12},{9,11},{10,... | collective-permute-start | bytes 393224 | tf_op jit(solution)/shard_map/ppermute | solution.py:344
  63.7 5.0 %collective-permute-start.25 = (f16[64,1024]{1,0:T(8,128)(2,1)S(1)}, f16[64,1024]{1,0:T(8,128)(2,1)S(1)}, u32[]{:S(2)}, u32[]{:S(2)}) collective-permute-start(f16[64,1024]{1,0:T(8,128)(2,1)S(1)} %pad_maximum_fusion.3), channel_id=1, source_target_pairs={{0,2},{1,5},{2,0},{3,7},{4,6},{5,1},{6,4},{7,3},{8,10},{9,13},{10,... | collective-permute-start | bytes 393224 | tf_op jit(solution)/shard_map/ppermute | solution.py:344

commit v4 on v3

--- a/solution.py
+++ b/solution.py
@@ -42,14 +42,10 @@
     zs = [z / jnp.sqrt(norm_sq + 1e-06) for z, norm_sq in zip(zs, sums)]
     for _ in range(NS_STEPS):
         boths = [jnp.concatenate(split(z), axis=1) for z in zs]
-        grams = []
-        for both in boths:
-            k = both.shape[0]
-            hi, lo = both[:, :k], both[:, k:]
-            pair = jnp.concatenate(
-                [jnp.concatenate([hi, hi], axis=1), jnp.concatenate([lo, lo], axis=1)], axis=0
-            )
-            grams.append(dot_t(both, pair))
+        k = zs[0].shape[0]
+        flips = [both.T for both in boths]
+        boths_t = [jnp.concatenate([f[:k], f[k:]], axis=1) for f in flips]
+        grams = [dot(both, jnp.concatenate([bt, bt], axis=0)) for both, bt in zip(boths, boths_t)]
         grams = [jnp.concatenate(split(halves(gram)), axis=1) for gram in grams]
         moved = [
             dot(gram, jnp.concatenate([both, both], axis=0)) for gram, both in zip(grams, boths)
@@ -122,10 +118,12 @@
         xs = []
         m_ts = []
         for first, keep, pick in members:
-            for i in range(n_subjects):
-                xs.append(dot(window(i, first, keep), pick).astype(BF16))
-            m_ts.append(dot(window(n_subjects, first, keep), pick))
-        m_ts = [m.T.astype(BF16) for m in m_ts]
+            rows = [window(i, first, keep) for i in range(n_subjects + 1)]
+            picked = dot(jnp.concatenate(rows, axis=0), pick).astype(BF16)
+            frames = rows[0].shape[0]
+            xs += [picked[i * frames : (i + 1) * frames] for i in range(n_subjects)]
+            m_ts.append(picked[n_subjects * frames :])
+        m_ts = [m.T for m in m_ts]
         zs = []
         for member in range(group):
             mine = xs[member * n_subjects : (member + 1) * n_subjects]

time: 70.9 us -> 69.1 us (0.975)
  Pallas kernels: 17.4 us -> 15.6 us
    pallas_call x1, Pallas kernels: 16 us -> 14.2 us  [align(): pl.pallas_call(functools.partial(align_kernel, n_subjects, n_centres, gro...]
where the time goes in v4:
time: 69.1 us; the launch traced here: 68.8 us
  starting transfers between devices  37.1 us (54%)
  Pallas kernels  15.6 us (23%)
  waiting for transfers between devices  7.33 us (11%)
  other arithmetic  5.68 us (8%)
  local copies, waits for them, and re-layouts  2.15 us (3%)
  between operations  0.99 us (1%)
    ppermute x24, starting transfers between devices, swap(): return lax.ppermute(value, ('subj', 'vert'), self.pairs(phase, m))  36.4 us
    pallas_call x1, Pallas kernels, align(): pl.pallas_call(functools.partial(align_kernel, n_subjects, n_centres, gro...  14.2 us
    ppermute x24, waiting for transfers between devices, swap(): return lax.ppermute(value, ('subj', 'vert'), self.pairs(phase, m))  5.91 us
    concatenate x1, other arithmetic, local(): jnp.concatenate([end[:, inner:inner + k], begin, end[:, :inner], end[:, i...  1.5 us
    ppermute x2, waiting for transfers between devices, core_swap(): return lax.ppermute(value, 'vert', [(0, 1), (1, 0)])  1.42 us
  transfers between devices with their start and end apart: 26, of which 7 were waited for; matrix products, arithmetic and copies ran while one was open for 6% of the time, Pallas kernels for 0%

profile of v4, /device:TPU:0, one launch (start us, length us, event | category | flops | bytes accessed | tf_op | source)
XLA Modules:
  0.0 68.8 jit_solution(13720443645953859675)
XLA Ops:
  0.6 0.9 %constant_dynamic-slice_fusion = bf16[2,256,128]{2,1,0:T(8,128)(2,1)S(1)} fusion(bf16[2,256,2048]{2,1,0:T(8,128)(2,1)} %data_ref.1, s32[]{:T(128)S(6)} %select_n.323), kind=kLoop, calls=%fused_computation.112 | loop fusion | bytes 262148 | tf_op jit(solution)/shard_map/dynamic_slice | solution.py:393
  1.6 0.9 %dynamic-slice_bitcast_fusion = bf16[1,256,128]{2,1,0:T(8,128)(2,1)S(1)} fusion(bf16[256,2048]{1,0:T(8,128)(2,1)} %tmpl_ref.1, s32[]{:T(128)S(6)} %select_n.323), kind=kLoop, calls=%fused_computation.81 | loop fusion | bytes 131076 | tf_op jit(solution)/shard_map/broadcast_in_dim | solution.py:394
  2.4 0.5 collective-permute-start
  3.0 0.7 %broadcast_add_fusion.nb_ref = s32[16,128]{1,0:T(8,128)S(1)} fusion(s32[16,128]{1,0:T(8,128)} %param.7), kind=kLoop, calls=%fused_computation.113 | loop fusion | flops 2048 | bytes 16384 | tf_op jit(solution)/shard_map/add | solution.py:402
  3.7 0.1 add_convert_fusion.meta_ref
  3.7 0.7 broadcast_subtract_fusion.pos_ref
  4.4 14.2 %align.1 = (bf16[2,256,2048]{2,1,0:T(8,128)(2,1)}, f32[256,1152]{1,0:T(8,128)S(1)}, f32[256,768]{1,0:T(8,128)S(1)}, f32[2,264,128]{2,1,0:T(8,128)S(1)}, f32[2,26...) custom-call(s32[2]{0:T(128)S(1)} %add_convert_fusion.meta_ref, ...), custom_call_target="tpu_custom_call" | custom-call | flops 16000000000 | bytes 8000000 | tf_op jit(solution)/shard_map/align/pallas_call | solution.py:214
  18.6 0.1 collective-permute-start.1
  18.8 1.4 %collective-permute-done.1.low_ref.high_ref = f32[2,264,128]{2,1,0:T(8,128)S(1)} collective-permute-done((f32[2,264,128]{2,1,0:T(8,128)S(1)}, f32[2,264,128]{2,1,0:T(8,128)S(1)}, u32[]{:S(2)}, u32[]{:S(2)}) %collective-permute-start.1) | collective-permute-done | bytes 270368 | tf_op jit(solution)/shard_map/ppermute | solution.py:302
  20.3 1.4 %edges.1 = (bf16[2,256,2048]{2,1,0:T(8,128)(2,1)}, f32[256,1152]{1,0:T(8,128)S(1)}) custom-call(s32[2]{0:T(128)S(1)} %add_convert_fusion.meta_ref, f32[2,256,128]{2,1,0:T(8,128)S(1)} %get-tuple-element.14.low_edge, f32[2,256,128]{2,1,0:T(8,128)S(1)} %get-tuple-element.15.high_edge, ...), custom_call_target="tpu_custom_call", output_to_operand_aliasing={{0}: (7, {})} | custom-call | flops 1000000000 | bytes 2000000 | tf_op jit(solution)/shard_map/edges/pallas_call | solution.py:281
  21.6 0.1 dynamic-slice_convert_fusion.5
  21.7 3.7 %collective-permute-start.2 = (f16[64,1152]{1,0:T(8,128)(2,1)S(1)}, f16[64,1152]{1,0:T(8,128)(2,1)S(1)}, u32[]{:S(2)}, u32[]{:S(2)}) collective-permute-start(f16[64,1152]{1,0:T(8,128)(2,1)S(1)} %get-tuple-element.49), channel_id=1, source_target_pairs={{0,6},{1,7},{2,4},{3,5},{4,2},{5,3},{6,0},{7,1},{8,14},{9,15},{10,... | collective-permute-start | bytes 442376 | tf_op jit(solution)/shard_map/ppermute | solution.py:342
  25.4 0.5 collective-permute-start.3
  25.9 0.1 collective-permute-start.4
  26.1 2.9 %collective-permute-start.14 = (f16[64,1152]{1,0:T(8,128)(2,1)S(1)}, f16[64,1152]{1,0:T(8,128)(2,1)S(1)}, u32[]{:S(2)}, u32[]{:S(2)}) collective-permute-start(f16[64,1152]{1,0:T(8,128)(2,1)S(1)} %get-tuple-element.46), channel_id=1, source_target_pairs={{0,6},{1,7},{2,4},{3,5},{4,2},{5,3},{6,0},{7,1},{8,14},{9,15},{10,... | collective-permute-start | bytes 442376 | tf_op jit(solution)/shard_map/ppermute | solution.py:342
  29.0 0.5 collective-permute-start.15
  29.5 0.6 collective-permute-done.2
  30.1 1.9 %collective-permute-start.16 = (f16[64,1152]{1,0:T(8,128)(2,1)S(1)}, f16[64,1152]{1,0:T(8,128)(2,1)S(1)}, u32[]{:S(2)}, u32[]{:S(2)}) collective-permute-start(f16[64,1152]{1,0:T(8,128)(2,1)S(1)} %get-tuple-element.47), channel_id=1, source_target_pairs={{0,2},{1,5},{2,0},{3,7},{4,6},{5,1},{6,4},{7,3},{8,10},{9,13},{10,... | collective-permute-start | bytes 442376 | tf_op jit(solution)/shard_map/ppermute | solution.py:342
  32.0 1.7 %collective-permute-done.3 = f16[64,1152]{1,0:T(8,128)(2,1)S(1)} collective-permute-done((f16[64,1152]{1,0:T(8,128)(2,1)S(1)}, f16[64,1152]{1,0:T(8,128)(2,1)S(1)}, u32[]{:S(2)}, u32[]{:S(2)}) %collective-permute-start.3) | collective-permute-done | bytes 147488 | tf_op jit(solution)/shard_map/ppermute | solution.py:342
  33.7 0.0 collective-permute-done.4
  33.8 0.2 fusion.29
  34.0 0.1 fusion.3
  34.1 0.1 broadcast_in_dim.12
  34.2 2.7 %collective-permute-start.6 = (f16[16,1152]{1,0:T(8,128)(2,1)S(1)}, f16[16,1152]{1,0:T(8,128)(2,1)S(1)}, u32[]{:S(2)}, u32[]{:S(2)}) collective-permute-start(f16[16,1152]{1,0:T(8,128)(2,1)S(1)} %get-tuple-element.68), channel_id=1, source_target_pairs={{0,16},{1,9},{2,18},{3,11},{4,20},{5,13},{6,22},{7,15},{8,24},{9,1... | collective-permute-start | bytes 110600 | tf_op jit(solution)/shard_map/ppermute | solution.py:342
  36.9 1.6 %collective-permute-start.7 = (f16[16,1152]{1,0:T(8,128)(2,1)S(1)}, f16[16,1152]{1,0:T(8,128)(2,1)S(1)}, u32[]{:S(2)}, u32[]{:S(2)}) collective-permute-start(f16[16,1152]{1,0:T(8,128)(2,1)S(1)} %get-tuple-element.69), channel_id=1, source_target_pairs={{0,8},{1,17},{2,10},{3,19},{4,12},{5,21},{6,14},{7,23},{8,0},{9,25... | collective-permute-start | bytes 110600 | tf_op jit(solution)/shard_map/ppermute | solution.py:342
  38.5 2.0 %collective-permute-start.5 = (f16[16,1152]{1,0:T(8,128)(2,1)S(1)}, f16[16,1152]{1,0:T(8,128)(2,1)S(1)}, u32[]{:S(2)}, u32[]{:S(2)}) collective-permute-start(f16[16,1152]{1,0:T(8,128)(2,1)S(1)} %get-tuple-element.67), channel_id=1, source_target_pairs={{0,24},{1,25},{2,26},{3,27},{4,28},{5,29},{6,30},{7,31},{8,16},{9,... | collective-permute-start | bytes 110600 | tf_op jit(solution)/shard_map/ppermute | solution.py:342
  40.6 0.2 fusion.28
  40.8 0.2 fusion
  40.9 0.1 broadcast_in_dim.14
  41.0 2.7 %collective-permute-start.17 = (f16[16,1152]{1,0:T(8,128)(2,1)S(1)}, f16[16,1152]{1,0:T(8,128)(2,1)S(1)}, u32[]{:S(2)}, u32[]{:S(2)}) collective-permute-start(f16[16,1152]{1,0:T(8,128)(2,1)S(1)} %get-tuple-element.63), channel_id=1, source_target_pairs={{0,24},{1,25},{2,26},{3,27},{4,28},{5,29},{6,30},{7,31},{8,16},{9,... | collective-permute-start | bytes 110600 | tf_op jit(solution)/shard_map/ppermute | solution.py:342
  43.7 1.8 %collective-permute-start.19 = (f16[16,1152]{1,0:T(8,128)(2,1)S(1)}, f16[16,1152]{1,0:T(8,128)(2,1)S(1)}, u32[]{:S(2)}, u32[]{:S(2)}) collective-permute-start(f16[16,1152]{1,0:T(8,128)(2,1)S(1)} %get-tuple-element.65), channel_id=1, source_target_pairs={{0,8},{1,17},{2,10},{3,19},{4,12},{5,21},{6,14},{7,23},{8,0},{9,25... | collective-permute-start | bytes 110600 | tf_op jit(solution)/shard_map/ppermute | solution.py:342
  45.5 0.2 multiply_reduce_fusion.1
  45.7 0.1 fusion.25
  45.8 0.3 collective-permute-start.10
  46.2 2.4 %collective-permute-start.8 = (f16[16,1024]{1,0:T(8,128)(2,1)S(1)}, f16[16,1024]{1,0:T(8,128)(2,1)S(1)}, u32[]{:S(2)}, u32[]{:S(2)}) collective-permute-start(f16[16,1024]{1,0:T(8,128)(2,1)S(1)} %fusion.25), channel_id=1, source_target_pairs={{0,24},{1,25},{2,26},{3,27},{4,28},{5,29},{6,30},{7,31},{8,16},{9,... | collective-permute-start | bytes 98312 | tf_op jit(solution)/shard_map/ppermute | solution.py:342
  48.6 0.8 %collective-permute-start.9 = (f16[16,1024]{1,0:T(8,128)(2,1)S(1)}, f16[16,1024]{1,0:T(8,128)(2,1)S(1)}, u32[]{:S(2)}, u32[]{:S(2)}) collective-permute-start(f16[16,1024]{1,0:T(8,128)(2,1)S(1)} %fusion.25), channel_id=1, source_target_pairs={{0,16},{1,9},{2,18},{3,11},{4,20},{5,13},{6,22},{7,15},{8,24},{9,1... | collective-permute-start | bytes 98312 | tf_op jit(solution)/shard_map/ppermute | solution.py:342
  49.5 0.2 multiply_reduce_fusion
  49.6 0.1 fusion.21
  49.8 2.7 %collective-permute-start.20 = (f16[16,1024]{1,0:T(8,128)(2,1)S(1)}, f16[16,1024]{1,0:T(8,128)(2,1)S(1)}, u32[]{:S(2)}, u32[]{:S(2)}) collective-permute-start(f16[16,1024]{1,0:T(8,128)(2,1)S(1)} %fusion.21), channel_id=1, source_target_pairs={{0,24},{1,25},{2,26},{3,27},{4,28},{5,29},{6,30},{7,31},{8,16},{9,... | collective-permute-start | bytes 98312 | tf_op jit(solution)/shard_map/ppermute | solution.py:342
  52.4 0.0 collective-permute-start.21
  52.5 0.1 mul.311
  52.5 0.1 mul.281
  52.6 1.8 %collective-permute-start.22 = (f16[16,1024]{1,0:T(8,128)(2,1)S(1)}, f16[16,1024]{1,0:T(8,128)(2,1)S(1)}, u32[]{:S(2)}, u32[]{:S(2)}) collective-permute-start(f16[16,1024]{1,0:T(8,128)(2,1)S(1)} %fusion.21), channel_id=1, source_target_pairs={{0,8},{1,17},{2,10},{3,19},{4,12},{5,21},{6,14},{7,23},{8,0},{9,25... | collective-permute-start | bytes 98312 | tf_op jit(solution)/shard_map/ppermute | solution.py:342
  54.5 0.1 select_select_fusion.15
  54.6 2.6 %collective-permute-start.11 = (f16[64,1024]{1,0:T(8,128)(2,1)S(1)}, f16[64,1024]{1,0:T(8,128)(2,1)S(1)}, u32[]{:S(2)}, u32[]{:S(2)}) collective-permute-start(f16[64,1024]{1,0:T(8,128)(2,1)S(1)} %pad_maximum_fusion.2), channel_id=1, source_target_pairs={{0,6},{1,7},{2,4},{3,5},{4,2},{5,3},{6,0},{7,1},{8,14},{9,15},{10,... | collective-permute-start | bytes 393224 | tf_op jit(solution)/shard_map/ppermute | solution.py:342
  57.1 0.5 collective-permute-start.12
  57.6 0.5 collective-permute-start.13
  58.1 0.1 select_select_fusion.11
  58.2 2.6 %collective-permute-start.23 = (f16[64,1024]{1,0:T(8,128)(2,1)S(1)}, f16[64,1024]{1,0:T(8,128)(2,1)S(1)}, u32[]{:S(2)}, u32[]{:S(2)}) collective-permute-start(f16[64,1024]{1,0:T(8,128)(2,1)S(1)} %pad_maximum_fusion.3), channel_id=1, source_target_pairs={{0,6},{1,7},{2,4},{3,5},{4,2},{5,3},{6,0},{7,1},{8,14},{9,15},{10,... | collective-permute-start | bytes 393224 | tf_op jit(solution)/shard_map/ppermute | solution.py:342
  60.8 0.5 collective-permute-start.24
  61.3 0.6 collective-permute-done.11
  61.9 1.5 %collective-permute-start.25 = (f16[64,1024]{1,0:T(8,128)(2,1)S(1)}, f16[64,1024]{1,0:T(8,128)(2,1)S(1)}, u32[]{:S(2)}, u32[]{:S(2)}) collective-permute-start(f16[64,1024]{1,0:T(8,128)(2,1)S(1)} %pad_maximum_fusion.3), channel_id=1, source_target_pairs={{0,2},{1,5},{2,0},{3,7},{4,6},{5,1},{6,4},{7,3},{8,10},{9,13},{10,... | collective-permute-start | bytes 393224 | tf_op jit(solution)/shard_map/ppermute | solution.py:342
  63.4 0.7 collective-permute-done.12
  64.1 0.1 select_select_fusion.6
  64.2 0.1 select_select_fusion.7
  64.4 0.2 convert_multiply_fusion.1
  64.5 0.1 slice.171
  64.6 0.9 %collective-permute-done.23 = f16[64,1024]{1,0:T(8,128)(2,1)S(1)} collective-permute-done((f16[64,1024]{1,0:T(8,128)(2,1)S(1)}, f16[64,1024]{1,0:T(8,128)(2,1)S(1)}, u32[]{:S(2)}, u32[]{:S(2)}) %collective-permute-start.23) | collective-permute-done | bytes 131104 | tf_op jit(solution)/shard_map/ppermute | solution.py:342
  65.5 1.4 %collective-permute-done.24 = f16[64,1024]{1,0:T(8,128)(2,1)S(1)} collective-permute-done((f16[64,1024]{1,0:T(8,128)(2,1)S(1)}, f16[64,1024]{1,0:T(8,128)(2,1)S(1)}, u32[]{:S(2)}, u32[]{:S(2)}) %collective-permute-start.24) | collective-permute-done | bytes 131104 | tf_op jit(solution)/shard_map/ppermute | solution.py:342
  66.9 0.0 collective-permute-done.25
  66.9 0.1 select_select_fusion.2
  67.0 0.1 select_select_fusion.3
  67.2 0.2 convert_multiply_fusion
  67.3 1.5 %pad_maximum_fusion = f32[256,2048]{1,0:T(8,128)} fusion(f32[256,128]{1,0:T(8,128)S(1)} %get-tuple-element.53, f32[256,768]{1,0:T(8,128)S(1)} %slice.171, f32[256,1024]{1,0:T(8,128)S(1)} %convert_multiply_fusion, f32[256,128]{1,0:T(8,128)S(1)} %get-tuple-element.52), kind=kLoop, calls=%fused_computation | loop fusion | flops 1572864 | bytes 4194304 | tf_op jit(solution)/shard_map/concatenate | solution.py:424
  (40 shorter events, 0.5 us)
Async XLA Ops:
  2.4 2.0 %collective-permute-start = (bf16[3,256,128]{2,1,0:T(8,128)(2,1)S(1)}, bf16[3,256,128]{2,1,0:T(8,128)(2,1)S(1)}, u32[]{:S(2)}, u32[]{:S(2)}) collective-permute-start(bf16[3,256,128]{2,1,0:T(8,128)(2,1)S(1)} %pad_maximum_fusion.1), channel_id=1, source_target_pairs={{0,1},{1,0},{2,3},{3,2},{4,5},{5,4},{6,7},{7,6},{8,9},{9,8},{10,11... | collective-permute-start | bytes 589832 | tf_op jit(solution)/shard_map/ppermute | solution.py:302
  18.6 1.6 %collective-permute-start.1 = (f32[2,264,128]{2,1,0:T(8,128)S(1)}, f32[2,264,128]{2,1,0:T(8,128)S(1)}, u32[]{:S(2)}, u32[]{:S(2)}) collective-permute-start(f32[2,264,128]{2,1,0:T(8,128)S(1)} %broadcast_select_fusion), channel_id=1, source_target_pairs={{0,1},{1,0},{2,3},{3,2},{4,5},{5,4},{6,7},{7,6},{8,9},{9,8},{10,11... | collective-permute-start | bytes 811016 | tf_op jit(solution)/shard_map/ppermute | solution.py:302
  21.7 8.4 %collective-permute-start.2 = (f16[64,1152]{1,0:T(8,128)(2,1)S(1)}, f16[64,1152]{1,0:T(8,128)(2,1)S(1)}, u32[]{:S(2)}, u32[]{:S(2)}) collective-permute-start(f16[64,1152]{1,0:T(8,128)(2,1)S(1)} %get-tuple-element.49), channel_id=1, source_target_pairs={{0,6},{1,7},{2,4},{3,5},{4,2},{5,3},{6,0},{7,1},{8,14},{9,15},{10,... | collective-permute-start | bytes 442376 | tf_op jit(solution)/shard_map/ppermute | solution.py:342
  25.4 8.3 %collective-permute-start.3 = (f16[64,1152]{1,0:T(8,128)(2,1)S(1)}, f16[64,1152]{1,0:T(8,128)(2,1)S(1)}, u32[]{:S(2)}, u32[]{:S(2)}) collective-permute-start(f16[64,1152]{1,0:T(8,128)(2,1)S(1)} %get-tuple-element.51), channel_id=1, source_target_pairs={{0,4},{1,3},{2,6},{3,1},{4,0},{5,7},{6,2},{7,5},{8,12},{9,11},{10,... | collective-permute-start | bytes 442376 | tf_op jit(solution)/shard_map/ppermute | solution.py:342
  25.9 7.9 %collective-permute-start.4 = (f16[64,1152]{1,0:T(8,128)(2,1)S(1)}, f16[64,1152]{1,0:T(8,128)(2,1)S(1)}, u32[]{:S(2)}, u32[]{:S(2)}) collective-permute-start(f16[64,1152]{1,0:T(8,128)(2,1)S(1)} %get-tuple-element.50), channel_id=1, source_target_pairs={{0,2},{1,5},{2,0},{3,7},{4,6},{5,1},{6,4},{7,3},{8,10},{9,13},{10,... | collective-permute-start | bytes 442376 | tf_op jit(solution)/shard_map/ppermute | solution.py:342
  26.1 12.4 %collective-permute-start.14 = (f16[64,1152]{1,0:T(8,128)(2,1)S(1)}, f16[64,1152]{1,0:T(8,128)(2,1)S(1)}, u32[]{:S(2)}, u32[]{:S(2)}) collective-permute-start(f16[64,1152]{1,0:T(8,128)(2,1)S(1)} %get-tuple-element.46), channel_id=1, source_target_pairs={{0,6},{1,7},{2,4},{3,5},{4,2},{5,3},{6,0},{7,1},{8,14},{9,15},{10,... | collective-permute-start | bytes 442376 | tf_op jit(solution)/shard_map/ppermute | solution.py:342
  29.0 11.5 %collective-permute-start.15 = (f16[64,1152]{1,0:T(8,128)(2,1)S(1)}, f16[64,1152]{1,0:T(8,128)(2,1)S(1)}, u32[]{:S(2)}, u32[]{:S(2)}) collective-permute-start(f16[64,1152]{1,0:T(8,128)(2,1)S(1)} %get-tuple-element.48), channel_id=1, source_target_pairs={{0,4},{1,3},{2,6},{3,1},{4,0},{5,7},{6,2},{7,5},{8,12},{9,11},{10,... | collective-permute-start | bytes 442376 | tf_op jit(solution)/shard_map/ppermute | solution.py:342
  30.1 10.5 %collective-permute-start.16 = (f16[64,1152]{1,0:T(8,128)(2,1)S(1)}, f16[64,1152]{1,0:T(8,128)(2,1)S(1)}, u32[]{:S(2)}, u32[]{:S(2)}) collective-permute-start(f16[64,1152]{1,0:T(8,128)(2,1)S(1)} %get-tuple-element.47), channel_id=1, source_target_pairs={{0,2},{1,5},{2,0},{3,7},{4,6},{5,1},{6,4},{7,3},{8,10},{9,13},{10,... | collective-permute-start | bytes 442376 | tf_op jit(solution)/shard_map/ppermute | solution.py:342
  34.2 9.5 %collective-permute-start.6 = (f16[16,1152]{1,0:T(8,128)(2,1)S(1)}, f16[16,1152]{1,0:T(8,128)(2,1)S(1)}, u32[]{:S(2)}, u32[]{:S(2)}) collective-permute-start(f16[16,1152]{1,0:T(8,128)(2,1)S(1)} %get-tuple-element.68), channel_id=1, source_target_pairs={{0,16},{1,9},{2,18},{3,11},{4,20},{5,13},{6,22},{7,15},{8,24},{9,1... | collective-permute-start | bytes 110600 | tf_op jit(solution)/shard_map/ppermute | solution.py:342
  36.9 8.6 %collective-permute-start.7 = (f16[16,1152]{1,0:T(8,128)(2,1)S(1)}, f16[16,1152]{1,0:T(8,128)(2,1)S(1)}, u32[]{:S(2)}, u32[]{:S(2)}) collective-permute-start(f16[16,1152]{1,0:T(8,128)(2,1)S(1)} %get-tuple-element.69), channel_id=1, source_target_pairs={{0,8},{1,17},{2,10},{3,19},{4,12},{5,21},{6,14},{7,23},{8,0},{9,25... | collective-permute-start | bytes 110600 | tf_op jit(solution)/shard_map/ppermute | solution.py:342
  38.5 7.0 %collective-permute-start.5 = (f16[16,1152]{1,0:T(8,128)(2,1)S(1)}, f16[16,1152]{1,0:T(8,128)(2,1)S(1)}, u32[]{:S(2)}, u32[]{:S(2)}) collective-permute-start(f16[16,1152]{1,0:T(8,128)(2,1)S(1)} %get-tuple-element.67), channel_id=1, source_target_pairs={{0,24},{1,25},{2,26},{3,27},{4,28},{5,29},{6,30},{7,31},{8,16},{9,... | collective-permute-start | bytes 110600 | tf_op jit(solution)/shard_map/ppermute | solution.py:342
  41.0 7.6 %collective-permute-start.17 = (f16[16,1152]{1,0:T(8,128)(2,1)S(1)}, f16[16,1152]{1,0:T(8,128)(2,1)S(1)}, u32[]{:S(2)}, u32[]{:S(2)}) collective-permute-start(f16[16,1152]{1,0:T(8,128)(2,1)S(1)} %get-tuple-element.63), channel_id=1, source_target_pairs={{0,24},{1,25},{2,26},{3,27},{4,28},{5,29},{6,30},{7,31},{8,16},{9,... | collective-permute-start | bytes 110600 | tf_op jit(solution)/shard_map/ppermute | solution.py:342
  43.7 5.7 %collective-permute-start.18 = (f16[16,1152]{1,0:T(8,128)(2,1)S(1)}, f16[16,1152]{1,0:T(8,128)(2,1)S(1)}, u32[]{:S(2)}, u32[]{:S(2)}) collective-permute-start(f16[16,1152]{1,0:T(8,128)(2,1)S(1)} %get-tuple-element.64), channel_id=1, source_target_pairs={{0,16},{1,9},{2,18},{3,11},{4,20},{5,13},{6,22},{7,15},{8,24},{9,1... | collective-permute-start | bytes 110600 | tf_op jit(solution)/shard_map/ppermute | solution.py:342
  43.7 5.7 %collective-permute-start.19 = (f16[16,1152]{1,0:T(8,128)(2,1)S(1)}, f16[16,1152]{1,0:T(8,128)(2,1)S(1)}, u32[]{:S(2)}, u32[]{:S(2)}) collective-permute-start(f16[16,1152]{1,0:T(8,128)(2,1)S(1)} %get-tuple-element.65), channel_id=1, source_target_pairs={{0,8},{1,17},{2,10},{3,19},{4,12},{5,21},{6,14},{7,23},{8,0},{9,25... | collective-permute-start | bytes 110600 | tf_op jit(solution)/shard_map/ppermute | solution.py:342
  45.8 6.8 %collective-permute-start.10 = (f16[16,1024]{1,0:T(8,128)(2,1)S(1)}, f16[16,1024]{1,0:T(8,128)(2,1)S(1)}, u32[]{:S(2)}, u32[]{:S(2)}) collective-permute-start(f16[16,1024]{1,0:T(8,128)(2,1)S(1)} %fusion.25), channel_id=1, source_target_pairs={{0,8},{1,17},{2,10},{3,19},{4,12},{5,21},{6,14},{7,23},{8,0},{9,25... | collective-permute-start | bytes 98312 | tf_op jit(solution)/shard_map/ppermute | solution.py:342
  46.2 8.3 %collective-permute-start.8 = (f16[16,1024]{1,0:T(8,128)(2,1)S(1)}, f16[16,1024]{1,0:T(8,128)(2,1)S(1)}, u32[]{:S(2)}, u32[]{:S(2)}) collective-permute-start(f16[16,1024]{1,0:T(8,128)(2,1)S(1)} %fusion.25), channel_id=1, source_target_pairs={{0,24},{1,25},{2,26},{3,27},{4,28},{5,29},{6,30},{7,31},{8,16},{9,... | collective-permute-start | bytes 98312 | tf_op jit(solution)/shard_map/ppermute | solution.py:342
  48.6 5.8 %collective-permute-start.9 = (f16[16,1024]{1,0:T(8,128)(2,1)S(1)}, f16[16,1024]{1,0:T(8,128)(2,1)S(1)}, u32[]{:S(2)}, u32[]{:S(2)}) collective-permute-start(f16[16,1024]{1,0:T(8,128)(2,1)S(1)} %fusion.25), channel_id=1, source_target_pairs={{0,16},{1,9},{2,18},{3,11},{4,20},{5,13},{6,22},{7,15},{8,24},{9,1... | collective-permute-start | bytes 98312 | tf_op jit(solution)/shard_map/ppermute | solution.py:342
  49.8 7.8 %collective-permute-start.20 = (f16[16,1024]{1,0:T(8,128)(2,1)S(1)}, f16[16,1024]{1,0:T(8,128)(2,1)S(1)}, u32[]{:S(2)}, u32[]{:S(2)}) collective-permute-start(f16[16,1024]{1,0:T(8,128)(2,1)S(1)} %fusion.21), channel_id=1, source_target_pairs={{0,24},{1,25},{2,26},{3,27},{4,28},{5,29},{6,30},{7,31},{8,16},{9,... | collective-permute-start | bytes 98312 | tf_op jit(solution)/shard_map/ppermute | solution.py:342
  52.4 5.7 %collective-permute-start.21 = (f16[16,1024]{1,0:T(8,128)(2,1)S(1)}, f16[16,1024]{1,0:T(8,128)(2,1)S(1)}, u32[]{:S(2)}, u32[]{:S(2)}) collective-permute-start(f16[16,1024]{1,0:T(8,128)(2,1)S(1)} %fusion.21), channel_id=1, source_target_pairs={{0,16},{1,9},{2,18},{3,11},{4,20},{5,13},{6,22},{7,15},{8,24},{9,1... | collective-permute-start | bytes 98312 | tf_op jit(solution)/shard_map/ppermute | solution.py:342
  52.6 5.5 %collective-permute-start.22 = (f16[16,1024]{1,0:T(8,128)(2,1)S(1)}, f16[16,1024]{1,0:T(8,128)(2,1)S(1)}, u32[]{:S(2)}, u32[]{:S(2)}) collective-permute-start(f16[16,1024]{1,0:T(8,128)(2,1)S(1)} %fusion.21), channel_id=1, source_target_pairs={{0,8},{1,17},{2,10},{3,19},{4,12},{5,21},{6,14},{7,23},{8,0},{9,25... | collective-permute-start | bytes 98312 | tf_op jit(solution)/shard_map/ppermute | solution.py:342
  54.6 7.3 %collective-permute-start.11 = (f16[64,1024]{1,0:T(8,128)(2,1)S(1)}, f16[64,1024]{1,0:T(8,128)(2,1)S(1)}, u32[]{:S(2)}, u32[]{:S(2)}) collective-permute-start(f16[64,1024]{1,0:T(8,128)(2,1)S(1)} %pad_maximum_fusion.2), channel_id=1, source_target_pairs={{0,6},{1,7},{2,4},{3,5},{4,2},{5,3},{6,0},{7,1},{8,14},{9,15},{10,... | collective-permute-start | bytes 393224 | tf_op jit(solution)/shard_map/ppermute | solution.py:342
  57.1 6.9 %collective-permute-start.12 = (f16[64,1024]{1,0:T(8,128)(2,1)S(1)}, f16[64,1024]{1,0:T(8,128)(2,1)S(1)}, u32[]{:S(2)}, u32[]{:S(2)}) collective-permute-start(f16[64,1024]{1,0:T(8,128)(2,1)S(1)} %pad_maximum_fusion.2), channel_id=1, source_target_pairs={{0,4},{1,3},{2,6},{3,1},{4,0},{5,7},{6,2},{7,5},{8,12},{9,11},{10,... | collective-permute-start | bytes 393224 | tf_op jit(solution)/shard_map/ppermute | solution.py:342
  57.6 6.5 %collective-permute-start.13 = (f16[64,1024]{1,0:T(8,128)(2,1)S(1)}, f16[64,1024]{1,0:T(8,128)(2,1)S(1)}, u32[]{:S(2)}, u32[]{:S(2)}) collective-permute-start(f16[64,1024]{1,0:T(8,128)(2,1)S(1)} %pad_maximum_fusion.2), channel_id=1, source_target_pairs={{0,2},{1,5},{2,0},{3,7},{4,6},{5,1},{6,4},{7,3},{8,10},{9,13},{10,... | collective-permute-start | bytes 393224 | tf_op jit(solution)/shard_map/ppermute | solution.py:342
  58.2 7.3 %collective-permute-start.23 = (f16[64,1024]{1,0:T(8,128)(2,1)S(1)}, f16[64,1024]{1,0:T(8,128)(2,1)S(1)}, u32[]{:S(2)}, u32[]{:S(2)}) collective-permute-start(f16[64,1024]{1,0:T(8,128)(2,1)S(1)} %pad_maximum_fusion.3), channel_id=1, source_target_pairs={{0,6},{1,7},{2,4},{3,5},{4,2},{5,3},{6,0},{7,1},{8,14},{9,15},{10,... | collective-permute-start | bytes 393224 | tf_op jit(solution)/shard_map/ppermute | solution.py:342
  60.8 6.1 %collective-permute-start.24 = (f16[64,1024]{1,0:T(8,128)(2,1)S(1)}, f16[64,1024]{1,0:T(8,128)(2,1)S(1)}, u32[]{:S(2)}, u32[]{:S(2)}) collective-permute-start(f16[64,1024]{1,0:T(8,128)(2,1)S(1)} %pad_maximum_fusion.3), channel_id=1, source_target_pairs={{0,4},{1,3},{2,6},{3,1},{4,0},{5,7},{6,2},{7,5},{8,12},{9,11},{10,... | collective-permute-start | bytes 393224 | tf_op jit(solution)/shard_map/ppermute | solution.py:342
  61.9 5.0 %collective-permute-start.25 = (f16[64,1024]{1,0:T(8,128)(2,1)S(1)}, f16[64,1024]{1,0:T(8,128)(2,1)S(1)}, u32[]{:S(2)}, u32[]{:S(2)}) collective-permute-start(f16[64,1024]{1,0:T(8,128)(2,1)S(1)} %pad_maximum_fusion.3), channel_id=1, source_target_pairs={{0,2},{1,5},{2,0},{3,7},{4,6},{5,1},{6,4},{7,3},{8,10},{9,13},{10,... | collective-permute-start | bytes 393224 | tf_op jit(solution)/shard_map/ppermute | solution.py:342

commit v5 on v4

--- a/solution.py
+++ b/solution.py
@@ -298,6 +298,36 @@
     )(meta, low_edge, high_edge, edge_hits, from_low, from_high, rest, aligned)
 
 
+def facing_kernel(start_ref, data_ref, tmpl_ref, out_ref, sems):
+    n_subjects = data_ref.shape[0]
+    k = out_ref.shape[2]
+    lanes = pl.ds(pl.multiple_of(start_ref[0], k), k)
+    copies = [pltpu.make_async_copy(tmpl_ref.at[:, lanes], out_ref.at[n_subjects], sems.at[n_subjects])]
+    for i in range(n_subjects):
+        copies.append(pltpu.make_async_copy(data_ref.at[i, :, lanes], out_ref.at[i], sems.at[i]))
+    for copy in copies:
+        copy.start()
+    for copy in copies:
+        copy.wait()
+
+
+def facing_columns(data, template, start, k):
+    n_subjects, frames, _ = data.shape
+    vmem = pl.BlockSpec(memory_space=pltpu.VMEM)
+    hbm = pl.BlockSpec(memory_space=pl.ANY)
+    smem = pl.BlockSpec(memory_space=pltpu.SMEM)
+    return pl.pallas_call(
+        facing_kernel,
+        out_shape=jax.ShapeDtypeStruct((n_subjects + 1, frames, k), BF16),
+        in_specs=[smem, hbm, hbm],
+        out_specs=vmem,
+        scratch_shapes=[pltpu.SemaphoreType.DMA((n_subjects + 1,))],
+        compiler_params=pltpu.CompilerParams(vmem_limit_bytes=4 * 1024 * 1024),
+        cost_estimate=pl.CostEstimate(flops=0, bytes_accessed=800_000, transcendentals=0),
+        name="facing",
+    )(start, pltpu.with_memory_space_constraint(data, pltpu.HBM), pltpu.with_memory_space_constraint(template, pltpu.HBM))
+
+
 def core_swap(value):
     return lax.ppermute(value, "vert", [(0, 1), (1, 0)])
 
@@ -388,12 +418,8 @@
     verts = lax.axis_size("vert")
     meta = jnp.stack([v > 0, v < verts - 1]).astype(jnp.int32)
     if verts == 2:
-        start = jnp.where(v == 0, own - k, 0)
-        facing = (
-            lax.dynamic_slice_in_dim(data, start, k, 2),
-            lax.dynamic_slice_in_dim(template, start, k, 1)[None],
-        )
-        low = high = core_swap(jnp.concatenate(facing, axis=0))
+        start = jnp.where(v == 0, own - k, 0).astype(jnp.int32).reshape(1)
+        low = high = core_swap(facing_columns(data, template, start, k))
     else:
         first_edge = jnp.concatenate([data[:, :, :k], template[None, :, :k]], axis=0)
         last_edge = jnp.concatenate([data[:, :, own - k :], template[None, :, own - k :]], axis=0)

time: 69.1 us -> 68.1 us (0.986)
  local copies, waits for them, and re-layouts: 2.15 us -> 0.39 us
  other arithmetic: 5.68 us -> 4.31 us
  Pallas kernels: 15.6 us -> 16.5 us
    pallas_call x0 -> x1, Pallas kernels: none -> 0.94 us  [facing_columns(): pl.pallas_call(facing_kernel, out_shape=jax.ShapeDtypeStruct((n_subjects...]
    dynamic_slice x1 -> x0, local copies, waits for them, and re-layouts: 0.92 us -> none  [local(): lax.dynamic_slice_in_dim(data, start, k, 2)]
    broadcast_in_dim x1 -> x0, local copies, waits for them, and re-layouts: 0.85 us -> none  [local(): lax.dynamic_slice_in_dim(template, start, k, 1)[None]]
    ppermute x2, waiting for transfers between devices: 1.42 us -> 2.17 us  [core_swap(): return lax.ppermute(value, 'vert', [(0, 1), (1, 0)])]
    add x1, other arithmetic: 0.7 us -> 0.01 us  [local(): neighbours + k]
  transfers between devices with their start and end apart: 26 -> 26, of which waited for: 7 -> 9; matrix products, arithmetic and copies ran while one was open for 6% -> 4% of each run, Pallas kernels for 0% -> 0%
where the time goes in v5:
time: 68.1 us; the launch traced here: 67.9 us
  starting transfers between devices  37.7 us (55%)
  Pallas kernels  16.5 us (24%)
  waiting for transfers between devices  8.02 us (12%)
  other arithmetic  4.31 us (6%)
  between operations  0.96 us (1%)
    ppermute x24, starting transfers between devices, swap(): return lax.ppermute(value, ('subj', 'vert'), self.pairs(phase, m))  36.8 us
    pallas_call x1, Pallas kernels, align(): pl.pallas_call(functools.partial(align_kernel, n_subjects, n_centres, gro...  14.2 us
    ppermute x24, waiting for transfers between devices, swap(): return lax.ppermute(value, ('subj', 'vert'), self.pairs(phase, m))  5.86 us
    ppermute x2, waiting for transfers between devices, core_swap(): return lax.ppermute(value, 'vert', [(0, 1), (1, 0)])  2.17 us
    concatenate x1, other arithmetic, local(): jnp.concatenate([end[:, inner:inner + k], begin, end[:, :inner], end[:, i...  1.5 us
    pallas_call x1, Pallas kernels, finish_edges(): pl.pallas_call(functools.partial(edges_kernel, n_subjects), out_shape=(ja...  1.36 us
  transfers between devices with their start and end apart: 26, of which 9 were waited for; matrix products, arithmetic and copies ran while one was open for 4% of the time, Pallas kernels for 0%

profile of v5, /device:TPU:0, one launch (start us, length us, event | category | flops | bytes accessed | tf_op | source)
XLA Modules:
  0.0 67.9 jit_solution(6604037254743128336)
XLA Ops:
  0.7 0.9 %facing.1 = bf16[3,256,128]{2,1,0:T(8,128)(2,1)S(1)} custom-call(s32[1]{0:T(128)} %bitcast.2.start_ref, bf16[2,256,2048]{2,1,0:T(8,128)(2,1)} %data_ref.3, bf16[256,2048]{1,0:T(8,128)(2,1)} %tmpl_ref.3), custom_call_target="tpu_custom_call" | custom-call | bytes 800000 | tf_op jit(solution)/shard_map/facing/pallas_call | solution.py:319
  1.6 0.5 collective-permute-start
  2.1 0.1 add_convert_fusion.meta_ref
  2.2 1.0 %collective-permute-done.low_ref.high_ref = bf16[3,256,128]{2,1,0:T(8,128)(2,1)S(1)} collective-permute-done((bf16[3,256,128]{2,1,0:T(8,128)(2,1)S(1)}, bf16[3,256,128]{2,1,0:T(8,128)(2,1)S(1)}, u32[]{:S(2)}, u32[]{:S(2)}) %collective-permute-start) | collective-permute-done | bytes 196640 | tf_op jit(solution)/shard_map/ppermute | solution.py:332
  3.2 14.2 %align.1 = (bf16[2,256,2048]{2,1,0:T(8,128)(2,1)}, f32[256,1152]{1,0:T(8,128)S(1)}, f32[256,768]{1,0:T(8,128)S(1)}, f32[2,264,128]{2,1,0:T(8,128)S(1)}, f32[2,26...) custom-call(s32[2]{0:T(128)S(1)} %add_convert_fusion.meta_ref, ...), custom_call_target="tpu_custom_call" | custom-call | flops 16000000000 | bytes 8000000 | tf_op jit(solution)/shard_map/align/pallas_call | solution.py:214
  17.5 0.4 collective-permute-start.1
  17.9 1.2 %collective-permute-done.1.low_ref.high_ref = f32[2,264,128]{2,1,0:T(8,128)S(1)} collective-permute-done((f32[2,264,128]{2,1,0:T(8,128)S(1)}, f32[2,264,128]{2,1,0:T(8,128)S(1)}, u32[]{:S(2)}, u32[]{:S(2)}) %collective-permute-start.1) | collective-permute-done | bytes 270368 | tf_op jit(solution)/shard_map/ppermute | solution.py:332
  19.1 1.4 %edges.1 = (bf16[2,256,2048]{2,1,0:T(8,128)(2,1)}, f32[256,1152]{1,0:T(8,128)S(1)}) custom-call(s32[2]{0:T(128)S(1)} %add_convert_fusion.meta_ref, f32[2,256,128]{2,1,0:T(8,128)S(1)} %get-tuple-element.14.low_edge, f32[2,256,128]{2,1,0:T(8,128)S(1)} %get-tuple-element.15.high_edge, ...), custom_call_target="tpu_custom_call", output_to_operand_aliasing={{0}: (7, {})} | custom-call | flops 1000000000 | bytes 2000000 | tf_op jit(solution)/shard_map/edges/pallas_call | solution.py:281
  20.5 0.1 dynamic-slice_convert_fusion.5
  20.5 3.9 %collective-permute-start.2 = (f16[64,1152]{1,0:T(8,128)(2,1)S(1)}, f16[64,1152]{1,0:T(8,128)(2,1)S(1)}, u32[]{:S(2)}, u32[]{:S(2)}) collective-permute-start(f16[64,1152]{1,0:T(8,128)(2,1)S(1)} %get-tuple-element.49), channel_id=1, source_target_pairs={{0,6},{1,7},{2,4},{3,5},{4,2},{5,3},{6,0},{7,1},{8,14},{9,15},{10,... | collective-permute-start | bytes 442376 | tf_op jit(solution)/shard_map/ppermute | solution.py:372
  24.4 0.5 collective-permute-start.3
  24.9 0.1 collective-permute-start.4
  25.1 2.9 %collective-permute-start.14 = (f16[64,1152]{1,0:T(8,128)(2,1)S(1)}, f16[64,1152]{1,0:T(8,128)(2,1)S(1)}, u32[]{:S(2)}, u32[]{:S(2)}) collective-permute-start(f16[64,1152]{1,0:T(8,128)(2,1)S(1)} %get-tuple-element.46), channel_id=1, source_target_pairs={{0,6},{1,7},{2,4},{3,5},{4,2},{5,3},{6,0},{7,1},{8,14},{9,15},{10,... | collective-permute-start | bytes 442376 | tf_op jit(solution)/shard_map/ppermute | solution.py:372
  28.0 0.5 collective-permute-start.15
  28.5 0.5 collective-permute-done.2
  29.0 2.0 %collective-permute-start.16 = (f16[64,1152]{1,0:T(8,128)(2,1)S(1)}, f16[64,1152]{1,0:T(8,128)(2,1)S(1)}, u32[]{:S(2)}, u32[]{:S(2)}) collective-permute-start(f16[64,1152]{1,0:T(8,128)(2,1)S(1)} %get-tuple-element.47), channel_id=1, source_target_pairs={{0,2},{1,5},{2,0},{3,7},{4,6},{5,1},{6,4},{7,3},{8,10},{9,13},{10,... | collective-permute-start | bytes 442376 | tf_op jit(solution)/shard_map/ppermute | solution.py:372
  31.1 1.7 %collective-permute-done.3 = f16[64,1152]{1,0:T(8,128)(2,1)S(1)} collective-permute-done((f16[64,1152]{1,0:T(8,128)(2,1)S(1)}, f16[64,1152]{1,0:T(8,128)(2,1)S(1)}, u32[]{:S(2)}, u32[]{:S(2)}) %collective-permute-start.3) | collective-permute-done | bytes 147488 | tf_op jit(solution)/shard_map/ppermute | solution.py:372
  32.8 0.0 collective-permute-done.4
  32.8 0.2 fusion.29
  33.0 0.1 fusion.3
  33.2 0.1 broadcast_in_dim.9
  33.3 2.7 %collective-permute-start.6 = (f16[16,1152]{1,0:T(8,128)(2,1)S(1)}, f16[16,1152]{1,0:T(8,128)(2,1)S(1)}, u32[]{:S(2)}, u32[]{:S(2)}) collective-permute-start(f16[16,1152]{1,0:T(8,128)(2,1)S(1)} %get-tuple-element.68), channel_id=1, source_target_pairs={{0,16},{1,9},{2,18},{3,11},{4,20},{5,13},{6,22},{7,15},{8,24},{9,1... | collective-permute-start | bytes 110600 | tf_op jit(solution)/shard_map/ppermute | solution.py:372
  36.0 1.6 %collective-permute-start.7 = (f16[16,1152]{1,0:T(8,128)(2,1)S(1)}, f16[16,1152]{1,0:T(8,128)(2,1)S(1)}, u32[]{:S(2)}, u32[]{:S(2)}) collective-permute-start(f16[16,1152]{1,0:T(8,128)(2,1)S(1)} %get-tuple-element.69), channel_id=1, source_target_pairs={{0,8},{1,17},{2,10},{3,19},{4,12},{5,21},{6,14},{7,23},{8,0},{9,25... | collective-permute-start | bytes 110600 | tf_op jit(solution)/shard_map/ppermute | solution.py:372
  37.6 2.0 %collective-permute-start.5 = (f16[16,1152]{1,0:T(8,128)(2,1)S(1)}, f16[16,1152]{1,0:T(8,128)(2,1)S(1)}, u32[]{:S(2)}, u32[]{:S(2)}) collective-permute-start(f16[16,1152]{1,0:T(8,128)(2,1)S(1)} %get-tuple-element.67), channel_id=1, source_target_pairs={{0,24},{1,25},{2,26},{3,27},{4,28},{5,29},{6,30},{7,31},{8,16},{9,... | collective-permute-start | bytes 110600 | tf_op jit(solution)/shard_map/ppermute | solution.py:372
  39.5 0.0 collective-permute-done.15
  39.6 0.2 fusion.28
  39.8 0.2 fusion
  40.0 0.1 broadcast_in_dim.11
  40.1 2.4 %collective-permute-start.17 = (f16[16,1152]{1,0:T(8,128)(2,1)S(1)}, f16[16,1152]{1,0:T(8,128)(2,1)S(1)}, u32[]{:S(2)}, u32[]{:S(2)}) collective-permute-start(f16[16,1152]{1,0:T(8,128)(2,1)S(1)} %get-tuple-element.63), channel_id=1, source_target_pairs={{0,24},{1,25},{2,26},{3,27},{4,28},{5,29},{6,30},{7,31},{8,16},{9,... | collective-permute-start | bytes 110600 | tf_op jit(solution)/shard_map/ppermute | solution.py:372
  42.5 0.0 collective-permute-start.18
  42.5 2.0 %collective-permute-start.19 = (f16[16,1152]{1,0:T(8,128)(2,1)S(1)}, f16[16,1152]{1,0:T(8,128)(2,1)S(1)}, u32[]{:S(2)}, u32[]{:S(2)}) collective-permute-start(f16[16,1152]{1,0:T(8,128)(2,1)S(1)} %get-tuple-element.65), channel_id=1, source_target_pairs={{0,8},{1,17},{2,10},{3,19},{4,12},{5,21},{6,14},{7,23},{8,0},{9,25... | collective-permute-start | bytes 110600 | tf_op jit(solution)/shard_map/ppermute | solution.py:372
  44.6 0.2 multiply_reduce_fusion.1
  44.8 0.1 fusion.25
  44.9 0.1 collective-permute-start.10
  45.0 2.4 %collective-permute-start.8 = (f16[16,1024]{1,0:T(8,128)(2,1)S(1)}, f16[16,1024]{1,0:T(8,128)(2,1)S(1)}, u32[]{:S(2)}, u32[]{:S(2)}) collective-permute-start(f16[16,1024]{1,0:T(8,128)(2,1)S(1)} %fusion.25), channel_id=1, source_target_pairs={{0,24},{1,25},{2,26},{3,27},{4,28},{5,29},{6,30},{7,31},{8,16},{9,... | collective-permute-start | bytes 98312 | tf_op jit(solution)/shard_map/ppermute | solution.py:372
  47.4 1.0 %collective-permute-start.9 = (f16[16,1024]{1,0:T(8,128)(2,1)S(1)}, f16[16,1024]{1,0:T(8,128)(2,1)S(1)}, u32[]{:S(2)}, u32[]{:S(2)}) collective-permute-start(f16[16,1024]{1,0:T(8,128)(2,1)S(1)} %fusion.25), channel_id=1, source_target_pairs={{0,16},{1,9},{2,18},{3,11},{4,20},{5,13},{6,22},{7,15},{8,24},{9,1... | collective-permute-start | bytes 98312 | tf_op jit(solution)/shard_map/ppermute | solution.py:372
  48.5 0.2 multiply_reduce_fusion
  48.7 0.1 fusion.21
  48.8 2.4 %collective-permute-start.20 = (f16[16,1024]{1,0:T(8,128)(2,1)S(1)}, f16[16,1024]{1,0:T(8,128)(2,1)S(1)}, u32[]{:S(2)}, u32[]{:S(2)}) collective-permute-start(f16[16,1024]{1,0:T(8,128)(2,1)S(1)} %fusion.21), channel_id=1, source_target_pairs={{0,24},{1,25},{2,26},{3,27},{4,28},{5,29},{6,30},{7,31},{8,16},{9,... | collective-permute-start | bytes 98312 | tf_op jit(solution)/shard_map/ppermute | solution.py:372
  51.3 0.1 collective-permute-start.21
  51.3 0.1 mul.311
  51.4 0.1 mul.281
  51.5 2.0 %collective-permute-start.22 = (f16[16,1024]{1,0:T(8,128)(2,1)S(1)}, f16[16,1024]{1,0:T(8,128)(2,1)S(1)}, u32[]{:S(2)}, u32[]{:S(2)}) collective-permute-start(f16[16,1024]{1,0:T(8,128)(2,1)S(1)} %fusion.21), channel_id=1, source_target_pairs={{0,8},{1,17},{2,10},{3,19},{4,12},{5,21},{6,14},{7,23},{8,0},{9,25... | collective-permute-start | bytes 98312 | tf_op jit(solution)/shard_map/ppermute | solution.py:372
  53.5 0.1 select_select_fusion.15
  53.6 2.6 %collective-permute-start.11 = (f16[64,1024]{1,0:T(8,128)(2,1)S(1)}, f16[64,1024]{1,0:T(8,128)(2,1)S(1)}, u32[]{:S(2)}, u32[]{:S(2)}) collective-permute-start(f16[64,1024]{1,0:T(8,128)(2,1)S(1)} %pad_maximum_fusion.1), channel_id=1, source_target_pairs={{0,6},{1,7},{2,4},{3,5},{4,2},{5,3},{6,0},{7,1},{8,14},{9,15},{10,... | collective-permute-start | bytes 393224 | tf_op jit(solution)/shard_map/ppermute | solution.py:372
  56.2 0.5 collective-permute-start.12
  56.7 0.5 collective-permute-start.13
  57.2 0.1 select_select_fusion.11
  57.3 2.6 %collective-permute-start.23 = (f16[64,1024]{1,0:T(8,128)(2,1)S(1)}, f16[64,1024]{1,0:T(8,128)(2,1)S(1)}, u32[]{:S(2)}, u32[]{:S(2)}) collective-permute-start(f16[64,1024]{1,0:T(8,128)(2,1)S(1)} %pad_maximum_fusion.2), channel_id=1, source_target_pairs={{0,6},{1,7},{2,4},{3,5},{4,2},{5,3},{6,0},{7,1},{8,14},{9,15},{10,... | collective-permute-start | bytes 393224 | tf_op jit(solution)/shard_map/ppermute | solution.py:372
  59.9 0.5 collective-permute-start.24
  60.3 0.7 collective-permute-done.11
  61.0 1.5 %collective-permute-start.25 = (f16[64,1024]{1,0:T(8,128)(2,1)S(1)}, f16[64,1024]{1,0:T(8,128)(2,1)S(1)}, u32[]{:S(2)}, u32[]{:S(2)}) collective-permute-start(f16[64,1024]{1,0:T(8,128)(2,1)S(1)} %pad_maximum_fusion.2), channel_id=1, source_target_pairs={{0,2},{1,5},{2,0},{3,7},{4,6},{5,1},{6,4},{7,3},{8,10},{9,13},{10,... | collective-permute-start | bytes 393224 | tf_op jit(solution)/shard_map/ppermute | solution.py:372
  62.5 0.6 collective-permute-done.12
  63.1 0.1 select_select_fusion.6
  63.2 0.1 select_select_fusion.7
  63.3 0.2 convert_multiply_fusion.1
  63.5 0.1 slice.171
  63.6 0.9 %collective-permute-done.23 = f16[64,1024]{1,0:T(8,128)(2,1)S(1)} collective-permute-done((f16[64,1024]{1,0:T(8,128)(2,1)S(1)}, f16[64,1024]{1,0:T(8,128)(2,1)S(1)}, u32[]{:S(2)}, u32[]{:S(2)}) %collective-permute-start.23) | collective-permute-done | bytes 131104 | tf_op jit(solution)/shard_map/ppermute | solution.py:372
  64.5 1.4 %collective-permute-done.24 = f16[64,1024]{1,0:T(8,128)(2,1)S(1)} collective-permute-done((f16[64,1024]{1,0:T(8,128)(2,1)S(1)}, f16[64,1024]{1,0:T(8,128)(2,1)S(1)}, u32[]{:S(2)}, u32[]{:S(2)}) %collective-permute-start.24) | collective-permute-done | bytes 131104 | tf_op jit(solution)/shard_map/ppermute | solution.py:372
  65.9 0.1 collective-permute-done.25
  66.0 0.1 select_select_fusion.2
  66.1 0.1 select_select_fusion.3
  66.2 0.2 convert_multiply_fusion
  66.4 1.5 %pad_maximum_fusion = f32[256,2048]{1,0:T(8,128)} fusion(f32[256,128]{1,0:T(8,128)S(1)} %get-tuple-element.53, f32[256,768]{1,0:T(8,128)S(1)} %slice.171, f32[256,1024]{1,0:T(8,128)S(1)} %convert_multiply_fusion, f32[256,128]{1,0:T(8,128)S(1)} %get-tuple-element.52), kind=kLoop, calls=%fused_computation | loop fusion | flops 1572864 | bytes 4194304 | tf_op jit(solution)/shard_map/concatenate | solution.py:450
  (42 shorter events, 0.5 us)
Async XLA Ops:
  0.6 1.5 %copy-start = (s32[16,128]{1,0:T(8,128)S(1)}, s32[16,128]{1,0:T(8,128)}, u32[]{:S(2)}) copy-start(s32[16,128]{1,0:T(8,128)} %param.7) | copy-start | bytes 24580
  0.6 1.6 %copy-start.1 = (s32[16]{0:T(128)S(1)}, s32[16]{0:T(128)}, u32[]{:S(2)}) copy-start(s32[16]{0:T(128)} %param.6) | copy-start | bytes 196
  1.6 1.6 %collective-permute-start = (bf16[3,256,128]{2,1,0:T(8,128)(2,1)S(1)}, bf16[3,256,128]{2,1,0:T(8,128)(2,1)S(1)}, u32[]{:S(2)}, u32[]{:S(2)}) collective-permute-start(bf16[3,256,128]{2,1,0:T(8,128)(2,1)S(1)} %facing.1), channel_id=1, source_target_pairs={{0,1},{1,0},{2,3},{3,2},{4,5},{5,4},{6,7},{7,6},{8,9},{9,8},{10,11... | collective-permute-start | bytes 589832 | tf_op jit(solution)/shard_map/ppermute | solution.py:332
  17.5 1.6 %collective-permute-start.1 = (f32[2,264,128]{2,1,0:T(8,128)S(1)}, f32[2,264,128]{2,1,0:T(8,128)S(1)}, u32[]{:S(2)}, u32[]{:S(2)}) collective-permute-start(f32[2,264,128]{2,1,0:T(8,128)S(1)} %broadcast_select_fusion), channel_id=1, source_target_pairs={{0,1},{1,0},{2,3},{3,2},{4,5},{5,4},{6,7},{7,6},{8,9},{9,8},{10,11... | collective-permute-start | bytes 811016 | tf_op jit(solution)/shard_map/ppermute | solution.py:332
  20.5 8.5 %collective-permute-start.2 = (f16[64,1152]{1,0:T(8,128)(2,1)S(1)}, f16[64,1152]{1,0:T(8,128)(2,1)S(1)}, u32[]{:S(2)}, u32[]{:S(2)}) collective-permute-start(f16[64,1152]{1,0:T(8,128)(2,1)S(1)} %get-tuple-element.49), channel_id=1, source_target_pairs={{0,6},{1,7},{2,4},{3,5},{4,2},{5,3},{6,0},{7,1},{8,14},{9,15},{10,... | collective-permute-start | bytes 442376 | tf_op jit(solution)/shard_map/ppermute | solution.py:372
  24.4 8.3 %collective-permute-start.3 = (f16[64,1152]{1,0:T(8,128)(2,1)S(1)}, f16[64,1152]{1,0:T(8,128)(2,1)S(1)}, u32[]{:S(2)}, u32[]{:S(2)}) collective-permute-start(f16[64,1152]{1,0:T(8,128)(2,1)S(1)} %get-tuple-element.51), channel_id=1, source_target_pairs={{0,4},{1,3},{2,6},{3,1},{4,0},{5,7},{6,2},{7,5},{8,12},{9,11},{10,... | collective-permute-start | bytes 442376 | tf_op jit(solution)/shard_map/ppermute | solution.py:372
  24.9 7.9 %collective-permute-start.4 = (f16[64,1152]{1,0:T(8,128)(2,1)S(1)}, f16[64,1152]{1,0:T(8,128)(2,1)S(1)}, u32[]{:S(2)}, u32[]{:S(2)}) collective-permute-start(f16[64,1152]{1,0:T(8,128)(2,1)S(1)} %get-tuple-element.50), channel_id=1, source_target_pairs={{0,2},{1,5},{2,0},{3,7},{4,6},{5,1},{6,4},{7,3},{8,10},{9,13},{10,... | collective-permute-start | bytes 442376 | tf_op jit(solution)/shard_map/ppermute | solution.py:372
  25.1 12.5 %collective-permute-start.14 = (f16[64,1152]{1,0:T(8,128)(2,1)S(1)}, f16[64,1152]{1,0:T(8,128)(2,1)S(1)}, u32[]{:S(2)}, u32[]{:S(2)}) collective-permute-start(f16[64,1152]{1,0:T(8,128)(2,1)S(1)} %get-tuple-element.46), channel_id=1, source_target_pairs={{0,6},{1,7},{2,4},{3,5},{4,2},{5,3},{6,0},{7,1},{8,14},{9,15},{10,... | collective-permute-start | bytes 442376 | tf_op jit(solution)/shard_map/ppermute | solution.py:372
  28.0 11.5 %collective-permute-start.15 = (f16[64,1152]{1,0:T(8,128)(2,1)S(1)}, f16[64,1152]{1,0:T(8,128)(2,1)S(1)}, u32[]{:S(2)}, u32[]{:S(2)}) collective-permute-start(f16[64,1152]{1,0:T(8,128)(2,1)S(1)} %get-tuple-element.48), channel_id=1, source_target_pairs={{0,4},{1,3},{2,6},{3,1},{4,0},{5,7},{6,2},{7,5},{8,12},{9,11},{10,... | collective-permute-start | bytes 442376 | tf_op jit(solution)/shard_map/ppermute | solution.py:372
  29.0 10.6 %collective-permute-start.16 = (f16[64,1152]{1,0:T(8,128)(2,1)S(1)}, f16[64,1152]{1,0:T(8,128)(2,1)S(1)}, u32[]{:S(2)}, u32[]{:S(2)}) collective-permute-start(f16[64,1152]{1,0:T(8,128)(2,1)S(1)} %get-tuple-element.47), channel_id=1, source_target_pairs={{0,2},{1,5},{2,0},{3,7},{4,6},{5,1},{6,4},{7,3},{8,10},{9,13},{10,... | collective-permute-start | bytes 442376 | tf_op jit(solution)/shard_map/ppermute | solution.py:372
  33.3 9.2 %collective-permute-start.6 = (f16[16,1152]{1,0:T(8,128)(2,1)S(1)}, f16[16,1152]{1,0:T(8,128)(2,1)S(1)}, u32[]{:S(2)}, u32[]{:S(2)}) collective-permute-start(f16[16,1152]{1,0:T(8,128)(2,1)S(1)} %get-tuple-element.68), channel_id=1, source_target_pairs={{0,16},{1,9},{2,18},{3,11},{4,20},{5,13},{6,22},{7,15},{8,24},{9,1... | collective-permute-start | bytes 110600 | tf_op jit(solution)/shard_map/ppermute | solution.py:372
  36.0 8.6 %collective-permute-start.7 = (f16[16,1152]{1,0:T(8,128)(2,1)S(1)}, f16[16,1152]{1,0:T(8,128)(2,1)S(1)}, u32[]{:S(2)}, u32[]{:S(2)}) collective-permute-start(f16[16,1152]{1,0:T(8,128)(2,1)S(1)} %get-tuple-element.69), channel_id=1, source_target_pairs={{0,8},{1,17},{2,10},{3,19},{4,12},{5,21},{6,14},{7,23},{8,0},{9,25... | collective-permute-start | bytes 110600 | tf_op jit(solution)/shard_map/ppermute | solution.py:372
  37.6 7.0 %collective-permute-start.5 = (f16[16,1152]{1,0:T(8,128)(2,1)S(1)}, f16[16,1152]{1,0:T(8,128)(2,1)S(1)}, u32[]{:S(2)}, u32[]{:S(2)}) collective-permute-start(f16[16,1152]{1,0:T(8,128)(2,1)S(1)} %get-tuple-element.67), channel_id=1, source_target_pairs={{0,24},{1,25},{2,26},{3,27},{4,28},{5,29},{6,30},{7,31},{8,16},{9,... | collective-permute-start | bytes 110600 | tf_op jit(solution)/shard_map/ppermute | solution.py:372
  40.1 7.3 %collective-permute-start.17 = (f16[16,1152]{1,0:T(8,128)(2,1)S(1)}, f16[16,1152]{1,0:T(8,128)(2,1)S(1)}, u32[]{:S(2)}, u32[]{:S(2)}) collective-permute-start(f16[16,1152]{1,0:T(8,128)(2,1)S(1)} %get-tuple-element.63), channel_id=1, source_target_pairs={{0,24},{1,25},{2,26},{3,27},{4,28},{5,29},{6,30},{7,31},{8,16},{9,... | collective-permute-start | bytes 110600 | tf_op jit(solution)/shard_map/ppermute | solution.py:372
  42.5 6.0 %collective-permute-start.18 = (f16[16,1152]{1,0:T(8,128)(2,1)S(1)}, f16[16,1152]{1,0:T(8,128)(2,1)S(1)}, u32[]{:S(2)}, u32[]{:S(2)}) collective-permute-start(f16[16,1152]{1,0:T(8,128)(2,1)S(1)} %get-tuple-element.64), channel_id=1, source_target_pairs={{0,16},{1,9},{2,18},{3,11},{4,20},{5,13},{6,22},{7,15},{8,24},{9,1... | collective-permute-start | bytes 110600 | tf_op jit(solution)/shard_map/ppermute | solution.py:372
  42.5 6.0 %collective-permute-start.19 = (f16[16,1152]{1,0:T(8,128)(2,1)S(1)}, f16[16,1152]{1,0:T(8,128)(2,1)S(1)}, u32[]{:S(2)}, u32[]{:S(2)}) collective-permute-start(f16[16,1152]{1,0:T(8,128)(2,1)S(1)} %get-tuple-element.65), channel_id=1, source_target_pairs={{0,8},{1,17},{2,10},{3,19},{4,12},{5,21},{6,14},{7,23},{8,0},{9,25... | collective-permute-start | bytes 110600 | tf_op jit(solution)/shard_map/ppermute | solution.py:372
  44.9 6.6 %collective-permute-start.10 = (f16[16,1024]{1,0:T(8,128)(2,1)S(1)}, f16[16,1024]{1,0:T(8,128)(2,1)S(1)}, u32[]{:S(2)}, u32[]{:S(2)}) collective-permute-start(f16[16,1024]{1,0:T(8,128)(2,1)S(1)} %fusion.25), channel_id=1, source_target_pairs={{0,8},{1,17},{2,10},{3,19},{4,12},{5,21},{6,14},{7,23},{8,0},{9,25... | collective-permute-start | bytes 98312 | tf_op jit(solution)/shard_map/ppermute | solution.py:372
  45.0 8.5 %collective-permute-start.8 = (f16[16,1024]{1,0:T(8,128)(2,1)S(1)}, f16[16,1024]{1,0:T(8,128)(2,1)S(1)}, u32[]{:S(2)}, u32[]{:S(2)}) collective-permute-start(f16[16,1024]{1,0:T(8,128)(2,1)S(1)} %fusion.25), channel_id=1, source_target_pairs={{0,24},{1,25},{2,26},{3,27},{4,28},{5,29},{6,30},{7,31},{8,16},{9,... | collective-permute-start | bytes 98312 | tf_op jit(solution)/shard_map/ppermute | solution.py:372
  47.4 6.1 %collective-permute-start.9 = (f16[16,1024]{1,0:T(8,128)(2,1)S(1)}, f16[16,1024]{1,0:T(8,128)(2,1)S(1)}, u32[]{:S(2)}, u32[]{:S(2)}) collective-permute-start(f16[16,1024]{1,0:T(8,128)(2,1)S(1)} %fusion.25), channel_id=1, source_target_pairs={{0,16},{1,9},{2,18},{3,11},{4,20},{5,13},{6,22},{7,15},{8,24},{9,1... | collective-permute-start | bytes 98312 | tf_op jit(solution)/shard_map/ppermute | solution.py:372
  48.8 7.8 %collective-permute-start.20 = (f16[16,1024]{1,0:T(8,128)(2,1)S(1)}, f16[16,1024]{1,0:T(8,128)(2,1)S(1)}, u32[]{:S(2)}, u32[]{:S(2)}) collective-permute-start(f16[16,1024]{1,0:T(8,128)(2,1)S(1)} %fusion.21), channel_id=1, source_target_pairs={{0,24},{1,25},{2,26},{3,27},{4,28},{5,29},{6,30},{7,31},{8,16},{9,... | collective-permute-start | bytes 98312 | tf_op jit(solution)/shard_map/ppermute | solution.py:372
  51.3 5.9 %collective-permute-start.21 = (f16[16,1024]{1,0:T(8,128)(2,1)S(1)}, f16[16,1024]{1,0:T(8,128)(2,1)S(1)}, u32[]{:S(2)}, u32[]{:S(2)}) collective-permute-start(f16[16,1024]{1,0:T(8,128)(2,1)S(1)} %fusion.21), channel_id=1, source_target_pairs={{0,16},{1,9},{2,18},{3,11},{4,20},{5,13},{6,22},{7,15},{8,24},{9,1... | collective-permute-start | bytes 98312 | tf_op jit(solution)/shard_map/ppermute | solution.py:372
  51.5 5.7 %collective-permute-start.22 = (f16[16,1024]{1,0:T(8,128)(2,1)S(1)}, f16[16,1024]{1,0:T(8,128)(2,1)S(1)}, u32[]{:S(2)}, u32[]{:S(2)}) collective-permute-start(f16[16,1024]{1,0:T(8,128)(2,1)S(1)} %fusion.21), channel_id=1, source_target_pairs={{0,8},{1,17},{2,10},{3,19},{4,12},{5,21},{6,14},{7,23},{8,0},{9,25... | collective-permute-start | bytes 98312 | tf_op jit(solution)/shard_map/ppermute | solution.py:372
  53.6 7.4 %collective-permute-start.11 = (f16[64,1024]{1,0:T(8,128)(2,1)S(1)}, f16[64,1024]{1,0:T(8,128)(2,1)S(1)}, u32[]{:S(2)}, u32[]{:S(2)}) collective-permute-start(f16[64,1024]{1,0:T(8,128)(2,1)S(1)} %pad_maximum_fusion.1), channel_id=1, source_target_pairs={{0,6},{1,7},{2,4},{3,5},{4,2},{5,3},{6,0},{7,1},{8,14},{9,15},{10,... | collective-permute-start | bytes 393224 | tf_op jit(solution)/shard_map/ppermute | solution.py:372
  56.2 6.9 %collective-permute-start.12 = (f16[64,1024]{1,0:T(8,128)(2,1)S(1)}, f16[64,1024]{1,0:T(8,128)(2,1)S(1)}, u32[]{:S(2)}, u32[]{:S(2)}) collective-permute-start(f16[64,1024]{1,0:T(8,128)(2,1)S(1)} %pad_maximum_fusion.1), channel_id=1, source_target_pairs={{0,4},{1,3},{2,6},{3,1},{4,0},{5,7},{6,2},{7,5},{8,12},{9,11},{10,... | collective-permute-start | bytes 393224 | tf_op jit(solution)/shard_map/ppermute | solution.py:372
  56.7 6.4 %collective-permute-start.13 = (f16[64,1024]{1,0:T(8,128)(2,1)S(1)}, f16[64,1024]{1,0:T(8,128)(2,1)S(1)}, u32[]{:S(2)}, u32[]{:S(2)}) collective-permute-start(f16[64,1024]{1,0:T(8,128)(2,1)S(1)} %pad_maximum_fusion.1), channel_id=1, source_target_pairs={{0,2},{1,5},{2,0},{3,7},{4,6},{5,1},{6,4},{7,3},{8,10},{9,13},{10,... | collective-permute-start | bytes 393224 | tf_op jit(solution)/shard_map/ppermute | solution.py:372
  57.3 7.2 %collective-permute-start.23 = (f16[64,1024]{1,0:T(8,128)(2,1)S(1)}, f16[64,1024]{1,0:T(8,128)(2,1)S(1)}, u32[]{:S(2)}, u32[]{:S(2)}) collective-permute-start(f16[64,1024]{1,0:T(8,128)(2,1)S(1)} %pad_maximum_fusion.2), channel_id=1, source_target_pairs={{0,6},{1,7},{2,4},{3,5},{4,2},{5,3},{6,0},{7,1},{8,14},{9,15},{10,... | collective-permute-start | bytes 393224 | tf_op jit(solution)/shard_map/ppermute | solution.py:372
  59.9 6.0 %collective-permute-start.24 = (f16[64,1024]{1,0:T(8,128)(2,1)S(1)}, f16[64,1024]{1,0:T(8,128)(2,1)S(1)}, u32[]{:S(2)}, u32[]{:S(2)}) collective-permute-start(f16[64,1024]{1,0:T(8,128)(2,1)S(1)} %pad_maximum_fusion.2), channel_id=1, source_target_pairs={{0,4},{1,3},{2,6},{3,1},{4,0},{5,7},{6,2},{7,5},{8,12},{9,11},{10,... | collective-permute-start | bytes 393224 | tf_op jit(solution)/shard_map/ppermute | solution.py:372
  61.0 5.0 %collective-permute-start.25 = (f16[64,1024]{1,0:T(8,128)(2,1)S(1)}, f16[64,1024]{1,0:T(8,128)(2,1)S(1)}, u32[]{:S(2)}, u32[]{:S(2)}) collective-permute-start(f16[64,1024]{1,0:T(8,128)(2,1)S(1)} %pad_maximum_fusion.2), channel_id=1, source_target_pairs={{0,2},{1,5},{2,0},{3,7},{4,6},{5,1},{6,4},{7,3},{8,10},{9,13},{10,... | collective-permute-start | bytes 393224 | tf_op jit(solution)/shard_map/ppermute | solution.py:372

commit v6 on v5

--- a/solution.py
+++ b/solution.py
@@ -206,7 +206,7 @@
     n_subjects, frames, own = data.shape
     n_centres, k = neighbours.shape
     n_wide = own + 2 * k
-    group = math.gcd(n_centres, 8)
+    group = math.gcd(n_centres, 16)
     begin = own // 16 * FIRST
     vmem = pl.BlockSpec(memory_space=pltpu.VMEM)
     hbm = pl.BlockSpec(memory_space=pl.ANY)

time: 68.1 us -> 68 us (level)
  no operation moved by 1% of the time
where the time goes in v6:
time: 68 us; the launch traced here: 67.8 us
  starting transfers between devices  37.7 us (55%)
  Pallas kernels  16.4 us (24%)
  waiting for transfers between devices  8.03 us (12%)
  other arithmetic  4.31 us (6%)
  between operations  0.95 us (1%)
    ppermute x24, starting transfers between devices, swap(): return lax.ppermute(value, ('subj', 'vert'), self.pairs(phase, m))  36.7 us
    pallas_call x1, Pallas kernels, align(): pl.pallas_call(functools.partial(align_kernel, n_subjects, n_centres, gro...  14.1 us
    ppermute x24, waiting for transfers between devices, swap(): return lax.ppermute(value, ('subj', 'vert'), self.pairs(phase, m))  5.86 us
    ppermute x2, waiting for transfers between devices, core_swap(): return lax.ppermute(value, 'vert', [(0, 1), (1, 0)])  2.18 us
    concatenate x1, other arithmetic, local(): jnp.concatenate([end[:, inner:inner + k], begin, end[:, :inner], end[:, i...  1.5 us
    pallas_call x1, Pallas kernels, finish_edges(): pl.pallas_call(functools.partial(edges_kernel, n_subjects), out_shape=(ja...  1.36 us
  transfers between devices with their start and end apart: 26, of which 9 were waited for; matrix products, arithmetic and copies ran while one was open for 4% of the time, Pallas kernels for 0%

profile of v6, /device:TPU:0, one launch (start us, length us, event | category | flops | bytes accessed | tf_op | source)
XLA Modules:
  0.0 67.8 jit_solution(16660692885577563643)
XLA Ops:
  0.7 0.9 %facing.1 = bf16[3,256,128]{2,1,0:T(8,128)(2,1)S(1)} custom-call(s32[1]{0:T(128)} %bitcast.2.start_ref, bf16[2,256,2048]{2,1,0:T(8,128)(2,1)} %data_ref.3, bf16[256,2048]{1,0:T(8,128)(2,1)} %tmpl_ref.3), custom_call_target="tpu_custom_call" | custom-call | bytes 800000 | tf_op jit(solution)/shard_map/facing/pallas_call | solution.py:319
  1.6 0.5 collective-permute-start
  2.1 0.1 add_convert_fusion.meta_ref
  2.2 1.0 %collective-permute-done.low_ref.high_ref = bf16[3,256,128]{2,1,0:T(8,128)(2,1)S(1)} collective-permute-done((bf16[3,256,128]{2,1,0:T(8,128)(2,1)S(1)}, bf16[3,256,128]{2,1,0:T(8,128)(2,1)S(1)}, u32[]{:S(2)}, u32[]{:S(2)}) %collective-permute-start) | collective-permute-done | bytes 196640 | tf_op jit(solution)/shard_map/ppermute | solution.py:332
  3.2 14.1 %align.1 = (bf16[2,256,2048]{2,1,0:T(8,128)(2,1)}, f32[256,1152]{1,0:T(8,128)S(1)}, f32[256,768]{1,0:T(8,128)S(1)}, f32[2,264,128]{2,1,0:T(8,128)S(1)}, f32[2,26...) custom-call(s32[2]{0:T(128)S(1)} %add_convert_fusion.meta_ref, ...), custom_call_target="tpu_custom_call" | custom-call | flops 16000000000 | bytes 8000000 | tf_op jit(solution)/shard_map/align/pallas_call | solution.py:214
  17.4 0.4 collective-permute-start.1
  17.8 1.2 %collective-permute-done.1.low_ref.high_ref = f32[2,264,128]{2,1,0:T(8,128)S(1)} collective-permute-done((f32[2,264,128]{2,1,0:T(8,128)S(1)}, f32[2,264,128]{2,1,0:T(8,128)S(1)}, u32[]{:S(2)}, u32[]{:S(2)}) %collective-permute-start.1) | collective-permute-done | bytes 270368 | tf_op jit(solution)/shard_map/ppermute | solution.py:332
  19.0 1.4 %edges.1 = (bf16[2,256,2048]{2,1,0:T(8,128)(2,1)}, f32[256,1152]{1,0:T(8,128)S(1)}) custom-call(s32[2]{0:T(128)S(1)} %add_convert_fusion.meta_ref, f32[2,256,128]{2,1,0:T(8,128)S(1)} %get-tuple-element.14.low_edge, f32[2,256,128]{2,1,0:T(8,128)S(1)} %get-tuple-element.15.high_edge, ...), custom_call_target="tpu_custom_call", output_to_operand_aliasing={{0}: (7, {})} | custom-call | flops 1000000000 | bytes 2000000 | tf_op jit(solution)/shard_map/edges/pallas_call | solution.py:281
  20.4 0.1 dynamic-slice_convert_fusion.5
  20.4 3.9 %collective-permute-start.2 = (f16[64,1152]{1,0:T(8,128)(2,1)S(1)}, f16[64,1152]{1,0:T(8,128)(2,1)S(1)}, u32[]{:S(2)}, u32[]{:S(2)}) collective-permute-start(f16[64,1152]{1,0:T(8,128)(2,1)S(1)} %get-tuple-element.49), channel_id=1, source_target_pairs={{0,6},{1,7},{2,4},{3,5},{4,2},{5,3},{6,0},{7,1},{8,14},{9,15},{10,... | collective-permute-start | bytes 442376 | tf_op jit(solution)/shard_map/ppermute | solution.py:372
  24.3 0.5 collective-permute-start.3
  24.8 0.1 collective-permute-start.4
  25.0 2.9 %collective-permute-start.14 = (f16[64,1152]{1,0:T(8,128)(2,1)S(1)}, f16[64,1152]{1,0:T(8,128)(2,1)S(1)}, u32[]{:S(2)}, u32[]{:S(2)}) collective-permute-start(f16[64,1152]{1,0:T(8,128)(2,1)S(1)} %get-tuple-element.46), channel_id=1, source_target_pairs={{0,6},{1,7},{2,4},{3,5},{4,2},{5,3},{6,0},{7,1},{8,14},{9,15},{10,... | collective-permute-start | bytes 442376 | tf_op jit(solution)/shard_map/ppermute | solution.py:372
  27.9 0.5 collective-permute-start.15
  28.4 0.5 collective-permute-done.2
  28.9 2.0 %collective-permute-start.16 = (f16[64,1152]{1,0:T(8,128)(2,1)S(1)}, f16[64,1152]{1,0:T(8,128)(2,1)S(1)}, u32[]{:S(2)}, u32[]{:S(2)}) collective-permute-start(f16[64,1152]{1,0:T(8,128)(2,1)S(1)} %get-tuple-element.47), channel_id=1, source_target_pairs={{0,2},{1,5},{2,0},{3,7},{4,6},{5,1},{6,4},{7,3},{8,10},{9,13},{10,... | collective-permute-start | bytes 442376 | tf_op jit(solution)/shard_map/ppermute | solution.py:372
  31.0 1.7 %collective-permute-done.3 = f16[64,1152]{1,0:T(8,128)(2,1)S(1)} collective-permute-done((f16[64,1152]{1,0:T(8,128)(2,1)S(1)}, f16[64,1152]{1,0:T(8,128)(2,1)S(1)}, u32[]{:S(2)}, u32[]{:S(2)}) %collective-permute-start.3) | collective-permute-done | bytes 147488 | tf_op jit(solution)/shard_map/ppermute | solution.py:372
  32.7 0.0 collective-permute-done.4
  32.7 0.2 fusion.29
  32.9 0.1 fusion.3
  33.1 0.1 broadcast_in_dim.9
  33.2 2.7 %collective-permute-start.6 = (f16[16,1152]{1,0:T(8,128)(2,1)S(1)}, f16[16,1152]{1,0:T(8,128)(2,1)S(1)}, u32[]{:S(2)}, u32[]{:S(2)}) collective-permute-start(f16[16,1152]{1,0:T(8,128)(2,1)S(1)} %get-tuple-element.68), channel_id=1, source_target_pairs={{0,16},{1,9},{2,18},{3,11},{4,20},{5,13},{6,22},{7,15},{8,24},{9,1... | collective-permute-start | bytes 110600 | tf_op jit(solution)/shard_map/ppermute | solution.py:372
  35.9 1.6 %collective-permute-start.7 = (f16[16,1152]{1,0:T(8,128)(2,1)S(1)}, f16[16,1152]{1,0:T(8,128)(2,1)S(1)}, u32[]{:S(2)}, u32[]{:S(2)}) collective-permute-start(f16[16,1152]{1,0:T(8,128)(2,1)S(1)} %get-tuple-element.69), channel_id=1, source_target_pairs={{0,8},{1,17},{2,10},{3,19},{4,12},{5,21},{6,14},{7,23},{8,0},{9,25... | collective-permute-start | bytes 110600 | tf_op jit(solution)/shard_map/ppermute | solution.py:372
  37.5 0.0 collective-permute-done.14
  37.5 2.0 %collective-permute-start.5 = (f16[16,1152]{1,0:T(8,128)(2,1)S(1)}, f16[16,1152]{1,0:T(8,128)(2,1)S(1)}, u32[]{:S(2)}, u32[]{:S(2)}) collective-permute-start(f16[16,1152]{1,0:T(8,128)(2,1)S(1)} %get-tuple-element.67), channel_id=1, source_target_pairs={{0,24},{1,25},{2,26},{3,27},{4,28},{5,29},{6,30},{7,31},{8,16},{9,... | collective-permute-start | bytes 110600 | tf_op jit(solution)/shard_map/ppermute | solution.py:372
  39.4 0.0 collective-permute-done.15
  39.5 0.2 fusion.28
  39.7 0.2 fusion
  39.9 0.1 broadcast_in_dim.11
  40.0 2.4 %collective-permute-start.17 = (f16[16,1152]{1,0:T(8,128)(2,1)S(1)}, f16[16,1152]{1,0:T(8,128)(2,1)S(1)}, u32[]{:S(2)}, u32[]{:S(2)}) collective-permute-start(f16[16,1152]{1,0:T(8,128)(2,1)S(1)} %get-tuple-element.63), channel_id=1, source_target_pairs={{0,24},{1,25},{2,26},{3,27},{4,28},{5,29},{6,30},{7,31},{8,16},{9,... | collective-permute-start | bytes 110600 | tf_op jit(solution)/shard_map/ppermute | solution.py:372
  42.4 2.0 %collective-permute-start.19 = (f16[16,1152]{1,0:T(8,128)(2,1)S(1)}, f16[16,1152]{1,0:T(8,128)(2,1)S(1)}, u32[]{:S(2)}, u32[]{:S(2)}) collective-permute-start(f16[16,1152]{1,0:T(8,128)(2,1)S(1)} %get-tuple-element.65), channel_id=1, source_target_pairs={{0,8},{1,17},{2,10},{3,19},{4,12},{5,21},{6,14},{7,23},{8,0},{9,25... | collective-permute-start | bytes 110600 | tf_op jit(solution)/shard_map/ppermute | solution.py:372
  44.5 0.2 multiply_reduce_fusion.1
  44.7 0.1 fusion.25
  44.8 0.1 collective-permute-start.10
  44.9 2.4 %collective-permute-start.8 = (f16[16,1024]{1,0:T(8,128)(2,1)S(1)}, f16[16,1024]{1,0:T(8,128)(2,1)S(1)}, u32[]{:S(2)}, u32[]{:S(2)}) collective-permute-start(f16[16,1024]{1,0:T(8,128)(2,1)S(1)} %fusion.25), channel_id=1, source_target_pairs={{0,24},{1,25},{2,26},{3,27},{4,28},{5,29},{6,30},{7,31},{8,16},{9,... | collective-permute-start | bytes 98312 | tf_op jit(solution)/shard_map/ppermute | solution.py:372
  47.3 1.0 %collective-permute-start.9 = (f16[16,1024]{1,0:T(8,128)(2,1)S(1)}, f16[16,1024]{1,0:T(8,128)(2,1)S(1)}, u32[]{:S(2)}, u32[]{:S(2)}) collective-permute-start(f16[16,1024]{1,0:T(8,128)(2,1)S(1)} %fusion.25), channel_id=1, source_target_pairs={{0,16},{1,9},{2,18},{3,11},{4,20},{5,13},{6,22},{7,15},{8,24},{9,1... | collective-permute-start | bytes 98312 | tf_op jit(solution)/shard_map/ppermute | solution.py:372
  48.4 0.2 multiply_reduce_fusion
  48.6 0.1 fusion.21
  48.7 2.4 %collective-permute-start.20 = (f16[16,1024]{1,0:T(8,128)(2,1)S(1)}, f16[16,1024]{1,0:T(8,128)(2,1)S(1)}, u32[]{:S(2)}, u32[]{:S(2)}) collective-permute-start(f16[16,1024]{1,0:T(8,128)(2,1)S(1)} %fusion.21), channel_id=1, source_target_pairs={{0,24},{1,25},{2,26},{3,27},{4,28},{5,29},{6,30},{7,31},{8,16},{9,... | collective-permute-start | bytes 98312 | tf_op jit(solution)/shard_map/ppermute | solution.py:372
  51.2 0.1 collective-permute-start.21
  51.2 0.1 mul.311
  51.3 0.1 mul.281
  51.4 2.0 %collective-permute-start.22 = (f16[16,1024]{1,0:T(8,128)(2,1)S(1)}, f16[16,1024]{1,0:T(8,128)(2,1)S(1)}, u32[]{:S(2)}, u32[]{:S(2)}) collective-permute-start(f16[16,1024]{1,0:T(8,128)(2,1)S(1)} %fusion.21), channel_id=1, source_target_pairs={{0,8},{1,17},{2,10},{3,19},{4,12},{5,21},{6,14},{7,23},{8,0},{9,25... | collective-permute-start | bytes 98312 | tf_op jit(solution)/shard_map/ppermute | solution.py:372
  53.4 0.1 select_select_fusion.15
  53.5 2.6 %collective-permute-start.11 = (f16[64,1024]{1,0:T(8,128)(2,1)S(1)}, f16[64,1024]{1,0:T(8,128)(2,1)S(1)}, u32[]{:S(2)}, u32[]{:S(2)}) collective-permute-start(f16[64,1024]{1,0:T(8,128)(2,1)S(1)} %pad_maximum_fusion.1), channel_id=1, source_target_pairs={{0,6},{1,7},{2,4},{3,5},{4,2},{5,3},{6,0},{7,1},{8,14},{9,15},{10,... | collective-permute-start | bytes 393224 | tf_op jit(solution)/shard_map/ppermute | solution.py:372
  56.1 0.5 collective-permute-start.12
  56.6 0.5 collective-permute-start.13
  57.1 0.1 select_select_fusion.11
  57.2 2.6 %collective-permute-start.23 = (f16[64,1024]{1,0:T(8,128)(2,1)S(1)}, f16[64,1024]{1,0:T(8,128)(2,1)S(1)}, u32[]{:S(2)}, u32[]{:S(2)}) collective-permute-start(f16[64,1024]{1,0:T(8,128)(2,1)S(1)} %pad_maximum_fusion.2), channel_id=1, source_target_pairs={{0,6},{1,7},{2,4},{3,5},{4,2},{5,3},{6,0},{7,1},{8,14},{9,15},{10,... | collective-permute-start | bytes 393224 | tf_op jit(solution)/shard_map/ppermute | solution.py:372
  59.8 0.5 collective-permute-start.24
  60.2 0.7 collective-permute-done.11
  60.9 1.5 %collective-permute-start.25 = (f16[64,1024]{1,0:T(8,128)(2,1)S(1)}, f16[64,1024]{1,0:T(8,128)(2,1)S(1)}, u32[]{:S(2)}, u32[]{:S(2)}) collective-permute-start(f16[64,1024]{1,0:T(8,128)(2,1)S(1)} %pad_maximum_fusion.2), channel_id=1, source_target_pairs={{0,2},{1,5},{2,0},{3,7},{4,6},{5,1},{6,4},{7,3},{8,10},{9,13},{10,... | collective-permute-start | bytes 393224 | tf_op jit(solution)/shard_map/ppermute | solution.py:372
  62.4 0.6 collective-permute-done.12
  63.0 0.1 select_select_fusion.6
  63.1 0.1 select_select_fusion.7
  63.2 0.2 convert_multiply_fusion.1
  63.4 0.1 slice.171
  63.5 0.9 %collective-permute-done.23 = f16[64,1024]{1,0:T(8,128)(2,1)S(1)} collective-permute-done((f16[64,1024]{1,0:T(8,128)(2,1)S(1)}, f16[64,1024]{1,0:T(8,128)(2,1)S(1)}, u32[]{:S(2)}, u32[]{:S(2)}) %collective-permute-start.23) | collective-permute-done | bytes 131104 | tf_op jit(solution)/shard_map/ppermute | solution.py:372
  64.4 1.4 %collective-permute-done.24 = f16[64,1024]{1,0:T(8,128)(2,1)S(1)} collective-permute-done((f16[64,1024]{1,0:T(8,128)(2,1)S(1)}, f16[64,1024]{1,0:T(8,128)(2,1)S(1)}, u32[]{:S(2)}, u32[]{:S(2)}) %collective-permute-start.24) | collective-permute-done | bytes 131104 | tf_op jit(solution)/shard_map/ppermute | solution.py:372
  65.8 0.1 collective-permute-done.25
  65.9 0.1 select_select_fusion.2
  66.0 0.1 select_select_fusion.3
  66.1 0.2 convert_multiply_fusion
  66.3 1.5 %pad_maximum_fusion = f32[256,2048]{1,0:T(8,128)} fusion(f32[256,128]{1,0:T(8,128)S(1)} %get-tuple-element.53, f32[256,768]{1,0:T(8,128)S(1)} %slice.171, f32[256,1024]{1,0:T(8,128)S(1)} %convert_multiply_fusion, f32[256,128]{1,0:T(8,128)S(1)} %get-tuple-element.52), kind=kLoop, calls=%fused_computation | loop fusion | flops 1572864 | bytes 4194304 | tf_op jit(solution)/shard_map/concatenate | solution.py:450
  (42 shorter events, 0.5 us)
Async XLA Ops:
  0.6 1.5 %copy-start = (s32[16,128]{1,0:T(8,128)S(1)}, s32[16,128]{1,0:T(8,128)}, u32[]{:S(2)}) copy-start(s32[16,128]{1,0:T(8,128)} %param.7) | copy-start | bytes 24580
  0.6 1.6 %copy-start.1 = (s32[16]{0:T(128)S(1)}, s32[16]{0:T(128)}, u32[]{:S(2)}) copy-start(s32[16]{0:T(128)} %param.6) | copy-start | bytes 196
  1.6 1.6 %collective-permute-start = (bf16[3,256,128]{2,1,0:T(8,128)(2,1)S(1)}, bf16[3,256,128]{2,1,0:T(8,128)(2,1)S(1)}, u32[]{:S(2)}, u32[]{:S(2)}) collective-permute-start(bf16[3,256,128]{2,1,0:T(8,128)(2,1)S(1)} %facing.1), channel_id=1, source_target_pairs={{0,1},{1,0},{2,3},{3,2},{4,5},{5,4},{6,7},{7,6},{8,9},{9,8},{10,11... | collective-permute-start | bytes 589832 | tf_op jit(solution)/shard_map/ppermute | solution.py:332
  17.4 1.6 %collective-permute-start.1 = (f32[2,264,128]{2,1,0:T(8,128)S(1)}, f32[2,264,128]{2,1,0:T(8,128)S(1)}, u32[]{:S(2)}, u32[]{:S(2)}) collective-permute-start(f32[2,264,128]{2,1,0:T(8,128)S(1)} %broadcast_select_fusion), channel_id=1, source_target_pairs={{0,1},{1,0},{2,3},{3,2},{4,5},{5,4},{6,7},{7,6},{8,9},{9,8},{10,11... | collective-permute-start | bytes 811016 | tf_op jit(solution)/shard_map/ppermute | solution.py:332
  20.4 8.5 %collective-permute-start.2 = (f16[64,1152]{1,0:T(8,128)(2,1)S(1)}, f16[64,1152]{1,0:T(8,128)(2,1)S(1)}, u32[]{:S(2)}, u32[]{:S(2)}) collective-permute-start(f16[64,1152]{1,0:T(8,128)(2,1)S(1)} %get-tuple-element.49), channel_id=1, source_target_pairs={{0,6},{1,7},{2,4},{3,5},{4,2},{5,3},{6,0},{7,1},{8,14},{9,15},{10,... | collective-permute-start | bytes 442376 | tf_op jit(solution)/shard_map/ppermute | solution.py:372
  24.3 8.3 %collective-permute-start.3 = (f16[64,1152]{1,0:T(8,128)(2,1)S(1)}, f16[64,1152]{1,0:T(8,128)(2,1)S(1)}, u32[]{:S(2)}, u32[]{:S(2)}) collective-permute-start(f16[64,1152]{1,0:T(8,128)(2,1)S(1)} %get-tuple-element.51), channel_id=1, source_target_pairs={{0,4},{1,3},{2,6},{3,1},{4,0},{5,7},{6,2},{7,5},{8,12},{9,11},{10,... | collective-permute-start | bytes 442376 | tf_op jit(solution)/shard_map/ppermute | solution.py:372
  24.8 7.9 %collective-permute-start.4 = (f16[64,1152]{1,0:T(8,128)(2,1)S(1)}, f16[64,1152]{1,0:T(8,128)(2,1)S(1)}, u32[]{:S(2)}, u32[]{:S(2)}) collective-permute-start(f16[64,1152]{1,0:T(8,128)(2,1)S(1)} %get-tuple-element.50), channel_id=1, source_target_pairs={{0,2},{1,5},{2,0},{3,7},{4,6},{5,1},{6,4},{7,3},{8,10},{9,13},{10,... | collective-permute-start | bytes 442376 | tf_op jit(solution)/shard_map/ppermute | solution.py:372
  25.0 12.5 %collective-permute-start.14 = (f16[64,1152]{1,0:T(8,128)(2,1)S(1)}, f16[64,1152]{1,0:T(8,128)(2,1)S(1)}, u32[]{:S(2)}, u32[]{:S(2)}) collective-permute-start(f16[64,1152]{1,0:T(8,128)(2,1)S(1)} %get-tuple-element.46), channel_id=1, source_target_pairs={{0,6},{1,7},{2,4},{3,5},{4,2},{5,3},{6,0},{7,1},{8,14},{9,15},{10,... | collective-permute-start | bytes 442376 | tf_op jit(solution)/shard_map/ppermute | solution.py:372
  27.9 11.5 %collective-permute-start.15 = (f16[64,1152]{1,0:T(8,128)(2,1)S(1)}, f16[64,1152]{1,0:T(8,128)(2,1)S(1)}, u32[]{:S(2)}, u32[]{:S(2)}) collective-permute-start(f16[64,1152]{1,0:T(8,128)(2,1)S(1)} %get-tuple-element.48), channel_id=1, source_target_pairs={{0,4},{1,3},{2,6},{3,1},{4,0},{5,7},{6,2},{7,5},{8,12},{9,11},{10,... | collective-permute-start | bytes 442376 | tf_op jit(solution)/shard_map/ppermute | solution.py:372
  28.9 10.5 %collective-permute-start.16 = (f16[64,1152]{1,0:T(8,128)(2,1)S(1)}, f16[64,1152]{1,0:T(8,128)(2,1)S(1)}, u32[]{:S(2)}, u32[]{:S(2)}) collective-permute-start(f16[64,1152]{1,0:T(8,128)(2,1)S(1)} %get-tuple-element.47), channel_id=1, source_target_pairs={{0,2},{1,5},{2,0},{3,7},{4,6},{5,1},{6,4},{7,3},{8,10},{9,13},{10,... | collective-permute-start | bytes 442376 | tf_op jit(solution)/shard_map/ppermute | solution.py:372
  33.2 9.2 %collective-permute-start.6 = (f16[16,1152]{1,0:T(8,128)(2,1)S(1)}, f16[16,1152]{1,0:T(8,128)(2,1)S(1)}, u32[]{:S(2)}, u32[]{:S(2)}) collective-permute-start(f16[16,1152]{1,0:T(8,128)(2,1)S(1)} %get-tuple-element.68), channel_id=1, source_target_pairs={{0,16},{1,9},{2,18},{3,11},{4,20},{5,13},{6,22},{7,15},{8,24},{9,1... | collective-permute-start | bytes 110600 | tf_op jit(solution)/shard_map/ppermute | solution.py:372
  35.9 8.6 %collective-permute-start.7 = (f16[16,1152]{1,0:T(8,128)(2,1)S(1)}, f16[16,1152]{1,0:T(8,128)(2,1)S(1)}, u32[]{:S(2)}, u32[]{:S(2)}) collective-permute-start(f16[16,1152]{1,0:T(8,128)(2,1)S(1)} %get-tuple-element.69), channel_id=1, source_target_pairs={{0,8},{1,17},{2,10},{3,19},{4,12},{5,21},{6,14},{7,23},{8,0},{9,25... | collective-permute-start | bytes 110600 | tf_op jit(solution)/shard_map/ppermute | solution.py:372
  37.5 7.0 %collective-permute-start.5 = (f16[16,1152]{1,0:T(8,128)(2,1)S(1)}, f16[16,1152]{1,0:T(8,128)(2,1)S(1)}, u32[]{:S(2)}, u32[]{:S(2)}) collective-permute-start(f16[16,1152]{1,0:T(8,128)(2,1)S(1)} %get-tuple-element.67), channel_id=1, source_target_pairs={{0,24},{1,25},{2,26},{3,27},{4,28},{5,29},{6,30},{7,31},{8,16},{9,... | collective-permute-start | bytes 110600 | tf_op jit(solution)/shard_map/ppermute | solution.py:372
  40.0 7.3 %collective-permute-start.17 = (f16[16,1152]{1,0:T(8,128)(2,1)S(1)}, f16[16,1152]{1,0:T(8,128)(2,1)S(1)}, u32[]{:S(2)}, u32[]{:S(2)}) collective-permute-start(f16[16,1152]{1,0:T(8,128)(2,1)S(1)} %get-tuple-element.63), channel_id=1, source_target_pairs={{0,24},{1,25},{2,26},{3,27},{4,28},{5,29},{6,30},{7,31},{8,16},{9,... | collective-permute-start | bytes 110600 | tf_op jit(solution)/shard_map/ppermute | solution.py:372
  42.4 5.9 %collective-permute-start.18 = (f16[16,1152]{1,0:T(8,128)(2,1)S(1)}, f16[16,1152]{1,0:T(8,128)(2,1)S(1)}, u32[]{:S(2)}, u32[]{:S(2)}) collective-permute-start(f16[16,1152]{1,0:T(8,128)(2,1)S(1)} %get-tuple-element.64), channel_id=1, source_target_pairs={{0,16},{1,9},{2,18},{3,11},{4,20},{5,13},{6,22},{7,15},{8,24},{9,1... | collective-permute-start | bytes 110600 | tf_op jit(solution)/shard_map/ppermute | solution.py:372
  42.4 6.0 %collective-permute-start.19 = (f16[16,1152]{1,0:T(8,128)(2,1)S(1)}, f16[16,1152]{1,0:T(8,128)(2,1)S(1)}, u32[]{:S(2)}, u32[]{:S(2)}) collective-permute-start(f16[16,1152]{1,0:T(8,128)(2,1)S(1)} %get-tuple-element.65), channel_id=1, source_target_pairs={{0,8},{1,17},{2,10},{3,19},{4,12},{5,21},{6,14},{7,23},{8,0},{9,25... | collective-permute-start | bytes 110600 | tf_op jit(solution)/shard_map/ppermute | solution.py:372
  44.8 6.6 %collective-permute-start.10 = (f16[16,1024]{1,0:T(8,128)(2,1)S(1)}, f16[16,1024]{1,0:T(8,128)(2,1)S(1)}, u32[]{:S(2)}, u32[]{:S(2)}) collective-permute-start(f16[16,1024]{1,0:T(8,128)(2,1)S(1)} %fusion.25), channel_id=1, source_target_pairs={{0,8},{1,17},{2,10},{3,19},{4,12},{5,21},{6,14},{7,23},{8,0},{9,25... | collective-permute-start | bytes 98312 | tf_op jit(solution)/shard_map/ppermute | solution.py:372
  44.9 8.5 %collective-permute-start.8 = (f16[16,1024]{1,0:T(8,128)(2,1)S(1)}, f16[16,1024]{1,0:T(8,128)(2,1)S(1)}, u32[]{:S(2)}, u32[]{:S(2)}) collective-permute-start(f16[16,1024]{1,0:T(8,128)(2,1)S(1)} %fusion.25), channel_id=1, source_target_pairs={{0,24},{1,25},{2,26},{3,27},{4,28},{5,29},{6,30},{7,31},{8,16},{9,... | collective-permute-start | bytes 98312 | tf_op jit(solution)/shard_map/ppermute | solution.py:372
  47.3 6.1 %collective-permute-start.9 = (f16[16,1024]{1,0:T(8,128)(2,1)S(1)}, f16[16,1024]{1,0:T(8,128)(2,1)S(1)}, u32[]{:S(2)}, u32[]{:S(2)}) collective-permute-start(f16[16,1024]{1,0:T(8,128)(2,1)S(1)} %fusion.25), channel_id=1, source_target_pairs={{0,16},{1,9},{2,18},{3,11},{4,20},{5,13},{6,22},{7,15},{8,24},{9,1... | collective-permute-start | bytes 98312 | tf_op jit(solution)/shard_map/ppermute | solution.py:372
  48.7 7.8 %collective-permute-start.20 = (f16[16,1024]{1,0:T(8,128)(2,1)S(1)}, f16[16,1024]{1,0:T(8,128)(2,1)S(1)}, u32[]{:S(2)}, u32[]{:S(2)}) collective-permute-start(f16[16,1024]{1,0:T(8,128)(2,1)S(1)} %fusion.21), channel_id=1, source_target_pairs={{0,24},{1,25},{2,26},{3,27},{4,28},{5,29},{6,30},{7,31},{8,16},{9,... | collective-permute-start | bytes 98312 | tf_op jit(solution)/shard_map/ppermute | solution.py:372
  51.2 5.9 %collective-permute-start.21 = (f16[16,1024]{1,0:T(8,128)(2,1)S(1)}, f16[16,1024]{1,0:T(8,128)(2,1)S(1)}, u32[]{:S(2)}, u32[]{:S(2)}) collective-permute-start(f16[16,1024]{1,0:T(8,128)(2,1)S(1)} %fusion.21), channel_id=1, source_target_pairs={{0,16},{1,9},{2,18},{3,11},{4,20},{5,13},{6,22},{7,15},{8,24},{9,1... | collective-permute-start | bytes 98312 | tf_op jit(solution)/shard_map/ppermute | solution.py:372
  51.4 5.7 %collective-permute-start.22 = (f16[16,1024]{1,0:T(8,128)(2,1)S(1)}, f16[16,1024]{1,0:T(8,128)(2,1)S(1)}, u32[]{:S(2)}, u32[]{:S(2)}) collective-permute-start(f16[16,1024]{1,0:T(8,128)(2,1)S(1)} %fusion.21), channel_id=1, source_target_pairs={{0,8},{1,17},{2,10},{3,19},{4,12},{5,21},{6,14},{7,23},{8,0},{9,25... | collective-permute-start | bytes 98312 | tf_op jit(solution)/shard_map/ppermute | solution.py:372
  53.5 7.4 %collective-permute-start.11 = (f16[64,1024]{1,0:T(8,128)(2,1)S(1)}, f16[64,1024]{1,0:T(8,128)(2,1)S(1)}, u32[]{:S(2)}, u32[]{:S(2)}) collective-permute-start(f16[64,1024]{1,0:T(8,128)(2,1)S(1)} %pad_maximum_fusion.1), channel_id=1, source_target_pairs={{0,6},{1,7},{2,4},{3,5},{4,2},{5,3},{6,0},{7,1},{8,14},{9,15},{10,... | collective-permute-start | bytes 393224 | tf_op jit(solution)/shard_map/ppermute | solution.py:372
  56.1 6.9 %collective-permute-start.12 = (f16[64,1024]{1,0:T(8,128)(2,1)S(1)}, f16[64,1024]{1,0:T(8,128)(2,1)S(1)}, u32[]{:S(2)}, u32[]{:S(2)}) collective-permute-start(f16[64,1024]{1,0:T(8,128)(2,1)S(1)} %pad_maximum_fusion.1), channel_id=1, source_target_pairs={{0,4},{1,3},{2,6},{3,1},{4,0},{5,7},{6,2},{7,5},{8,12},{9,11},{10,... | collective-permute-start | bytes 393224 | tf_op jit(solution)/shard_map/ppermute | solution.py:372
  56.6 6.4 %collective-permute-start.13 = (f16[64,1024]{1,0:T(8,128)(2,1)S(1)}, f16[64,1024]{1,0:T(8,128)(2,1)S(1)}, u32[]{:S(2)}, u32[]{:S(2)}) collective-permute-start(f16[64,1024]{1,0:T(8,128)(2,1)S(1)} %pad_maximum_fusion.1), channel_id=1, source_target_pairs={{0,2},{1,5},{2,0},{3,7},{4,6},{5,1},{6,4},{7,3},{8,10},{9,13},{10,... | collective-permute-start | bytes 393224 | tf_op jit(solution)/shard_map/ppermute | solution.py:372
  57.2 7.2 %collective-permute-start.23 = (f16[64,1024]{1,0:T(8,128)(2,1)S(1)}, f16[64,1024]{1,0:T(8,128)(2,1)S(1)}, u32[]{:S(2)}, u32[]{:S(2)}) collective-permute-start(f16[64,1024]{1,0:T(8,128)(2,1)S(1)} %pad_maximum_fusion.2), channel_id=1, source_target_pairs={{0,6},{1,7},{2,4},{3,5},{4,2},{5,3},{6,0},{7,1},{8,14},{9,15},{10,... | collective-permute-start | bytes 393224 | tf_op jit(solution)/shard_map/ppermute | solution.py:372
  59.8 6.0 %collective-permute-start.24 = (f16[64,1024]{1,0:T(8,128)(2,1)S(1)}, f16[64,1024]{1,0:T(8,128)(2,1)S(1)}, u32[]{:S(2)}, u32[]{:S(2)}) collective-permute-start(f16[64,1024]{1,0:T(8,128)(2,1)S(1)} %pad_maximum_fusion.2), channel_id=1, source_target_pairs={{0,4},{1,3},{2,6},{3,1},{4,0},{5,7},{6,2},{7,5},{8,12},{9,11},{10,... | collective-permute-start | bytes 393224 | tf_op jit(solution)/shard_map/ppermute | solution.py:372
  60.9 5.0 %collective-permute-start.25 = (f16[64,1024]{1,0:T(8,128)(2,1)S(1)}, f16[64,1024]{1,0:T(8,128)(2,1)S(1)}, u32[]{:S(2)}, u32[]{:S(2)}) collective-permute-start(f16[64,1024]{1,0:T(8,128)(2,1)S(1)} %pad_maximum_fusion.2), channel_id=1, source_target_pairs={{0,2},{1,5},{2,0},{3,7},{4,6},{5,1},{6,4},{7,3},{8,10},{9,13},{10,... | collective-permute-start | bytes 393224 | tf_op jit(solution)/shard_map/ppermute | solution.py:372
